TPU v7x, 256 devices: a whole 4x4x8 slice. The times are simulated.
256 devices in a mesh: domain: 32 (over z_hi, x, y), band: 8 (over z_lo, core).
Axes of the slice: x: 4, y: 4, z: 8 (z_hi: 2, z_lo: 4; z = z_hi * 4 + z_lo), core: 2. Of those that a mesh axis runs over, the one named last changes fastest.
Arguments:
- orbitals: float32 [128, 128, 64, 128], P('band', 'domain'), may hold values from -8 to 8, as said below
- potential: float32 [128, 64, 128], P('domain'), may hold values from 0 to 1
Outputs:
- rotated: float32 [128, 128, 64, 128], P(None, 'domain', 'band')
Inputs may be any that keep to these rules, and one draw needn't show every extreme that they name: `orbitals`: entries of order one.
All inputs are finite; a program needn't handle non-finite values.
Results may differ from a plain program's by a relative error of at most 0.00015.
Values sent between devices are 32-bit elements; how exact they have to be, the bound alone decides.
No kernel may reach another device: no remote copies, remote signals or barrier semaphores. Data moves between devices by JAX's collectives and lax.ppermute only.
A program may use at most 128 MiB of HBM per device.

v0:
```python
import math

import jax
import jax.numpy as jnp
from jax import lax
from jax.sharding import PartitionSpec as P


def extended(block, sides, width):
    for axis, dim in sides:
        count = lax.axis_size(axis)
        forward = [(i, i + 1) for i in range(count - 1)]
        forward.append((count - 1, 0))
        backward = [(target, source) for source, target in forward]
        low = lax.ppermute(
            lax.slice_in_dim(block, block.shape[dim] - width, None, axis=dim), axis, forward
        )
        high = lax.ppermute(lax.slice_in_dim(block, 0, width, axis=dim), axis, backward)
        block = jnp.concatenate([low, block, high], axis=dim)
    return block


def shifted_apply(padded, pot_mid):
    middle = padded[:, 1:-1]
    beside = padded[:, 2:] + padded[:, :-2]
    beside = beside + jnp.roll(middle, 1, 2) + jnp.roll(middle, -1, 2)
    beside = beside + jnp.roll(middle, 1, 3) + jnp.roll(middle, -1, 3)
    hamil = (3.0 + pot_mid[None]) * middle - 0.5 * beside
    return (hamil - 4.5 * middle) / 2.5


def shallow_step(field, potential):
    padded = extended(field, (("domain", 1),), 1)
    return shifted_apply(padded, potential)


def body(orbitals, potential):
    first = shallow_step(orbitals, potential)
    second = 2.0 * shallow_step(first, potential) - orbitals
    filtered = 2.0 * shallow_step(second, potential) - first
    orb_total = orbitals.shape[0] * lax.axis_size("band")
    planes = orbitals.shape[1]
    ny_all = orbitals.shape[2]
    nx_all = orbitals.shape[3]
    stripe = ny_all // lax.axis_size("band")
    cell_total = planes * lax.axis_size("domain") * ny_all * nx_all
    banded = lax.all_to_all(filtered, "band", split_axis=2, concat_axis=0, tiled=True)
    flat = banded.reshape(orb_total, -1)
    partial_gram = jnp.dot(
        flat, flat.T, precision=lax.Precision.HIGHEST, preferred_element_type=jnp.float32
    )
    gram = lax.psum(partial_gram, ("domain", "band"))
    lower = jnp.linalg.cholesky(gram)
    solved = lax.linalg.triangular_solve(lower, flat, left_side=True, lower=True)
    scaled = solved * math.sqrt(cell_total)
    return scaled.reshape(orb_total, planes, stripe, nx_all)


def solution(mesh):
    in_specs = (P("band", "domain", None, None), P("domain", None, None))
    out_specs = P(None, "domain", "band", None)
    return jax.shard_map(body, mesh=mesh, in_specs=in_specs, out_specs=out_specs, check_vma=False)
```

profile of v0, /device:TPU:32, one launch (start us, length us, event | category | flops | bytes accessed | tf_op | source)
XLA Modules:
  0.0 443.7 jit_solution(13147372865584667590)
XLA Ops:
  6.5 0.0 copy-start
  6.5 0.0 all-reduce.2.cloned.1.call-start
  6.5 1.4 fusion.43
  8.0 11.0 %collective-permute-start = (f32[16,1,64,128]{3,2,1,0:T(8,128)S(1)}, f32[16,1,64,128]{3,2,1,0:T(8,128)S(1)}, u32[]{:S(2)}, u32[]{:S(2)}) collective-permute-start(f32[16,1,64,128]{3,2,1,0:T(8,128)S(1)} %get-tuple-element.27), channel_id=1, source_target_pairs={{8,0},{16,8},{24,16},{32,24},{40,32},{48,40},{56,48},{64,56},{72,6... | collective-permute-start | bytes 1572872 | tf_op jit(solution)/shard_map/ppermute | solution.py:18
  19.0 0.0 collective-permute-start.1
  19.0 0.0 copy-done
  19.0 0.7 fusion.46
  19.7 0.0 copy-start.1
  19.7 0.7 fusion.47
  20.5 0.1 copy-done.1
  20.7 0.6 fusion.45
  21.3 20.1 %collective-permute-done = f32[16,1,64,128]{3,2,1,0:T(8,128)S(1)} collective-permute-done((f32[16,1,64,128]{3,2,1,0:T(8,128)S(1)}, f32[16,1,64,128]{3,2,1,0:T(8,128)S(1)}, u32[]{:S(2)}, u32[]{:S(2)}) %collective-permute-start) | collective-permute-done | bytes 524320 | tf_op jit(solution)/shard_map/ppermute | solution.py:18
  41.4 10.3 %collective-permute-done.1 = f32[16,1,64,128]{3,2,1,0:T(8,128)S(1)} collective-permute-done((f32[16,1,64,128]{3,2,1,0:T(8,128)S(1)}, f32[16,1,64,128]{3,2,1,0:T(8,128)S(1)}, u32[]{:S(2)}, u32[]{:S(2)}) %collective-permute-start.1) | collective-permute-done | bytes 524320 | tf_op jit(solution)/shard_map/ppermute | solution.py:15
  51.7 2.3 broadcast_multiply_fusion
  54.0 0.1 fusion.42
  54.1 0.8 fusion.38
  54.9 0.8 fusion.39
  55.8 0.4 collective-permute-start.2
  56.1 1.7 collective-permute-start.3
  57.9 0.6 fusion.40
  58.6 15.9 %collective-permute-done.2 = f32[16,1,64,128]{3,2,1,0:T(8,128)S(1)} collective-permute-done((f32[16,1,64,128]{3,2,1,0:T(8,128)S(1)}, f32[16,1,64,128]{3,2,1,0:T(8,128)S(1)}, u32[]{:S(2)}, u32[]{:S(2)}) %collective-permute-start.2) | collective-permute-done | bytes 524320 | tf_op jit(solution)/shard_map/ppermute | solution.py:18
  74.5 10.4 %collective-permute-done.3 = f32[16,1,64,128]{3,2,1,0:T(8,128)S(1)} collective-permute-done((f32[16,1,64,128]{3,2,1,0:T(8,128)S(1)}, f32[16,1,64,128]{3,2,1,0:T(8,128)S(1)}, u32[]{:S(2)}, u32[]{:S(2)}) %collective-permute-start.3) | collective-permute-done | bytes 524320 | tf_op jit(solution)/shard_map/ppermute | solution.py:15
  84.9 2.5 fusion.19
  87.4 0.1 fusion.37
  87.5 0.6 fusion.35
  88.1 0.8 fusion.34
  89.0 0.4 collective-permute-start.4
  89.3 1.7 collective-permute-start.5
  91.1 0.8 fusion.33
  91.9 10.8 %collective-permute-done.4 = f32[16,1,64,128]{3,2,1,0:T(8,128)S(1)} collective-permute-done((f32[16,1,64,128]{3,2,1,0:T(8,128)S(1)}, f32[16,1,64,128]{3,2,1,0:T(8,128)S(1)}, u32[]{:S(2)}, u32[]{:S(2)}) %collective-permute-start.4) | collective-permute-done | bytes 524320 | tf_op jit(solution)/shard_map/ppermute | solution.py:18
  102.8 8.5 %collective-permute-done.5 = f32[16,1,64,128]{3,2,1,0:T(8,128)S(1)} collective-permute-done((f32[16,1,64,128]{3,2,1,0:T(8,128)S(1)}, f32[16,1,64,128]{3,2,1,0:T(8,128)S(1)}, u32[]{:S(2)}, u32[]{:S(2)}) %collective-permute-start.5) | collective-permute-done | bytes 524320 | tf_op jit(solution)/shard_map/ppermute | solution.py:15
  111.3 2.6 fusion.9
  113.9 1.2 copy.28
  115.2 56.2 %all_to_all.15 = f32[16,4,64,128]{3,0,1,2:T(8,128)S(1)} all-to-all(f32[16,4,64,128]{3,0,1,2:T(8,128)S(1)} %copy.28), channel_id=1, replica_groups=mesh['domain'=32,'band'=8] {'band'}, dimensions={2} | all-to-all | bytes 4194304 | tf_op jit(solution)/shard_map/all_to_all | solution.py:47
  171.3 2.5 copy.35
  173.8 1.7 reshape.18
  175.6 2.4 fusion.48
  178.0 0.0 all-reduce.2.cloned.1.call-update
  178.0 230.5 %all-reduce.2.cloned.1.call-done = f32[128,128]{0,1:T(8,128)} async-done(((f32[128,128]{0,1:T(8,128)}), f32[128,128]{0,1:T(8,128)}) %all-reduce.2.cloned.1.call-update) | async-done | bytes 65552 | tf_op jit(solution)/shard_map/psum | solution.py:52
  408.5 0.9 copy.31
  409.5 0.9 fusion.31
  410.3 11.7 %cholesky.16 = f32[128,128]{1,0:T(8,128)S(1)} custom-call(f32[128,128]{1,0:T(8,128)S(1)} %fusion.31), custom_call_target="Cholesky" | custom-call | tf_op jit(solution)/shard_map/jit(cholesky)/cholesky | solution.py:53
  422.1 0.6 compare_reduce_fusion
  422.7 0.7 fusion.29
  423.4 9.8 %custom-call.6 = f32[1,128,128]{1,2,0:T(8,128)S(1)} custom-call(f32[1,128,128]{2,1,0:T(8,128)S(1)} %fusion.29), custom_call_target="InvertDiagBlocksLowerTriangular" | custom-call | tf_op jit(solution)/shard_map/triangular_solve | solution.py:54
  433.2 1.9 fusion.28
  435.1 1.7 copy.33
  (5 shorter events, 0.2 us)
Async XLA Ops:
  6.5 12.4 %copy-start = (f32[16,4,64,128]{3,2,1,0:T(8,128)S(1)}, f32[16,4,64,128]{3,2,1,0:T(8,128)}, u32[]{:S(2)}) copy-start(f32[16,4,64,128]{3,2,1,0:T(8,128)} %param.2) | copy-start | bytes 6291460
  6.5 402.0 %all-reduce.2.cloned.1.call-start = ((), (), s32[]{:S(2)}) async-start(), calls=%async_computation.1 | async-start | bytes 131072 | tf_op jit(solution)/shard_map/psum | solution.py:52
  8.0 33.4 %collective-permute-start = (f32[16,1,64,128]{3,2,1,0:T(8,128)S(1)}, f32[16,1,64,128]{3,2,1,0:T(8,128)S(1)}, u32[]{:S(2)}, u32[]{:S(2)}) collective-permute-start(f32[16,1,64,128]{3,2,1,0:T(8,128)S(1)} %get-tuple-element.27), channel_id=1, source_target_pairs={{8,0},{16,8},{24,16},{32,24},{40,32},{48,40},{56,48},{64,56},{72,6... | collective-permute-start | bytes 1572872 | tf_op jit(solution)/shard_map/ppermute | solution.py:18
  19.0 32.7 %collective-permute-start.1 = (f32[16,1,64,128]{3,2,1,0:T(8,128)S(1)}, f32[16,1,64,128]{3,2,1,0:T(8,128)S(1)}, u32[]{:S(2)}, u32[]{:S(2)}) collective-permute-start(f32[16,1,64,128]{3,2,1,0:T(8,128)S(1)} %get-tuple-element.28), channel_id=1, source_target_pairs={{0,8},{8,16},{16,24},{24,32},{32,40},{40,48},{48,56},{56,64},{64,7... | collective-permute-start | bytes 1572872 | tf_op jit(solution)/shard_map/ppermute | solution.py:15
  19.7 0.9 copy-start.1
  55.8 18.7 %collective-permute-start.2 = (f32[16,1,64,128]{3,2,1,0:T(8,128)S(1)}, f32[16,1,64,128]{3,2,1,0:T(8,128)S(1)}, u32[]{:S(2)}, u32[]{:S(2)}) collective-permute-start(f32[16,1,64,128]{3,2,1,0:T(8,128)S(1)} %get-tuple-element.25), channel_id=1, source_target_pairs={{8,0},{16,8},{24,16},{32,24},{40,32},{48,40},{56,48},{64,56},{72,6... | collective-permute-start | bytes 1572872 | tf_op jit(solution)/shard_map/ppermute | solution.py:18
  56.1 28.7 %collective-permute-start.3 = (f32[16,1,64,128]{3,2,1,0:T(8,128)S(1)}, f32[16,1,64,128]{3,2,1,0:T(8,128)S(1)}, u32[]{:S(2)}, u32[]{:S(2)}) collective-permute-start(f32[16,1,64,128]{3,2,1,0:T(8,128)S(1)} %get-tuple-element.26), channel_id=1, source_target_pairs={{0,8},{8,16},{16,24},{24,32},{32,40},{40,48},{48,56},{56,64},{64,7... | collective-permute-start | bytes 1572872 | tf_op jit(solution)/shard_map/ppermute | solution.py:15
  89.0 13.8 %collective-permute-start.4 = (f32[16,1,64,128]{3,2,1,0:T(8,128)S(1)}, f32[16,1,64,128]{3,2,1,0:T(8,128)S(1)}, u32[]{:S(2)}, u32[]{:S(2)}) collective-permute-start(f32[16,1,64,128]{3,2,1,0:T(8,128)S(1)} %get-tuple-element.15), channel_id=1, source_target_pairs={{8,0},{16,8},{24,16},{32,24},{40,32},{48,40},{56,48},{64,56},{72,6... | collective-permute-start | bytes 1572872 | tf_op jit(solution)/shard_map/ppermute | solution.py:18
  89.3 22.0 %collective-permute-start.5 = (f32[16,1,64,128]{3,2,1,0:T(8,128)S(1)}, f32[16,1,64,128]{3,2,1,0:T(8,128)S(1)}, u32[]{:S(2)}, u32[]{:S(2)}) collective-permute-start(f32[16,1,64,128]{3,2,1,0:T(8,128)S(1)} %get-tuple-element.16), channel_id=1, source_target_pairs={{0,8},{8,16},{16,24},{24,32},{32,40},{40,48},{48,56},{56,64},{64,7... | collective-permute-start | bytes 1572872 | tf_op jit(solution)/shard_map/ppermute | solution.py:15
Sparse Core Ops, SparseCore 0:
  178.2 230.3 all-reduce.1
where the time goes:
time: 447 us; the launch traced here: 444 us
  waiting for transfers between devices  307 us (69%)
  blocking collectives  56.2 us (13%)
  other arithmetic  31.2 us (7%)
  local copies, waits for them, and re-layouts  16.6 us (4%)
  starting transfers between devices  15.2 us (3%)
  between operations  13.6 us (3%)
    psum x1, waiting for transfers between devices, body(): gram = lax.psum(partial_gram, ('domain', 'band'))  230 us
    all_to_all x1, blocking collectives, body(): lax.all_to_all(filtered, 'band', split_axis=2, concat_axis=0, tiled=True)  56.2 us
    ppermute x3, waiting for transfers between devices, extended(): lax.ppermute(lax.slice_in_dim(block, 0, width, axis=dim), axis, backward)  46.8 us
    ppermute x3, waiting for transfers between devices, extended(): lax.ppermute(lax.slice_in_dim(block, block.shape[dim] - width, None, axis...  29.2 us
    another operation x3, other arithmetic, body(): lower = jnp.linalg.cholesky(gram)  12.4 us
    ppermute x3, starting transfers between devices, extended(): lax.ppermute(lax.slice_in_dim(block, 0, width, axis=dim), axis, backward)  11.7 us
    another operation x2, other arithmetic, body(): lax.linalg.triangular_solve(lower, flat, left_side=True, lower=True)  10.5 us
  transfers between devices with their start and end apart: 7, of which 7 were waited for; matrix products, arithmetic and copies ran while one was open for 1% of the time, Pallas kernels for 0%

commit v1 on v0

v1 whole, which is shorter than its diff:
```python
import functools
import math

import jax
import jax.numpy as jnp
from jax import lax
from jax.experimental import pallas as pl
from jax.experimental.pallas import tpu as pltpu
from jax.sharding import PartitionSpec as P

DEPTH = 3
PARTS = 1


def permuted(block, axis, target):
    count = lax.axis_size(axis)
    return lax.ppermute(block, axis, [(i, target(i)) for i in range(count)])


def neighbours(plane):
    rows, lanes = plane.shape
    beside = pltpu.roll(plane, 1, 0) + pltpu.roll(plane, rows - 1, 0)
    return beside + pltpu.roll(plane, 1, 1) + pltpu.roll(plane, lanes - 1, 1)


def filter_kernel(planes, stripes, field, low, high, pot, pot_low, pot_high, *rest):
    outs, (one, two, three) = rest[:stripes], rest[stripes:]
    me = lax.axis_index("band")

    def source(k):
        if k < DEPTH:
            return low[0, k], pot_low[k]
        if k < DEPTH + planes:
            return field[0, k - DEPTH], pot[k - DEPTH]
        return high[0, k - DEPTH - planes], pot_high[k - DEPTH - planes]

    top = planes + 2 * DEPTH
    for k in range(1, top - 1):
        middle, local = source(k)
        beside = source(k - 1)[0] + source(k + 1)[0] + neighbours(middle)
        one[k] = (0.4 * local - 0.6) * middle - 0.2 * beside
    for k in range(2, top - 2):
        middle = one[k]
        beside = one[k - 1] + one[k + 1] + neighbours(middle)
        before, local = source(k)
        two[k] = (0.8 * local - 1.2) * middle - 0.4 * beside - before
    for k in range(3, top - 3):
        middle = two[k]
        beside = two[k - 1] + two[k + 1] + neighbours(middle)
        _, local = source(k)
        three[k - 3] = (0.8 * local - 1.2) * middle - 0.4 * beside - one[k]
    width = outs[0].shape[2]
    for slot in range(stripes):
        start = pl.multiple_of(jnp.bitwise_xor(me, slot) * width, width)
        outs[slot][0] = three[:, pl.ds(start, width), :]


def filtered_stripes(field, low, high, pot, pot_low, pot_high, stripes):
    count, planes, rows, lanes = field.shape
    width = rows // stripes
    top = planes + 2 * DEPTH

    def by_orbital(depth):
        return pl.BlockSpec((1, depth, rows, lanes), lambda i: (i, 0, 0, 0))

    def whole(depth):
        return pl.BlockSpec((depth, rows, lanes), lambda i: (0, 0, 0))

    out_spec = pl.BlockSpec((1, planes, width, lanes), lambda i: (i, 0, 0, 0))
    shape = jax.ShapeDtypeStruct((count, planes, width, lanes), jnp.float32)
    return pl.pallas_call(
        functools.partial(filter_kernel, planes, stripes),
        grid=(count,),
        in_specs=[by_orbital(planes), by_orbital(DEPTH), by_orbital(DEPTH)]
        + [whole(planes), whole(DEPTH), whole(DEPTH)],
        out_specs=[out_spec] * stripes,
        out_shape=[shape] * stripes,
        scratch_shapes=[
            pltpu.VMEM((top, rows, lanes), jnp.float32),
            pltpu.VMEM((top, rows, lanes), jnp.float32),
            pltpu.VMEM((planes, rows, lanes), jnp.float32),
        ],
        compiler_params=pltpu.CompilerParams(vmem_limit_bytes=32 * 1024 * 1024),
    )(field, low, high, pot, pot_low, pot_high)


def gram_kernel(pieces, cells, *rest):
    refs, (flat, gram) = rest[:-2], rest[-2:]
    me = lax.axis_index("band")
    lanes = refs[0].shape[1]
    share = refs[0].shape[0] // cells
    for index, ref in enumerate(refs):
        slot, piece = divmod(index, pieces)
        first = jnp.bitwise_xor(me, slot) * (share * pieces) + piece * share
        rows = pl.ds(pl.multiple_of(first, share), share)
        for r in range(cells):
            flat[rows, r * lanes : (r + 1) * lanes] = ref[pl.ds(r, share, stride=cells), :]
    whole = flat[...]
    gram[...] = lax.dot_general(
        whole,
        whole,
        (((1,), (1,)), ((), ())),
        precision=lax.Precision.HIGHEST,
        preferred_element_type=jnp.float32,
    )


def flat_and_gram(slots, orbitals):
    pieces = len(slots[0])
    _, planes, width, lanes = slots[0][0].shape
    cells = planes * width
    refs = [piece.reshape(-1, lanes) for slot in slots for piece in slot]
    return pl.pallas_call(
        functools.partial(gram_kernel, pieces, cells),
        out_shape=[
            jax.ShapeDtypeStruct((orbitals, cells * lanes), jnp.float32),
            jax.ShapeDtypeStruct((orbitals, orbitals), jnp.float32),
        ],
        compiler_params=pltpu.CompilerParams(vmem_limit_bytes=32 * 1024 * 1024),
    )(*refs)


def rotate_kernel(cells, inverse, flat, out):
    orbitals = inverse.shape[0]
    lanes = out.shape[1]
    solved = jnp.dot(
        inverse[...],
        flat[...],
        precision=lax.Precision.HIGHEST,
        preferred_element_type=jnp.float32,
    )
    for r in range(cells):
        out[pl.ds(r, orbitals, stride=cells), :] = solved[:, r * lanes : (r + 1) * lanes]


def rotated(inverse, flat, lanes):
    orbitals, columns = flat.shape
    cells = columns // lanes
    return pl.pallas_call(
        functools.partial(rotate_kernel, cells),
        out_shape=jax.ShapeDtypeStruct((orbitals * cells, lanes), jnp.float32),
        compiler_params=pltpu.CompilerParams(vmem_limit_bytes=32 * 1024 * 1024),
    )(inverse, flat)


def summed(gram):
    for bit in (1, 2, 4):
        gram = gram + permuted(gram, "band", lambda i: i ^ bit)
    side = 4
    turned = [
        permuted(gram, "domain", lambda i: i // side * side + (i + k) % side) for k in (1, 2, 3)
    ]
    gram = (gram + turned[0]) + (turned[1] + turned[2])
    plane = side * side
    turned = [
        permuted(gram, "domain", lambda i: i // plane * plane + (i + k * side) % plane)
        for k in (1, 2, 3)
    ]
    gram = (gram + turned[0]) + (turned[1] + turned[2])
    return gram + permuted(gram, "domain", lambda i: i ^ plane)


def body(orbitals, potential):
    domains = lax.axis_size("domain")
    stripes = lax.axis_size("band")
    own, planes, ny_all, nx_all = orbitals.shape
    width = ny_all // stripes
    orb_total = own * stripes
    cell_total = planes * domains * ny_all * nx_all
    up = lambda i: (i + 1) % domains
    down = lambda i: (i - 1) % domains

    pot_low = permuted(potential[planes - DEPTH :], "domain", up)
    pot_high = permuted(potential[:DEPTH], "domain", down)
    share = own // PARTS
    pieces = []
    for part in range(PARTS):
        field = orbitals[part * share : (part + 1) * share]
        low = permuted(field[:, planes - DEPTH :], "domain", up)
        high = permuted(field[:, :DEPTH], "domain", down)
        slots = filtered_stripes(field, low, high, potential, pot_low, pot_high, stripes)
        pieces.append(
            [slots[0]]
            + [permuted(slots[k], "band", lambda i: i ^ k) for k in range(1, stripes)]
        )
    slots = [[piece[k] for piece in pieces] for k in range(stripes)]
    flat, partial_gram = flat_and_gram(slots, orb_total)
    gram = summed(partial_gram)
    lower = jnp.linalg.cholesky(gram)
    inverse = lax.linalg.triangular_solve(
        lower, math.sqrt(cell_total) * jnp.eye(orb_total, dtype=jnp.float32), left_side=True, lower=True
    )
    return rotated(inverse, flat, nx_all).reshape(orb_total, planes, width, nx_all)


def solution(mesh):
    in_specs = (P("band", "domain", None, None), P("domain", None, None))
    out_specs = P(None, "domain", "band", None)
    return jax.shard_map(body, mesh=mesh, in_specs=in_specs, out_specs=out_specs, check_vma=False)
```

time: 447 us -> 217 us (0.49)
  waiting for transfers between devices: 307 us -> 145 us
  blocking collectives: 56.2 us -> 0 us
  starting transfers between devices: 15.2 us -> 32.8 us
  local copies, waits for them, and re-layouts: 16.6 us -> 2.53 us
  Pallas kernels: 0 us -> 14 us
  between operations: 13.6 us -> 0.18 us
  other arithmetic: 31.2 us -> 22.9 us
    psum x1 -> x0, waiting for transfers between devices: 230 us -> none  [body(): gram = lax.psum(partial_gram, ('domain', 'band'))]
    ppermute x6 -> x21, waiting for transfers between devices: 76.1 us -> 145 us  [permuted(): return lax.ppermute(block, axis, [(i, target(i)) for i in range(count)])]
    all_to_all x1 -> x0, blocking collectives: 56.2 us -> none  [body(): lax.all_to_all(filtered, 'band', split_axis=2, concat_axis=0, tiled=True)]
    ppermute x6 -> x21, starting transfers between devices: 15.2 us -> 32.8 us  [permuted(): return lax.ppermute(block, axis, [(i, target(i)) for i in range(count)])]
    pallas_call x0 -> x3, Pallas kernels: none -> 14 us  [the longest x1 6.72 us: filtered_stripes(): pl.pallas_call(functools.partial(filter_kernel, planes, stripes), grid=(c...]
    slice x15 -> x2, local copies, waits for them, and re-layouts: 8.32 us -> 2.35 us  [the longest x1 2.34 us: body(): high = permuted(field[:, :DEPTH], 'domain', down)]
    sub x2 -> x0, other arithmetic: 5.18 us -> none  [the longest x1 2.64 us: body(): filtered = 2.0 * shallow_step(second, potential) - first]
  transfers between devices with their start and end apart: 7 -> 21, of which waited for: 7 -> 17; matrix products, arithmetic and copies ran while one was open for 1% -> 0% of each run, Pallas kernels for 0% -> 0%
where the time goes in v1:
time: 217 us
  waiting for transfers between devices  145 us (67%)
  starting transfers between devices  32.8 us (15%)
  other arithmetic  22.9 us (11%)
  Pallas kernels  14 us (6%)
  local copies, waits for them, and re-layouts  2.53 us (1%)
    ppermute x21, waiting for transfers between devices, permuted(): return lax.ppermute(block, axis, [(i, target(i)) for i in range(count)])  145 us
    ppermute x21, starting transfers between devices, permuted(): return lax.ppermute(block, axis, [(i, target(i)) for i in range(count)])  32.8 us
    another operation x3, other arithmetic, body(): lower = jnp.linalg.cholesky(gram)  12.4 us
    another operation x2, other arithmetic, body(): lax.linalg.triangular_solve(lower, math.sqrt(cell_total) * jnp.eye(orb_to...  10.5 us
    pallas_call x1, Pallas kernels, filtered_stripes(): pl.pallas_call(functools.partial(filter_kernel, planes, stripes), grid=(c...  6.72 us
  transfers between devices with their start and end apart: 21, of which 17 were waited for; matrix products, arithmetic and copies ran while one was open for 0% of the time, Pallas kernels for 0%

profile of v1, /device:TPU:32, one launch (start us, length us, event | category | flops | bytes accessed | tf_op | source)
XLA Modules:
  0.0 217.3 jit_solution(11609839332969968385)
XLA Ops:
  0.0 0.0 copy-start.1
  0.0 0.0 copy-start
  0.0 2.3 %fusion.9 = (f32[16,3,64,128]{3,2,1,0:T(8,128)S(1)}, f32[16,3,64,128]{3,2,1,0:T(8,128)S(1)}) fusion(f32[16,4,64,128]{3,2,1,0:T(8,128)} %field.1), kind=kLoop, calls=%fused_computation.17 | loop fusion | bytes 6291456 | tf_op jit(solution)/shard_map/slice | solution.py:180
  2.3 11.0 %collective-permute-start.1 = (f32[16,3,64,128]{3,2,1,0:T(8,128)S(1)}, f32[16,3,64,128]{3,2,1,0:T(8,128)S(1)}, u32[]{:S(2)}, u32[]{:S(2)}) collective-permute-start(f32[16,3,64,128]{3,2,1,0:T(8,128)S(1)} %get-tuple-element.25), channel_id=1, source_target_pairs={{0,248},{8,0},{16,8},{24,16},{32,24},{40,32},{48,40},{56,48},{64,5... | collective-permute-start | bytes 4718600 | tf_op jit(solution)/shard_map/ppermute | solution.py:17
  13.4 0.0 collective-permute-start
  13.4 0.0 copy-done.1
  13.4 10.2 %collective-permute-start.3 = (f32[3,64,128]{2,1,0:T(8,128)S(1)}, f32[3,64,128]{2,1,0:T(8,128)S(1)}, u32[]{:S(2)}, u32[]{:S(2)}) collective-permute-start(f32[3,64,128]{2,1,0:T(8,128)S(1)} %get-tuple-element.27), channel_id=1, source_target_pairs={{0,248},{8,0},{16,8},{24,16},{32,24},{40,32},{48,40},{56,48},{64,5... | collective-permute-start | bytes 294920 | tf_op jit(solution)/shard_map/ppermute | solution.py:17
  23.6 0.0 collective-permute-start.2
  23.6 61.5 %collective-permute-done.3.pot_high = f32[3,64,128]{2,1,0:T(8,128)S(1)} collective-permute-done((f32[3,64,128]{2,1,0:T(8,128)S(1)}, f32[3,64,128]{2,1,0:T(8,128)S(1)}, u32[]{:S(2)}, u32[]{:S(2)}) %collective-permute-start.3) | collective-permute-done | bytes 98336 | tf_op jit(solution)/shard_map/ppermute | solution.py:17
  85.1 10.5 %collective-permute-done.2.pot_low = f32[3,64,128]{2,1,0:T(8,128)S(1)} collective-permute-done((f32[3,64,128]{2,1,0:T(8,128)S(1)}, f32[3,64,128]{2,1,0:T(8,128)S(1)}, u32[]{:S(2)}, u32[]{:S(2)}) %collective-permute-start.2) | collective-permute-done | bytes 98336 | tf_op jit(solution)/shard_map/ppermute | solution.py:17
  95.5 0.0 collective-permute-done.1.high
  95.5 0.0 collective-permute-done.low
  95.5 0.0 copy-done
  95.6 6.7 %shard_map.28 = (f32[16,4,8,128]{3,2,1,0:T(8,128)S(1)}, f32[16,4,8,128]{3,2,1,0:T(8,128)S(1)}, f32[16,4,8,128]{3,2,1,0:T(8,128)S(1)}, f32[16,4,8,128]{3,2,1,0:T(...) custom-call(f32[16,4,64,128]{3,2,1,0:T(8,128)S(1)} %copy-done, ...), custom_call_target="tpu_custom_call" | custom-call | tf_op jit(solution)/shard_map/pallas_call | solution.py:71
  102.3 0.1 collective-permute-start.4
  102.4 1.1 collective-permute-start.5
  103.5 0.7 collective-permute-start.6
  104.3 0.3 collective-permute-start.7
  104.5 2.3 %collective-permute-start.8 = (f32[16,4,8,128]{3,2,1,0:T(8,128)S(1)}, f32[16,4,8,128]{3,2,1,0:T(8,128)S(1)}, u32[]{:S(2)}, u32[]{:S(2)}) collective-permute-start(f32[16,4,8,128]{3,2,1,0:T(8,128)S(1)} %get-tuple-element.20), channel_id=1, source_target_pairs={{0,5},{1,4},{2,7},{3,6},{4,1},{5,0},{6,3},{7,2},{8,13},{9,12},{10,... | collective-permute-start | bytes 786440 | tf_op jit(solution)/shard_map/ppermute | solution.py:17
  106.9 0.0 collective-permute-done.4
  106.9 0.0 collective-permute-start.9
  106.9 10.9 %collective-permute-done.5 = f32[16,4,8,128]{3,2,1,0:T(8,128)S(1)} collective-permute-done((f32[16,4,8,128]{3,2,1,0:T(8,128)S(1)}, f32[16,4,8,128]{3,2,1,0:T(8,128)S(1)}, u32[]{:S(2)}, u32[]{:S(2)}) %collective-permute-start.5) | collective-permute-done | bytes 262176 | tf_op jit(solution)/shard_map/ppermute | solution.py:17
  117.7 1.7 collective-permute-start.10
  119.4 3.5 %collective-permute-done.6 = f32[16,4,8,128]{3,2,1,0:T(8,128)S(1)} collective-permute-done((f32[16,4,8,128]{3,2,1,0:T(8,128)S(1)}, f32[16,4,8,128]{3,2,1,0:T(8,128)S(1)}, u32[]{:S(2)}, u32[]{:S(2)}) %collective-permute-start.6) | collective-permute-done | bytes 262176 | tf_op jit(solution)/shard_map/ppermute | solution.py:17
  122.9 0.0 collective-permute-done.7
  122.9 16.4 %collective-permute-done.8 = f32[16,4,8,128]{3,2,1,0:T(8,128)S(1)} collective-permute-done((f32[16,4,8,128]{3,2,1,0:T(8,128)S(1)}, f32[16,4,8,128]{3,2,1,0:T(8,128)S(1)}, u32[]{:S(2)}, u32[]{:S(2)}) %collective-permute-start.8) | collective-permute-done | bytes 262176 | tf_op jit(solution)/shard_map/ppermute | solution.py:17
  139.3 8.3 %collective-permute-done.9 = f32[16,4,8,128]{3,2,1,0:T(8,128)S(1)} collective-permute-done((f32[16,4,8,128]{3,2,1,0:T(8,128)S(1)}, f32[16,4,8,128]{3,2,1,0:T(8,128)S(1)}, u32[]{:S(2)}, u32[]{:S(2)}) %collective-permute-start.9) | collective-permute-done | bytes 262176 | tf_op jit(solution)/shard_map/ppermute | solution.py:17
  147.6 4.5 %collective-permute-done.10 = f32[16,4,8,128]{3,2,1,0:T(8,128)S(1)} collective-permute-done((f32[16,4,8,128]{3,2,1,0:T(8,128)S(1)}, f32[16,4,8,128]{3,2,1,0:T(8,128)S(1)}, u32[]{:S(2)}, u32[]{:S(2)}) %collective-permute-start.10) | collective-permute-done | bytes 262176 | tf_op jit(solution)/shard_map/ppermute | solution.py:17
  152.1 3.1 %shard_map.29 = (f32[128,4096]{1,0:T(8,128)S(1)}, f32[128,128]{1,0:T(8,128)S(1)}) custom-call(f32[512,128]{1,0:T(8,128)S(1)} %bitcast.18, f32[512,128]{1,0:T(8,128)S(1)} %bitcast.19, f32[512,128]{1,0:T(8,128)S(1)} %bitcast.20, f32[512,128]{1,0:T(8,128)S(1)} %bitcast.21, f32[512,128]{1,0:T(8,128)S(1)} %bitcast.22, f32[512,128]{1,0:T(8,128)S(1)} %bitcast.23, ...), custom_call_target="tpu_custom_call" | custom-call | tf_op jit(solution)/shard_map/pallas_call | solution.py:113
  155.2 0.1 copy.4
  155.3 0.5 collective-permute-start.11
  155.8 0.9 collective-permute-done.11
  156.7 0.1 collective-permute-start.12
  156.8 4.3 %collective-permute-done.12 = f32[128,128]{0,1:T(8,128)S(1)} collective-permute-done((f32[128,128]{0,1:T(8,128)S(1)}, f32[128,128]{0,1:T(8,128)S(1)}, u32[]{:S(2)}, u32[]{:S(2)}) %collective-permute-start.12) | collective-permute-done | bytes 65568 | tf_op jit(solution)/shard_map/ppermute | solution.py:17
  161.1 0.3 collective-permute-start.13
  161.4 5.2 %collective-permute-done.13 = f32[128,128]{0,1:T(8,128)S(1)} collective-permute-done((f32[128,128]{0,1:T(8,128)S(1)}, f32[128,128]{0,1:T(8,128)S(1)}, u32[]{:S(2)}, u32[]{:S(2)}) %collective-permute-start.13) | collective-permute-done | bytes 65568 | tf_op jit(solution)/shard_map/ppermute | solution.py:17
  166.6 0.1 collective-permute-start.16
  166.7 0.1 collective-permute-start.15
  166.8 1.9 collective-permute-start.14
  168.7 2.2 %collective-permute-done.16 = f32[128,128]{0,1:T(8,128)S(1)} collective-permute-done((f32[128,128]{0,1:T(8,128)S(1)}, f32[128,128]{0,1:T(8,128)S(1)}, u32[]{:S(2)}, u32[]{:S(2)}) %collective-permute-start.16) | collective-permute-done | bytes 65568 | tf_op jit(solution)/shard_map/ppermute | solution.py:17
  170.9 1.8 collective-permute-done.15
  172.7 0.9 collective-permute-done.14
  173.6 0.1 collective-permute-start.19
  173.7 0.1 collective-permute-start.18
  173.8 1.9 collective-permute-start.17
  175.7 2.2 %collective-permute-done.19 = f32[128,128]{0,1:T(8,128)S(1)} collective-permute-done((f32[128,128]{0,1:T(8,128)S(1)}, f32[128,128]{0,1:T(8,128)S(1)}, u32[]{:S(2)}, u32[]{:S(2)}) %collective-permute-start.19) | collective-permute-done | bytes 65568 | tf_op jit(solution)/shard_map/ppermute | solution.py:17
  178.0 1.6 collective-permute-done.18
  179.6 1.1 collective-permute-done.17
  180.7 0.3 collective-permute-start.20
  181.0 8.8 %collective-permute-done.20 = f32[128,128]{0,1:T(8,128)S(1)} collective-permute-done((f32[128,128]{0,1:T(8,128)S(1)}, f32[128,128]{0,1:T(8,128)S(1)}, u32[]{:S(2)}, u32[]{:S(2)}) %collective-permute-start.20) | collective-permute-done | bytes 65568 | tf_op jit(solution)/shard_map/ppermute | solution.py:17
  189.8 0.1 copy.5
  190.0 11.7 %cholesky.17 = f32[128,128]{1,0:T(8,128)S(1)} custom-call(f32[128,128]{1,0:T(8,128)S(1)} %fusion.3), custom_call_target="Cholesky" | custom-call | tf_op jit(solution)/shard_map/jit(cholesky)/cholesky | solution.py:189
  201.7 0.6 compare_reduce_fusion
  202.3 0.7 fusion
  203.0 9.8 %custom-call.6 = f32[1,128,128]{1,2,0:T(8,128)S(1)} custom-call(f32[1,128,128]{2,1,0:T(8,128)S(1)} %fusion), custom_call_target="InvertDiagBlocksLowerTriangular" | custom-call | tf_op jit(solution)/shard_map/triangular_solve | solution.py:190
  212.8 0.3 fusion.1.inverse
  213.1 4.2 %shard_map.30 = f32[4096,128]{1,0:T(8,128)} custom-call(f32[128,128]{1,0:T(8,128)S(1)} %fusion.1.inverse, f32[128,4096]{1,0:T(8,128)S(1)} %get-tuple-element.24.flat), custom_call_target="tpu_custom_call" | custom-call | tf_op jit(solution)/shard_map/pallas_call | solution.py:139
  (9 shorter events, 0.1 us)
Async XLA Ops:
  0.0 13.4 %copy-start.1 = (f32[4,64,128]{2,1,0:T(8,128)S(1)}, f32[4,64,128]{2,1,0:T(8,128)}, u32[]{:S(2)}) copy-start(f32[4,64,128]{2,1,0:T(8,128)} %pot.1) | copy-start | bytes 393220
  0.0 95.5 %copy-start = (f32[16,4,64,128]{3,2,1,0:T(8,128)S(1)}, f32[16,4,64,128]{3,2,1,0:T(8,128)}, u32[]{:S(2)}) copy-start(f32[16,4,64,128]{3,2,1,0:T(8,128)} %field.1) | copy-start | bytes 6291460
  2.3 93.2 %collective-permute-start.1 = (f32[16,3,64,128]{3,2,1,0:T(8,128)S(1)}, f32[16,3,64,128]{3,2,1,0:T(8,128)S(1)}, u32[]{:S(2)}, u32[]{:S(2)}) collective-permute-start(f32[16,3,64,128]{3,2,1,0:T(8,128)S(1)} %get-tuple-element.25), channel_id=1, source_target_pairs={{0,248},{8,0},{16,8},{24,16},{32,24},{40,32},{48,40},{56,48},{64,5... | collective-permute-start | bytes 4718600 | tf_op jit(solution)/shard_map/ppermute | solution.py:17
  13.4 82.2 %collective-permute-start = (f32[16,3,64,128]{3,2,1,0:T(8,128)S(1)}, f32[16,3,64,128]{3,2,1,0:T(8,128)S(1)}, u32[]{:S(2)}, u32[]{:S(2)}) collective-permute-start(f32[16,3,64,128]{3,2,1,0:T(8,128)S(1)} %get-tuple-element.26), channel_id=1, source_target_pairs={{0,8},{8,16},{16,24},{24,32},{32,40},{40,48},{48,56},{56,64},{64,7... | collective-permute-start | bytes 4718600 | tf_op jit(solution)/shard_map/ppermute | solution.py:17
  13.4 71.7 %collective-permute-start.3 = (f32[3,64,128]{2,1,0:T(8,128)S(1)}, f32[3,64,128]{2,1,0:T(8,128)S(1)}, u32[]{:S(2)}, u32[]{:S(2)}) collective-permute-start(f32[3,64,128]{2,1,0:T(8,128)S(1)} %get-tuple-element.27), channel_id=1, source_target_pairs={{0,248},{8,0},{16,8},{24,16},{32,24},{40,32},{48,40},{56,48},{64,5... | collective-permute-start | bytes 294920 | tf_op jit(solution)/shard_map/ppermute | solution.py:17
  23.6 71.9 %collective-permute-start.2 = (f32[3,64,128]{2,1,0:T(8,128)S(1)}, f32[3,64,128]{2,1,0:T(8,128)S(1)}, u32[]{:S(2)}, u32[]{:S(2)}) collective-permute-start(f32[3,64,128]{2,1,0:T(8,128)S(1)} %get-tuple-element.28), channel_id=1, source_target_pairs={{0,8},{8,16},{16,24},{24,32},{32,40},{40,48},{48,56},{56,64},{64,7... | collective-permute-start | bytes 294920 | tf_op jit(solution)/shard_map/ppermute | solution.py:17
  102.3 4.6 %collective-permute-start.4 = (f32[16,4,8,128]{3,2,1,0:T(8,128)S(1)}, f32[16,4,8,128]{3,2,1,0:T(8,128)S(1)}, u32[]{:S(2)}, u32[]{:S(2)}) collective-permute-start(f32[16,4,8,128]{3,2,1,0:T(8,128)S(1)} %get-tuple-element.16), channel_id=1, source_target_pairs={{0,1},{1,0},{2,3},{3,2},{4,5},{5,4},{6,7},{7,6},{8,9},{9,8},{10,11... | collective-permute-start | bytes 786440 | tf_op jit(solution)/shard_map/ppermute | solution.py:17
  102.4 15.4 %collective-permute-start.5 = (f32[16,4,8,128]{3,2,1,0:T(8,128)S(1)}, f32[16,4,8,128]{3,2,1,0:T(8,128)S(1)}, u32[]{:S(2)}, u32[]{:S(2)}) collective-permute-start(f32[16,4,8,128]{3,2,1,0:T(8,128)S(1)} %get-tuple-element.17), channel_id=1, source_target_pairs={{0,2},{1,3},{2,0},{3,1},{4,6},{5,7},{6,4},{7,5},{8,10},{9,11},{10,... | collective-permute-start | bytes 786440 | tf_op jit(solution)/shard_map/ppermute | solution.py:17
  103.5 19.4 %collective-permute-start.6 = (f32[16,4,8,128]{3,2,1,0:T(8,128)S(1)}, f32[16,4,8,128]{3,2,1,0:T(8,128)S(1)}, u32[]{:S(2)}, u32[]{:S(2)}) collective-permute-start(f32[16,4,8,128]{3,2,1,0:T(8,128)S(1)} %get-tuple-element.18), channel_id=1, source_target_pairs={{0,3},{1,2},{2,1},{3,0},{4,7},{5,6},{6,5},{7,4},{8,11},{9,10},{10,... | collective-permute-start | bytes 786440 | tf_op jit(solution)/shard_map/ppermute | solution.py:17
  104.3 18.6 %collective-permute-start.7 = (f32[16,4,8,128]{3,2,1,0:T(8,128)S(1)}, f32[16,4,8,128]{3,2,1,0:T(8,128)S(1)}, u32[]{:S(2)}, u32[]{:S(2)}) collective-permute-start(f32[16,4,8,128]{3,2,1,0:T(8,128)S(1)} %get-tuple-element.19), channel_id=1, source_target_pairs={{0,4},{1,5},{2,6},{3,7},{4,0},{5,1},{6,2},{7,3},{8,12},{9,13},{10,... | collective-permute-start | bytes 786440 | tf_op jit(solution)/shard_map/ppermute | solution.py:17
  104.5 34.8 %collective-permute-start.8 = (f32[16,4,8,128]{3,2,1,0:T(8,128)S(1)}, f32[16,4,8,128]{3,2,1,0:T(8,128)S(1)}, u32[]{:S(2)}, u32[]{:S(2)}) collective-permute-start(f32[16,4,8,128]{3,2,1,0:T(8,128)S(1)} %get-tuple-element.20), channel_id=1, source_target_pairs={{0,5},{1,4},{2,7},{3,6},{4,1},{5,0},{6,3},{7,2},{8,13},{9,12},{10,... | collective-permute-start | bytes 786440 | tf_op jit(solution)/shard_map/ppermute | solution.py:17
  106.9 40.8 %collective-permute-start.9 = (f32[16,4,8,128]{3,2,1,0:T(8,128)S(1)}, f32[16,4,8,128]{3,2,1,0:T(8,128)S(1)}, u32[]{:S(2)}, u32[]{:S(2)}) collective-permute-start(f32[16,4,8,128]{3,2,1,0:T(8,128)S(1)} %get-tuple-element.21), channel_id=1, source_target_pairs={{0,6},{1,7},{2,4},{3,5},{4,2},{5,3},{6,0},{7,1},{8,14},{9,15},{10,... | collective-permute-start | bytes 786440 | tf_op jit(solution)/shard_map/ppermute | solution.py:17
  117.7 34.4 %collective-permute-start.10 = (f32[16,4,8,128]{3,2,1,0:T(8,128)S(1)}, f32[16,4,8,128]{3,2,1,0:T(8,128)S(1)}, u32[]{:S(2)}, u32[]{:S(2)}) collective-permute-start(f32[16,4,8,128]{3,2,1,0:T(8,128)S(1)} %get-tuple-element.22), channel_id=1, source_target_pairs={{0,7},{1,6},{2,5},{3,4},{4,3},{5,2},{6,1},{7,0},{8,15},{9,14},{10,... | collective-permute-start | bytes 786440 | tf_op jit(solution)/shard_map/ppermute | solution.py:17
  155.3 1.4 collective-permute-start.11
  156.7 4.4 %collective-permute-start.12 = (f32[128,128]{0,1:T(8,128)S(1)}, f32[128,128]{0,1:T(8,128)S(1)}, u32[]{:S(2)}, u32[]{:S(2)}) collective-permute-start(f32[128,128]{0,1:T(8,128)S(1)} %add.41), channel_id=1, source_target_pairs={{0,2},{1,3},{2,0},{3,1},{4,6},{5,7},{6,4},{7,5},{8,10},{9,11},{10,... | collective-permute-start | bytes 196616 | tf_op jit(solution)/shard_map/ppermute | solution.py:17
  161.1 5.4 %collective-permute-start.13 = (f32[128,128]{0,1:T(8,128)S(1)}, f32[128,128]{0,1:T(8,128)S(1)}, u32[]{:S(2)}, u32[]{:S(2)}) collective-permute-start(f32[128,128]{0,1:T(8,128)S(1)} %add.42), channel_id=1, source_target_pairs={{0,4},{1,5},{2,6},{3,7},{4,0},{5,1},{6,2},{7,3},{8,12},{9,13},{10,... | collective-permute-start | bytes 196616 | tf_op jit(solution)/shard_map/ppermute | solution.py:17
  166.6 4.3 %collective-permute-start.16 = (f32[128,128]{0,1:T(8,128)S(1)}, f32[128,128]{0,1:T(8,128)S(1)}, u32[]{:S(2)}, u32[]{:S(2)}) collective-permute-start(f32[128,128]{0,1:T(8,128)S(1)} %add.43), channel_id=1, source_target_pairs={{0,24},{8,0},{16,8},{24,16},{32,56},{40,32},{48,40},{56,48},{64,88... | collective-permute-start | bytes 196616 | tf_op jit(solution)/shard_map/ppermute | solution.py:17
  166.7 6.0 %collective-permute-start.15 = (f32[128,128]{0,1:T(8,128)S(1)}, f32[128,128]{0,1:T(8,128)S(1)}, u32[]{:S(2)}, u32[]{:S(2)}) collective-permute-start(f32[128,128]{0,1:T(8,128)S(1)} %add.43), channel_id=1, source_target_pairs={{0,16},{8,24},{16,0},{24,8},{32,48},{40,56},{48,32},{56,40},{64,80... | collective-permute-start | bytes 196616 | tf_op jit(solution)/shard_map/ppermute | solution.py:17
  166.8 6.8 %collective-permute-start.14 = (f32[128,128]{0,1:T(8,128)S(1)}, f32[128,128]{0,1:T(8,128)S(1)}, u32[]{:S(2)}, u32[]{:S(2)}) collective-permute-start(f32[128,128]{0,1:T(8,128)S(1)} %add.43), channel_id=1, source_target_pairs={{0,8},{8,16},{16,24},{24,0},{32,40},{40,48},{48,56},{56,32},{64,72... | collective-permute-start | bytes 196616 | tf_op jit(solution)/shard_map/ppermute | solution.py:17
  173.6 4.3 %collective-permute-start.19 = (f32[128,128]{0,1:T(8,128)S(1)}, f32[128,128]{0,1:T(8,128)S(1)}, u32[]{:S(2)}, u32[]{:S(2)}) collective-permute-start(f32[128,128]{0,1:T(8,128)S(1)} %add_add_fusion.1), channel_id=1, source_target_pairs={{0,96},{8,104},{16,112},{24,120},{32,0},{40,8},{48,16},{56,24},{64... | collective-permute-start | bytes 196616 | tf_op jit(solution)/shard_map/ppermute | solution.py:17
  173.7 5.9 %collective-permute-start.18 = (f32[128,128]{0,1:T(8,128)S(1)}, f32[128,128]{0,1:T(8,128)S(1)}, u32[]{:S(2)}, u32[]{:S(2)}) collective-permute-start(f32[128,128]{0,1:T(8,128)S(1)} %add_add_fusion.1), channel_id=1, source_target_pairs={{0,64},{8,72},{16,80},{24,88},{32,96},{40,104},{48,112},{56,120},{... | collective-permute-start | bytes 196616 | tf_op jit(solution)/shard_map/ppermute | solution.py:17
  173.8 6.8 %collective-permute-start.17 = (f32[128,128]{0,1:T(8,128)S(1)}, f32[128,128]{0,1:T(8,128)S(1)}, u32[]{:S(2)}, u32[]{:S(2)}) collective-permute-start(f32[128,128]{0,1:T(8,128)S(1)} %add_add_fusion.1), channel_id=1, source_target_pairs={{0,32},{8,40},{16,48},{24,56},{32,64},{40,72},{48,80},{56,88},{64,... | collective-permute-start | bytes 196616 | tf_op jit(solution)/shard_map/ppermute | solution.py:17
  180.7 9.2 %collective-permute-start.20 = (f32[128,128]{0,1:T(8,128)S(1)}, f32[128,128]{0,1:T(8,128)S(1)}, u32[]{:S(2)}, u32[]{:S(2)}) collective-permute-start(f32[128,128]{0,1:T(8,128)S(1)} %add_add_fusion), channel_id=1, source_target_pairs={{0,128},{8,136},{16,144},{24,152},{32,160},{40,168},{48,176},{56,1... | collective-permute-start | bytes 196616 | tf_op jit(solution)/shard_map/ppermute | solution.py:17

commit v2 on v1

v2 whole, which is shorter than its diff:
```python
import functools
import math

import jax
import jax.numpy as jnp
from jax import lax
from jax.experimental import pallas as pl
from jax.experimental.pallas import tpu as pltpu
from jax.sharding import PartitionSpec as P

DEPTH = 3
PARTS = 1
PANEL = 32
SIDE = 4
SHARES = (6, 4, 3, 3)


def permuted(block, axis, target):
    count = lax.axis_size(axis)
    return lax.ppermute(block, axis, [(i, target(i)) for i in range(count)])


def neighbours(plane):
    rows, lanes = plane.shape
    beside = pltpu.roll(plane, 1, 0) + pltpu.roll(plane, rows - 1, 0)
    return beside + pltpu.roll(plane, 1, 1) + pltpu.roll(plane, lanes - 1, 1)


def filter_kernel(shares, stripes, field, low, high, pot, pot_low, pot_high, pot_seam, *rest):
    routes = len(shares)
    seams, outs = rest[:routes], rest[routes : routes + stripes]
    zero, one, two, three, local = rest[routes + stripes :]
    me = lax.axis_index("band")
    at = lax.rem(lax.axis_index("domain"), SIDE * SIDE)
    at_low, at_high = at == 0, at == SIDE * SIDE - 1
    planes = field.shape[1]
    top = planes + 2 * DEPTH
    width = outs[0].shape[2]
    own = pl.ds(DEPTH, planes)
    local[own] = 0.8 * pot[...] - 1.2
    local[:DEPTH] = 0.8 * jnp.where(at_low, pot_seam[...], pot_low[...]) - 1.2
    local[planes + DEPTH :] = 0.8 * jnp.where(at_high, pot_seam[...], pot_high[...]) - 1.2

    def one_orbital(orbital, seam_plane):
        zero[own] = field[orbital]
        for k in range(DEPTH):
            zero[k] = jnp.where(at_low, seam_plane(k), low[orbital, k])
            zero[planes + DEPTH + k] = jnp.where(at_high, seam_plane(k), high[orbital, k])
        for k in range(1, top - 1):
            beside = zero[k - 1] + zero[k + 1] + neighbours(zero[k])
            one[k] = (0.5 * local[k]) * zero[k] - 0.2 * beside
        for k in range(2, top - 2):
            beside = one[k - 1] + one[k + 1] + neighbours(one[k])
            two[k] = local[k] * one[k] - 0.4 * beside - zero[k]
        for k in range(3, top - 3):
            beside = two[k - 1] + two[k + 1] + neighbours(two[k])
            three[k - 3] = local[k] * two[k] - 0.4 * beside - one[k]
        for slot in range(stripes):
            start = pl.multiple_of(jnp.bitwise_xor(me, slot) * width, width)
            outs[slot][orbital] = three[:, pl.ds(start, width), :]

    first = 0
    for share, seam in zip(shares, seams):

        def step(i, carry, first=first, seam=seam):
            one_orbital(first + i, lambda k: seam[i, k])
            return carry

        lax.fori_loop(0, share, step, 0)
        first += share


def filtered_stripes(field, low, high, pots, seams, stripes):
    count, planes, rows, lanes = field.shape
    width = rows // stripes
    top = planes + 2 * DEPTH
    shares = [seam.shape[0] for seam in seams]
    shape = jax.ShapeDtypeStruct((count, planes, width, lanes), jnp.float32)
    return pl.pallas_call(
        functools.partial(filter_kernel, shares, stripes),
        out_shape=[shape] * stripes,
        scratch_shapes=[
            pltpu.VMEM((top, rows, lanes), jnp.float32),
            pltpu.VMEM((top, rows, lanes), jnp.float32),
            pltpu.VMEM((top, rows, lanes), jnp.float32),
            pltpu.VMEM((planes, rows, lanes), jnp.float32),
            pltpu.VMEM((top, rows, lanes), jnp.float32),
        ],
        compiler_params=pltpu.CompilerParams(vmem_limit_bytes=40 * 1024 * 1024),
    )(field, low, high, *pots, *seams)


def inner_pairs(step):
    half = SIDE * SIDE
    seam = half - 1 if step == 1 else 0
    return [(i, i + step) for i in range(2 * half) if i % half != seam]


def seam_pairs():
    half = SIDE * SIDE
    pairs = []
    for h in (0, 1):
        other = (1 - h) * half
        pairs += [(h * half + half - 1, other), (h * half, other + half - 1)]
    return pairs


def detour_pairs(route):
    half, last = SIDE * SIDE, SIDE - 1
    up, down = route * SIDE + last, (last - route) * SIDE
    out, back = [], []
    for h in (0, 1):
        other = (1 - h) * half
        out += [(h * half + half - 1, other + up), (h * half, other + down)]
        back += [(other + up, other), (other + down, other + half - 1)]
    return out, back


def halos(block):
    lows, highs = block[..., :DEPTH, :, :], block[..., block.shape[-3] - DEPTH :, :, :]
    low = lax.ppermute(highs, "domain", inner_pairs(1))
    high = lax.ppermute(lows, "domain", inner_pairs(-1))
    at = lax.rem(lax.axis_index("domain"), SIDE * SIDE)
    return low, high, jnp.where(at == 0, lows, highs)


def gram_kernel(pieces, cells, *rest):
    refs, (flat, gram) = rest[:-2], rest[-2:]
    me = lax.axis_index("band")
    lanes = refs[0].shape[1]
    share = refs[0].shape[0] // cells
    for index, ref in enumerate(refs):
        slot, piece = divmod(index, pieces)
        first = jnp.bitwise_xor(me, slot) * (share * pieces) + piece * share
        rows = pl.ds(pl.multiple_of(first, share), share)
        for r in range(cells):
            flat[rows, r * lanes : (r + 1) * lanes] = ref[pl.ds(r, share, stride=cells), :]
    whole = flat[...]
    gram[...] = lax.dot_general(
        whole,
        whole,
        (((1,), (1,)), ((), ())),
        precision=lax.Precision.HIGHEST,
        preferred_element_type=jnp.float32,
    )


def flat_and_gram(slots, orbitals):
    pieces = len(slots[0])
    _, planes, width, lanes = slots[0][0].shape
    cells = planes * width
    refs = [piece.reshape(-1, lanes) for slot in slots for piece in slot]
    return pl.pallas_call(
        functools.partial(gram_kernel, pieces, cells),
        out_shape=[
            jax.ShapeDtypeStruct((orbitals, cells * lanes), jnp.float32),
            jax.ShapeDtypeStruct((orbitals, orbitals), jnp.float32),
        ],
        compiler_params=pltpu.CompilerParams(vmem_limit_bytes=32 * 1024 * 1024),
    )(*refs)


def factor_kernel(panel, scale, gram, out, left, right):
    orbitals = gram.shape[0]
    row = lax.broadcasted_iota(jnp.int32, (orbitals, orbitals), 0)
    lane = lax.broadcasted_iota(jnp.int32, (orbitals, orbitals), 1)
    left[...] = gram[...]
    right[...] = jnp.where(row == lane, scale, 0.0)
    inner = lax.broadcasted_iota(jnp.int32, (panel, orbitals), 0)
    for start in range(0, orbitals, panel):
        stop = start + panel
        rows_left = left[start:stop]
        rows_right = right[start:stop]
        columns = [
            jnp.broadcast_to(rows_left[:, start + k : start + k + 1], (panel, orbitals))
            for k in range(panel)
        ]
        roots = jnp.zeros((panel, orbitals), jnp.float32)
        for j in range(panel):
            pivot = jnp.broadcast_to(columns[j][j : j + 1], (panel, orbitals))
            roots = jnp.where(inner == j, lax.rsqrt(pivot), roots)
            if j == panel - 1:
                break
            factor = jnp.where(inner > j, columns[j] / pivot, 0.0)
            for k in range(j + 1, panel):
                columns[k] = columns[k] - factor * columns[k][j : j + 1]
            rows_left = rows_left - factor * rows_left[j : j + 1]
            rows_right = rows_right - factor * rows_right[j : j + 1]
        rows_left = rows_left * roots
        rows_right = rows_right * roots
        out[start:stop] = rows_right
        if stop < orbitals:
            for ref, rows in ((left, rows_left), (right, rows_right)):
                update = lax.dot_general(
                    rows_left,
                    rows,
                    (((0,), (0,)), ((), ())),
                    precision=lax.Precision.HIGHEST,
                    preferred_element_type=jnp.float32,
                )
                ref[stop:] = ref[stop:] - update[stop:]


def scaled_inverse(gram, scale):
    orbitals = gram.shape[0]
    return pl.pallas_call(
        functools.partial(factor_kernel, PANEL, scale),
        out_shape=jax.ShapeDtypeStruct(gram.shape, jnp.float32),
        scratch_shapes=[pltpu.VMEM((orbitals, orbitals), jnp.float32)] * 2,
        compiler_params=pltpu.CompilerParams(vmem_limit_bytes=32 * 1024 * 1024),
    )(gram)


def rotate_kernel(cells, inverse, flat, out):
    orbitals = inverse.shape[0]
    lanes = out.shape[1]
    solved = jnp.dot(
        inverse[...],
        flat[...],
        precision=lax.Precision.HIGHEST,
        preferred_element_type=jnp.float32,
    )
    for r in range(cells):
        out[pl.ds(r, orbitals, stride=cells), :] = solved[:, r * lanes : (r + 1) * lanes]


def rotated(inverse, flat, lanes):
    orbitals, columns = flat.shape
    cells = columns // lanes
    return pl.pallas_call(
        functools.partial(rotate_kernel, cells),
        out_shape=jax.ShapeDtypeStruct((orbitals * cells, lanes), jnp.float32),
        compiler_params=pltpu.CompilerParams(vmem_limit_bytes=32 * 1024 * 1024),
    )(inverse, flat)


def summed(gram):
    for bit in (1, 2, 4):
        gram = gram + permuted(gram, "band", lambda i: i ^ bit)
    side = SIDE
    turned = [
        permuted(gram, "domain", lambda i: i // side * side + (i + k) % side) for k in (1, 2, 3)
    ]
    gram = (gram + turned[0]) + (turned[1] + turned[2])
    plane = side * side
    turned = [
        permuted(gram, "domain", lambda i: i // plane * plane + (i + k * side) % plane)
        for k in (1, 2, 3)
    ]
    gram = (gram + turned[0]) + (turned[1] + turned[2])
    return gram + permuted(gram, "domain", lambda i: i ^ plane)


def body(orbitals, potential):
    stripes = lax.axis_size("band")
    own, planes, ny_all, nx_all = orbitals.shape
    orb_total = own * stripes
    cell_total = planes * lax.axis_size("domain") * ny_all * nx_all

    pot_low, pot_high, pot_seam = halos(potential)
    pots = (potential, pot_low, pot_high, lax.ppermute(pot_seam, "domain", seam_pairs()))
    share = own // PARTS
    pieces = []
    for part in range(PARTS):
        field = orbitals[part * share : (part + 1) * share]
        low, high, across = halos(field)
        seams, first = [], 0
        for route, width in enumerate(SHARES):
            block = across[first : first + width]
            first += width
            if route == 0:
                seams.append(lax.ppermute(block, "domain", seam_pairs()))
            else:
                out, back = detour_pairs(route - 1)
                seams.append(lax.ppermute(lax.ppermute(block, "domain", out), "domain", back))
        slots = filtered_stripes(field, low, high, pots, seams, stripes)
        pieces.append(
            [slots[0]]
            + [permuted(slots[k], "band", lambda i: i ^ k) for k in range(1, stripes)]
        )
    slots = [[piece[k] for piece in pieces] for k in range(stripes)]
    flat, partial_gram = flat_and_gram(slots, orb_total)
    gram = summed(partial_gram)
    inverse = scaled_inverse(gram, math.sqrt(cell_total))
    return rotated(inverse, flat, nx_all).reshape(
        orb_total, planes, ny_all // stripes, nx_all
    )


def solution(mesh):
    in_specs = (P("band", "domain", None, None), P("domain", None, None))
    out_specs = P(None, "domain", "band", None)
    return jax.shard_map(body, mesh=mesh, in_specs=in_specs, out_specs=out_specs, check_vma=False)
```

time: 217 us -> 236 us (1.088)
  starting transfers between devices: 32.8 us -> 82.4 us
  other arithmetic: 22.9 us -> 2.65 us
  waiting for transfers between devices: 145 us -> 132 us
  Pallas kernels: 14 us -> 18.1 us
  local copies, waits for them, and re-layouts: 2.53 us -> 0.13 us
    ppermute x21 -> x17, waiting for transfers between devices: 145 us -> 65 us  [permuted(): return lax.ppermute(block, axis, [(i, target(i)) for i in range(count)])]
    ppermute x0 -> x12, waiting for transfers between devices: none -> 66.6 us  [the longest x3 31.7 us: body(): lax.ppermute(block, 'domain', out)]
    ppermute x0 -> x12, starting transfers between devices: none -> 45.6 us  [the longest x3 17.8 us: body(): lax.ppermute(block, 'domain', out)]
    another operation x5 -> x0, other arithmetic: 22.9 us -> none  [the longest x3 12.4 us: body(): lower = jnp.linalg.cholesky(gram)]
    pallas_call x1 -> x2, Pallas kernels: 6.72 us -> 10.8 us  [the longest x1 6.61 us: filtered_stripes(): pl.pallas_call(functools.partial(filter_kernel, shares, stripes), out_sha...]
    ppermute x21 -> x17, starting transfers between devices: 32.8 us -> 36.9 us  [permuted(): return lax.ppermute(block, axis, [(i, target(i)) for i in range(count)])]
    select_n x0 -> x2, other arithmetic: none -> 2.59 us  [halos(): return (low, high, jnp.where(at == 0, lows, highs))]
  transfers between devices with their start and end apart: 21 -> 29, of which waited for: 17 -> 21; matrix products, arithmetic and copies ran while one was open for 0% -> 0% of each run, Pallas kernels for 0% -> 0%
where the time goes in v2:
time: 236 us; the launch traced here: 235 us
  waiting for transfers between devices  132 us (56%)
  starting transfers between devices  82.4 us (35%)
  Pallas kernels  18.1 us (8%)
  other arithmetic  2.65 us (1%)
    ppermute x17, waiting for transfers between devices, permuted(): return lax.ppermute(block, axis, [(i, target(i)) for i in range(count)])  65 us
    ppermute x17, starting transfers between devices, permuted(): return lax.ppermute(block, axis, [(i, target(i)) for i in range(count)])  36.9 us
    ppermute x3, waiting for transfers between devices, body(): lax.ppermute(block, 'domain', out)  31.7 us
    ppermute x3, starting transfers between devices, body(): lax.ppermute(block, 'domain', out)  17.8 us
    ppermute x3, waiting for transfers between devices, body(): lax.ppermute(lax.ppermute(block, 'domain', out), 'domain', back)  14.1 us
    ppermute x1, starting transfers between devices, body(): lax.ppermute(pot_seam, 'domain', seam_pairs())  13.9 us
    ppermute x2, waiting for transfers between devices, halos(): low = lax.ppermute(highs, 'domain', inner_pairs(1))  13.2 us
    pallas_call x1, Pallas kernels, filtered_stripes(): pl.pallas_call(functools.partial(filter_kernel, shares, stripes), out_sha...  6.61 us
  transfers between devices with their start and end apart: 29, of which 21 were waited for; matrix products, arithmetic and copies ran while one was open for 0% of the time, Pallas kernels for 0%

profile of v2, /device:TPU:32, one launch (start us, length us, event | category | flops | bytes accessed | tf_op | source)
XLA Modules:
  0.0 235.2 jit_solution(4480639943171572859)
XLA Ops:
  0.0 2.6 %broadcast_select_fusion = (f32[16,3,64,128]{3,2,1,0:T(8,128)S(1)}, f32[16,3,64,128]{3,2,1,0:T(8,128)S(1)}, f32[16,3,64,128]{3,2,1,0:T(8,128)S(1)}) fusion(pred[]{:T(512)S(6)} %eq.4, f32[16,4,64,128]{3,2,1,0:T(8,128)} %field.1), kind=kLoop, calls=%fused_computation | loop fusion | flops 393216 | bytes 7864321 | tf_op jit(solution)/shard_map/jit(_where)/select_n | solution.py:124
  2.6 3.6 %collective-permute-start = (f32[16,3,64,128]{3,2,1,0:T(8,128)S(1)}, f32[16,3,64,128]{3,2,1,0:T(8,128)S(1)}, u32[]{:S(2)}, u32[]{:S(2)}) collective-permute-start(f32[16,3,64,128]{3,2,1,0:T(8,128)S(1)} %get-tuple-element.26), channel_id=1, source_target_pairs={{0,8},{8,16},{16,24},{24,32},{32,40},{40,48},{48,56},{56,64},{64,7... | collective-permute-start | bytes 4718600 | tf_op jit(solution)/shard_map/ppermute | solution.py:121
  6.2 1.3 collective-permute-start.1
  7.5 13.9 %collective-permute-start.4 = (f32[3,64,128]{2,1,0:T(8,128)S(1)}, f32[3,64,128]{2,1,0:T(8,128)S(1)}, u32[]{:S(2)}, u32[]{:S(2)}) collective-permute-start(f32[3,64,128]{2,1,0:T(8,128)S(1)} %get-tuple-element.30), channel_id=1, source_target_pairs={{120,128},{0,248},{248,0},{128,120},{121,129},{1,249},{249,1},{129... | collective-permute-start | bytes 294920 | tf_op jit(solution)/shard_map/ppermute | solution.py:261
  21.4 1.3 collective-permute-start.2
  22.7 1.3 collective-permute-start.3
  24.0 0.0 copy-start
  24.1 1.7 collective-permute-done.4.pot_seam
  25.7 2.8 %collective-permute-start.10 = (f32[3,3,64,128]{3,2,1,0:T(8,128)S(1)}, f32[3,3,64,128]{3,2,1,0:T(8,128)S(1)}, u32[]{:S(2)}, u32[]{:S(2)}) collective-permute-start(f32[3,3,64,128]{3,2,1,0:T(8,128)S(1)} %get-tuple-element.28), channel_id=1, source_target_pairs={{120,216},{0,160},{248,88},{128,32},{121,217},{1,161},{249,89},{12... | collective-permute-start | bytes 884744 | tf_op jit(solution)/shard_map/ppermute | solution.py:275
  28.6 13.2 %collective-permute-done.2.pot_low = f32[3,64,128]{2,1,0:T(8,128)S(1)} collective-permute-done((f32[3,64,128]{2,1,0:T(8,128)S(1)}, f32[3,64,128]{2,1,0:T(8,128)S(1)}, u32[]{:S(2)}, u32[]{:S(2)}) %collective-permute-start.2) | collective-permute-done | bytes 98336 | tf_op jit(solution)/shard_map/ppermute | solution.py:121
  41.8 13.7 %collective-permute-start.8 = (f32[3,3,64,128]{3,2,1,0:T(8,128)S(1)}, f32[3,3,64,128]{3,2,1,0:T(8,128)S(1)}, u32[]{:S(2)}, u32[]{:S(2)}) collective-permute-start(f32[3,3,64,128]{3,2,1,0:T(8,128)S(1)} %get-tuple-element.29), channel_id=1, source_target_pairs={{120,184},{0,192},{248,56},{128,64},{121,185},{1,193},{249,57},{12... | collective-permute-start | bytes 884744 | tf_op jit(solution)/shard_map/ppermute | solution.py:275
  55.5 0.0 collective-permute-done.3.pot_high
  55.5 1.3 collective-permute-start.6
  56.9 0.0 collective-permute-done.10
  56.9 1.3 collective-permute-start.11
  58.2 14.0 %collective-permute-done.8 = f32[3,3,64,128]{3,2,1,0:T(8,128)S(1)} collective-permute-done((f32[3,3,64,128]{3,2,1,0:T(8,128)S(1)}, f32[3,3,64,128]{3,2,1,0:T(8,128)S(1)}, u32[]{:S(2)}, u32[]{:S(2)}) %collective-permute-start.8) | collective-permute-done | bytes 294944 | tf_op jit(solution)/shard_map/ppermute | solution.py:275
  72.3 2.5 %collective-permute-start.5 = (f32[6,3,64,128]{3,2,1,0:T(8,128)S(1)}, f32[6,3,64,128]{3,2,1,0:T(8,128)S(1)}, u32[]{:S(2)}, u32[]{:S(2)}) collective-permute-start(f32[6,3,64,128]{3,2,1,0:T(8,128)S(1)} %slice.32), channel_id=1, source_target_pairs={{120,128},{0,248},{248,0},{128,120},{121,129},{1,249},{249,1},{129... | collective-permute-start | bytes 1769480 | tf_op jit(solution)/shard_map/ppermute | solution.py:272
  74.8 17.7 %collective-permute-done.6 = f32[4,3,64,128]{3,2,1,0:T(8,128)S(1)} collective-permute-done((f32[4,3,64,128]{3,2,1,0:T(8,128)S(1)}, f32[4,3,64,128]{3,2,1,0:T(8,128)S(1)}, u32[]{:S(2)}, u32[]{:S(2)}) %collective-permute-start.6) | collective-permute-done | bytes 393248 | tf_op jit(solution)/shard_map/ppermute | solution.py:275
  92.5 1.3 collective-permute-start.7
  93.7 0.0 collective-permute-done.11.rest_3_
  93.8 1.3 collective-permute-start.9
  95.1 10.6 %collective-permute-done.9.rest_2_ = f32[3,3,64,128]{3,2,1,0:T(8,128)S(1)} collective-permute-done((f32[3,3,64,128]{3,2,1,0:T(8,128)S(1)}, f32[3,3,64,128]{3,2,1,0:T(8,128)S(1)}, u32[]{:S(2)}, u32[]{:S(2)}) %collective-permute-start.9) | collective-permute-done | bytes 294944 | tf_op jit(solution)/shard_map/ppermute | solution.py:275
  105.7 5.9 %collective-permute-done.5.rest_0_ = f32[6,3,64,128]{3,2,1,0:T(8,128)S(1)} collective-permute-done((f32[6,3,64,128]{3,2,1,0:T(8,128)S(1)}, f32[6,3,64,128]{3,2,1,0:T(8,128)S(1)}, u32[]{:S(2)}, u32[]{:S(2)}) %collective-permute-start.5) | collective-permute-done | bytes 589856 | tf_op jit(solution)/shard_map/ppermute | solution.py:272
  111.6 3.5 %collective-permute-done.7.rest_1_ = f32[4,3,64,128]{3,2,1,0:T(8,128)S(1)} collective-permute-done((f32[4,3,64,128]{3,2,1,0:T(8,128)S(1)}, f32[4,3,64,128]{3,2,1,0:T(8,128)S(1)}, u32[]{:S(2)}, u32[]{:S(2)}) %collective-permute-start.7) | collective-permute-done | bytes 393248 | tf_op jit(solution)/shard_map/ppermute | solution.py:275
  115.1 0.0 collective-permute-done.low
  115.1 0.0 collective-permute-done.1.high
  115.1 6.6 %shard_map.28 = (f32[16,4,8,128]{3,2,1,0:T(8,128)S(1)}, f32[16,4,8,128]{3,2,1,0:T(8,128)S(1)}, f32[16,4,8,128]{3,2,1,0:T(8,128)S(1)}, f32[16,4,8,128]{3,2,1,0:T(...) custom-call(f32[16,4,64,128]{3,2,1,0:T(8,128)S(1)} %copy-done, ...), custom_call_target="tpu_custom_call" | custom-call | tf_op jit(solution)/shard_map/pallas_call | solution.py:79
  121.7 0.1 collective-permute-start.12
  121.8 0.1 collective-permute-start.13
  121.9 1.8 collective-permute-start.14
  123.7 17.5 %collective-permute-start.15 = (f32[16,4,8,128]{3,2,1,0:T(8,128)S(1)}, f32[16,4,8,128]{3,2,1,0:T(8,128)S(1)}, u32[]{:S(2)}, u32[]{:S(2)}) collective-permute-start(f32[16,4,8,128]{3,2,1,0:T(8,128)S(1)} %get-tuple-element.19), channel_id=1, source_target_pairs={{0,4},{1,5},{2,6},{3,7},{4,0},{5,1},{6,2},{7,3},{8,12},{9,13},{10,... | collective-permute-start | bytes 786440 | tf_op jit(solution)/shard_map/ppermute | solution.py:20
  141.2 0.0 collective-permute-start.16
  141.2 0.0 collective-permute-done.12
  141.2 2.9 %collective-permute-start.17 = (f32[16,4,8,128]{3,2,1,0:T(8,128)S(1)}, f32[16,4,8,128]{3,2,1,0:T(8,128)S(1)}, u32[]{:S(2)}, u32[]{:S(2)}) collective-permute-start(f32[16,4,8,128]{3,2,1,0:T(8,128)S(1)} %get-tuple-element.21), channel_id=1, source_target_pairs={{0,6},{1,7},{2,4},{3,5},{4,2},{5,3},{6,0},{7,1},{8,14},{9,15},{10,... | collective-permute-start | bytes 786440 | tf_op jit(solution)/shard_map/ppermute | solution.py:20
  144.1 0.0 collective-permute-done.13
  144.1 3.5 %collective-permute-start.18 = (f32[16,4,8,128]{3,2,1,0:T(8,128)S(1)}, f32[16,4,8,128]{3,2,1,0:T(8,128)S(1)}, u32[]{:S(2)}, u32[]{:S(2)}) collective-permute-start(f32[16,4,8,128]{3,2,1,0:T(8,128)S(1)} %get-tuple-element.22), channel_id=1, source_target_pairs={{0,7},{1,6},{2,5},{3,4},{4,3},{5,2},{6,1},{7,0},{8,15},{9,14},{10,... | collective-permute-start | bytes 786440 | tf_op jit(solution)/shard_map/ppermute | solution.py:20
  147.6 0.0 collective-permute-done.14
  147.6 22.8 %collective-permute-done.15 = f32[16,4,8,128]{3,2,1,0:T(8,128)S(1)} collective-permute-done((f32[16,4,8,128]{3,2,1,0:T(8,128)S(1)}, f32[16,4,8,128]{3,2,1,0:T(8,128)S(1)}, u32[]{:S(2)}, u32[]{:S(2)}) %collective-permute-start.15) | collective-permute-done | bytes 262176 | tf_op jit(solution)/shard_map/ppermute | solution.py:20
  170.4 5.6 %collective-permute-done.16 = f32[16,4,8,128]{3,2,1,0:T(8,128)S(1)} collective-permute-done((f32[16,4,8,128]{3,2,1,0:T(8,128)S(1)}, f32[16,4,8,128]{3,2,1,0:T(8,128)S(1)}, u32[]{:S(2)}, u32[]{:S(2)}) %collective-permute-start.16) | collective-permute-done | bytes 262176 | tf_op jit(solution)/shard_map/ppermute | solution.py:20
  176.0 6.3 %collective-permute-done.17 = f32[16,4,8,128]{3,2,1,0:T(8,128)S(1)} collective-permute-done((f32[16,4,8,128]{3,2,1,0:T(8,128)S(1)}, f32[16,4,8,128]{3,2,1,0:T(8,128)S(1)}, u32[]{:S(2)}, u32[]{:S(2)}) %collective-permute-start.17) | collective-permute-done | bytes 262176 | tf_op jit(solution)/shard_map/ppermute | solution.py:20
  182.3 5.0 %collective-permute-done.18 = f32[16,4,8,128]{3,2,1,0:T(8,128)S(1)} collective-permute-done((f32[16,4,8,128]{3,2,1,0:T(8,128)S(1)}, f32[16,4,8,128]{3,2,1,0:T(8,128)S(1)}, u32[]{:S(2)}, u32[]{:S(2)}) %collective-permute-start.18) | collective-permute-done | bytes 262176 | tf_op jit(solution)/shard_map/ppermute | solution.py:20
  187.3 3.1 %shard_map.29 = (f32[128,4096]{1,0:T(8,128)S(1)}, f32[128,128]{1,0:T(8,128)S(1)}) custom-call(f32[512,128]{1,0:T(8,128)S(1)} %bitcast.9, f32[512,128]{1,0:T(8,128)S(1)} %bitcast.10, f32[512,128]{1,0:T(8,128)S(1)} %bitcast.11, f32[512,128]{1,0:T(8,128)S(1)} %bitcast.12, f32[512,128]{1,0:T(8,128)S(1)} %bitcast.13, f32[512,128]{1,0:T(8,128)S(1)} %bitcast.14, ...), custom_call_target="tpu_custom_call" | custom-call | tf_op jit(solution)/shard_map/pallas_call | solution.py:153
  190.4 0.2 collective-permute-start.19
  190.6 1.1 collective-permute-done.19
  191.8 0.1 collective-permute-start.20
  191.9 4.3 %collective-permute-done.20 = f32[128,128]{1,0:T(8,128)S(1)} collective-permute-done((f32[128,128]{1,0:T(8,128)S(1)}, f32[128,128]{1,0:T(8,128)S(1)}, u32[]{:S(2)}, u32[]{:S(2)}) %collective-permute-start.20) | collective-permute-done | bytes 65568 | tf_op jit(solution)/shard_map/ppermute | solution.py:20
  196.1 1.2 collective-permute-start.21
  197.3 4.2 %collective-permute-done.21 = f32[128,128]{1,0:T(8,128)S(1)} collective-permute-done((f32[128,128]{1,0:T(8,128)S(1)}, f32[128,128]{1,0:T(8,128)S(1)}, u32[]{:S(2)}, u32[]{:S(2)}) %collective-permute-start.21) | collective-permute-done | bytes 65568 | tf_op jit(solution)/shard_map/ppermute | solution.py:20
  201.6 0.1 collective-permute-start.24
  201.7 0.1 collective-permute-start.23
  201.8 1.9 collective-permute-start.22
  203.7 2.2 collective-permute-done.24
  205.9 1.6 collective-permute-done.23
  207.5 1.1 collective-permute-done.22
  208.6 3.8 %collective-permute-start.27 = (f32[128,128]{1,0:T(8,128)S(1)}, f32[128,128]{1,0:T(8,128)S(1)}, u32[]{:S(2)}, u32[]{:S(2)}) collective-permute-start(f32[128,128]{1,0:T(8,128)S(1)} %add_add_fusion.1), channel_id=1, source_target_pairs={{0,96},{8,104},{16,112},{24,120},{32,0},{40,8},{48,16},{56,24},{64... | collective-permute-start | bytes 196616 | tf_op jit(solution)/shard_map/ppermute | solution.py:20
  212.4 0.0 collective-permute-start.26
  212.4 1.0 collective-permute-start.25
  213.3 1.6 collective-permute-done.27
  214.9 3.4 %collective-permute-done.26 = f32[128,128]{1,0:T(8,128)S(1)} collective-permute-done((f32[128,128]{1,0:T(8,128)S(1)}, f32[128,128]{1,0:T(8,128)S(1)}, u32[]{:S(2)}, u32[]{:S(2)}) %collective-permute-start.26) | collective-permute-done | bytes 65568 | tf_op jit(solution)/shard_map/ppermute | solution.py:20
  218.2 0.3 collective-permute-done.25
  218.6 2.7 %collective-permute-start.28 = (f32[128,128]{1,0:T(8,128)S(1)}, f32[128,128]{1,0:T(8,128)S(1)}, u32[]{:S(2)}, u32[]{:S(2)}) collective-permute-start(f32[128,128]{1,0:T(8,128)S(1)} %add_add_fusion), channel_id=1, source_target_pairs={{0,128},{8,136},{16,144},{24,152},{32,160},{40,168},{48,176},{56,1... | collective-permute-start | bytes 196616 | tf_op jit(solution)/shard_map/ppermute | solution.py:20
  221.3 5.6 %collective-permute-done.28 = f32[128,128]{1,0:T(8,128)S(1)} collective-permute-done((f32[128,128]{1,0:T(8,128)S(1)}, f32[128,128]{1,0:T(8,128)S(1)}, u32[]{:S(2)}, u32[]{:S(2)}) %collective-permute-start.28) | collective-permute-done | bytes 65568 | tf_op jit(solution)/shard_map/ppermute | solution.py:20
  226.8 4.2 %shard_map.30.inverse = f32[128,128]{1,0:T(8,128)S(1)} custom-call(f32[128,128]{1,0:T(8,128)S(1)} %add.39.gram), custom_call_target="tpu_custom_call" | custom-call | tf_op jit(solution)/shard_map/pallas_call | solution.py:206
  231.0 4.2 %shard_map.31 = f32[4096,128]{1,0:T(8,128)} custom-call(f32[128,128]{1,0:T(8,128)S(1)} %shard_map.30.inverse, f32[128,4096]{1,0:T(8,128)S(1)} %get-tuple-element.24.flat), custom_call_target="tpu_custom_call" | custom-call | tf_op jit(solution)/shard_map/pallas_call | solution.py:230
  (13 shorter events, 0.2 us)
Async XLA Ops:
  0.0 7.5 %copy-start.1 = (f32[4,64,128]{2,1,0:T(8,128)S(1)}, f32[4,64,128]{2,1,0:T(8,128)}, u32[]{:S(2)}) copy-start(f32[4,64,128]{2,1,0:T(8,128)} %pot.1) | copy-start | bytes 393220
  2.6 112.5 %collective-permute-start = (f32[16,3,64,128]{3,2,1,0:T(8,128)S(1)}, f32[16,3,64,128]{3,2,1,0:T(8,128)S(1)}, u32[]{:S(2)}, u32[]{:S(2)}) collective-permute-start(f32[16,3,64,128]{3,2,1,0:T(8,128)S(1)} %get-tuple-element.26), channel_id=1, source_target_pairs={{0,8},{8,16},{16,24},{24,32},{32,40},{40,48},{48,56},{56,64},{64,7... | collective-permute-start | bytes 4718600 | tf_op jit(solution)/shard_map/ppermute | solution.py:121
  6.2 108.9 %collective-permute-start.1 = (f32[16,3,64,128]{3,2,1,0:T(8,128)S(1)}, f32[16,3,64,128]{3,2,1,0:T(8,128)S(1)}, u32[]{:S(2)}, u32[]{:S(2)}) collective-permute-start(f32[16,3,64,128]{3,2,1,0:T(8,128)S(1)} %get-tuple-element.27), channel_id=1, source_target_pairs={{8,0},{16,8},{24,16},{32,24},{40,32},{48,40},{56,48},{64,56},{72,6... | collective-permute-start | bytes 4718600 | tf_op jit(solution)/shard_map/ppermute | solution.py:122
  7.5 18.2 %collective-permute-start.4 = (f32[3,64,128]{2,1,0:T(8,128)S(1)}, f32[3,64,128]{2,1,0:T(8,128)S(1)}, u32[]{:S(2)}, u32[]{:S(2)}) collective-permute-start(f32[3,64,128]{2,1,0:T(8,128)S(1)} %get-tuple-element.30), channel_id=1, source_target_pairs={{120,128},{0,248},{248,0},{128,120},{121,129},{1,249},{249,1},{129... | collective-permute-start | bytes 294920 | tf_op jit(solution)/shard_map/ppermute | solution.py:261
  21.4 20.4 %collective-permute-start.2 = (f32[3,64,128]{2,1,0:T(8,128)S(1)}, f32[3,64,128]{2,1,0:T(8,128)S(1)}, u32[]{:S(2)}, u32[]{:S(2)}) collective-permute-start(f32[3,64,128]{2,1,0:T(8,128)S(1)} %get-tuple-element.31), channel_id=1, source_target_pairs={{0,8},{8,16},{16,24},{24,32},{32,40},{40,48},{48,56},{56,64},{64,7... | collective-permute-start | bytes 294920 | tf_op jit(solution)/shard_map/ppermute | solution.py:121
  22.7 32.8 %collective-permute-start.3 = (f32[3,64,128]{2,1,0:T(8,128)S(1)}, f32[3,64,128]{2,1,0:T(8,128)S(1)}, u32[]{:S(2)}, u32[]{:S(2)}) collective-permute-start(f32[3,64,128]{2,1,0:T(8,128)S(1)} %get-tuple-element.32), channel_id=1, source_target_pairs={{8,0},{16,8},{24,16},{32,24},{40,32},{48,40},{56,48},{64,56},{72,6... | collective-permute-start | bytes 294920 | tf_op jit(solution)/shard_map/ppermute | solution.py:122
  24.0 91.1 %copy-start = (f32[16,4,64,128]{3,2,1,0:T(8,128)S(1)}, f32[16,4,64,128]{3,2,1,0:T(8,128)}, u32[]{:S(2)}) copy-start(f32[16,4,64,128]{3,2,1,0:T(8,128)} %field.1) | copy-start | bytes 6291460
  25.7 31.2 %collective-permute-start.10 = (f32[3,3,64,128]{3,2,1,0:T(8,128)S(1)}, f32[3,3,64,128]{3,2,1,0:T(8,128)S(1)}, u32[]{:S(2)}, u32[]{:S(2)}) collective-permute-start(f32[3,3,64,128]{3,2,1,0:T(8,128)S(1)} %get-tuple-element.28), channel_id=1, source_target_pairs={{120,216},{0,160},{248,88},{128,32},{121,217},{1,161},{249,89},{12... | collective-permute-start | bytes 884744 | tf_op jit(solution)/shard_map/ppermute | solution.py:275
  41.8 30.5 %collective-permute-start.8 = (f32[3,3,64,128]{3,2,1,0:T(8,128)S(1)}, f32[3,3,64,128]{3,2,1,0:T(8,128)S(1)}, u32[]{:S(2)}, u32[]{:S(2)}) collective-permute-start(f32[3,3,64,128]{3,2,1,0:T(8,128)S(1)} %get-tuple-element.29), channel_id=1, source_target_pairs={{120,184},{0,192},{248,56},{128,64},{121,185},{1,193},{249,57},{12... | collective-permute-start | bytes 884744 | tf_op jit(solution)/shard_map/ppermute | solution.py:275
  55.5 36.9 %collective-permute-start.6 = (f32[4,3,64,128]{3,2,1,0:T(8,128)S(1)}, f32[4,3,64,128]{3,2,1,0:T(8,128)S(1)}, u32[]{:S(2)}, u32[]{:S(2)}) collective-permute-start(f32[4,3,64,128]{3,2,1,0:T(8,128)S(1)} %slice.33), channel_id=1, source_target_pairs={{120,152},{0,224},{248,24},{128,96},{121,153},{1,225},{249,25},{12... | collective-permute-start | bytes 1179656 | tf_op jit(solution)/shard_map/ppermute | solution.py:275
  56.9 36.8 %collective-permute-start.11 = (f32[3,3,64,128]{3,2,1,0:T(8,128)S(1)}, f32[3,3,64,128]{3,2,1,0:T(8,128)S(1)}, u32[]{:S(2)}, u32[]{:S(2)}) collective-permute-start(f32[3,3,64,128]{3,2,1,0:T(8,128)S(1)} %collective-permute-done.10), channel_id=1, source_target_pairs={{216,128},{160,248},{88,0},{32,120},{217,129},{161,249},{89,1},{33... | collective-permute-start | bytes 884744 | tf_op jit(solution)/shard_map/ppermute | solution.py:275
  72.3 39.3 %collective-permute-start.5 = (f32[6,3,64,128]{3,2,1,0:T(8,128)S(1)}, f32[6,3,64,128]{3,2,1,0:T(8,128)S(1)}, u32[]{:S(2)}, u32[]{:S(2)}) collective-permute-start(f32[6,3,64,128]{3,2,1,0:T(8,128)S(1)} %slice.32), channel_id=1, source_target_pairs={{120,128},{0,248},{248,0},{128,120},{121,129},{1,249},{249,1},{129... | collective-permute-start | bytes 1769480 | tf_op jit(solution)/shard_map/ppermute | solution.py:272
  92.5 22.6 %collective-permute-start.7 = (f32[4,3,64,128]{3,2,1,0:T(8,128)S(1)}, f32[4,3,64,128]{3,2,1,0:T(8,128)S(1)}, u32[]{:S(2)}, u32[]{:S(2)}) collective-permute-start(f32[4,3,64,128]{3,2,1,0:T(8,128)S(1)} %collective-permute-done.6), channel_id=1, source_target_pairs={{152,128},{224,248},{24,0},{96,120},{153,129},{225,249},{25,1},{97... | collective-permute-start | bytes 1179656 | tf_op jit(solution)/shard_map/ppermute | solution.py:275
  93.8 11.9 %collective-permute-start.9 = (f32[3,3,64,128]{3,2,1,0:T(8,128)S(1)}, f32[3,3,64,128]{3,2,1,0:T(8,128)S(1)}, u32[]{:S(2)}, u32[]{:S(2)}) collective-permute-start(f32[3,3,64,128]{3,2,1,0:T(8,128)S(1)} %collective-permute-done.8), channel_id=1, source_target_pairs={{184,128},{192,248},{56,0},{64,120},{185,129},{193,249},{57,1},{65... | collective-permute-start | bytes 884744 | tf_op jit(solution)/shard_map/ppermute | solution.py:275
  121.7 19.5 %collective-permute-start.12 = (f32[16,4,8,128]{3,2,1,0:T(8,128)S(1)}, f32[16,4,8,128]{3,2,1,0:T(8,128)S(1)}, u32[]{:S(2)}, u32[]{:S(2)}) collective-permute-start(f32[16,4,8,128]{3,2,1,0:T(8,128)S(1)} %get-tuple-element.16), channel_id=1, source_target_pairs={{0,1},{1,0},{2,3},{3,2},{4,5},{5,4},{6,7},{7,6},{8,9},{9,8},{10,11... | collective-permute-start | bytes 786440 | tf_op jit(solution)/shard_map/ppermute | solution.py:20
  121.8 22.3 %collective-permute-start.13 = (f32[16,4,8,128]{3,2,1,0:T(8,128)S(1)}, f32[16,4,8,128]{3,2,1,0:T(8,128)S(1)}, u32[]{:S(2)}, u32[]{:S(2)}) collective-permute-start(f32[16,4,8,128]{3,2,1,0:T(8,128)S(1)} %get-tuple-element.17), channel_id=1, source_target_pairs={{0,2},{1,3},{2,0},{3,1},{4,6},{5,7},{6,4},{7,5},{8,10},{9,11},{10,... | collective-permute-start | bytes 786440 | tf_op jit(solution)/shard_map/ppermute | solution.py:20
  121.9 25.7 %collective-permute-start.14 = (f32[16,4,8,128]{3,2,1,0:T(8,128)S(1)}, f32[16,4,8,128]{3,2,1,0:T(8,128)S(1)}, u32[]{:S(2)}, u32[]{:S(2)}) collective-permute-start(f32[16,4,8,128]{3,2,1,0:T(8,128)S(1)} %get-tuple-element.18), channel_id=1, source_target_pairs={{0,3},{1,2},{2,1},{3,0},{4,7},{5,6},{6,5},{7,4},{8,11},{9,10},{10,... | collective-permute-start | bytes 786440 | tf_op jit(solution)/shard_map/ppermute | solution.py:20
  123.7 46.7 %collective-permute-start.15 = (f32[16,4,8,128]{3,2,1,0:T(8,128)S(1)}, f32[16,4,8,128]{3,2,1,0:T(8,128)S(1)}, u32[]{:S(2)}, u32[]{:S(2)}) collective-permute-start(f32[16,4,8,128]{3,2,1,0:T(8,128)S(1)} %get-tuple-element.19), channel_id=1, source_target_pairs={{0,4},{1,5},{2,6},{3,7},{4,0},{5,1},{6,2},{7,3},{8,12},{9,13},{10,... | collective-permute-start | bytes 786440 | tf_op jit(solution)/shard_map/ppermute | solution.py:20
  141.2 34.8 %collective-permute-start.16 = (f32[16,4,8,128]{3,2,1,0:T(8,128)S(1)}, f32[16,4,8,128]{3,2,1,0:T(8,128)S(1)}, u32[]{:S(2)}, u32[]{:S(2)}) collective-permute-start(f32[16,4,8,128]{3,2,1,0:T(8,128)S(1)} %get-tuple-element.20), channel_id=1, source_target_pairs={{0,5},{1,4},{2,7},{3,6},{4,1},{5,0},{6,3},{7,2},{8,13},{9,12},{10,... | collective-permute-start | bytes 786440 | tf_op jit(solution)/shard_map/ppermute | solution.py:20
  141.2 41.1 %collective-permute-start.17 = (f32[16,4,8,128]{3,2,1,0:T(8,128)S(1)}, f32[16,4,8,128]{3,2,1,0:T(8,128)S(1)}, u32[]{:S(2)}, u32[]{:S(2)}) collective-permute-start(f32[16,4,8,128]{3,2,1,0:T(8,128)S(1)} %get-tuple-element.21), channel_id=1, source_target_pairs={{0,6},{1,7},{2,4},{3,5},{4,2},{5,3},{6,0},{7,1},{8,14},{9,15},{10,... | collective-permute-start | bytes 786440 | tf_op jit(solution)/shard_map/ppermute | solution.py:20
  144.1 43.2 %collective-permute-start.18 = (f32[16,4,8,128]{3,2,1,0:T(8,128)S(1)}, f32[16,4,8,128]{3,2,1,0:T(8,128)S(1)}, u32[]{:S(2)}, u32[]{:S(2)}) collective-permute-start(f32[16,4,8,128]{3,2,1,0:T(8,128)S(1)} %get-tuple-element.22), channel_id=1, source_target_pairs={{0,7},{1,6},{2,5},{3,4},{4,3},{5,2},{6,1},{7,0},{8,15},{9,14},{10,... | collective-permute-start | bytes 786440 | tf_op jit(solution)/shard_map/ppermute | solution.py:20
  190.4 1.3 collective-permute-start.19
  191.8 4.4 %collective-permute-start.20 = (f32[128,128]{1,0:T(8,128)S(1)}, f32[128,128]{1,0:T(8,128)S(1)}, u32[]{:S(2)}, u32[]{:S(2)}) collective-permute-start(f32[128,128]{1,0:T(8,128)S(1)} %add.30), channel_id=1, source_target_pairs={{0,2},{1,3},{2,0},{3,1},{4,6},{5,7},{6,4},{7,5},{8,10},{9,11},{10,... | collective-permute-start | bytes 196616 | tf_op jit(solution)/shard_map/ppermute | solution.py:20
  196.1 5.4 %collective-permute-start.21 = (f32[128,128]{1,0:T(8,128)S(1)}, f32[128,128]{1,0:T(8,128)S(1)}, u32[]{:S(2)}, u32[]{:S(2)}) collective-permute-start(f32[128,128]{1,0:T(8,128)S(1)} %add.31), channel_id=1, source_target_pairs={{0,4},{1,5},{2,6},{3,7},{4,0},{5,1},{6,2},{7,3},{8,12},{9,13},{10,... | collective-permute-start | bytes 196616 | tf_op jit(solution)/shard_map/ppermute | solution.py:20
  201.6 4.3 %collective-permute-start.24 = (f32[128,128]{1,0:T(8,128)S(1)}, f32[128,128]{1,0:T(8,128)S(1)}, u32[]{:S(2)}, u32[]{:S(2)}) collective-permute-start(f32[128,128]{1,0:T(8,128)S(1)} %add.32), channel_id=1, source_target_pairs={{0,24},{8,0},{16,8},{24,16},{32,56},{40,32},{48,40},{56,48},{64,88... | collective-permute-start | bytes 196616 | tf_op jit(solution)/shard_map/ppermute | solution.py:20
  201.7 5.9 %collective-permute-start.23 = (f32[128,128]{1,0:T(8,128)S(1)}, f32[128,128]{1,0:T(8,128)S(1)}, u32[]{:S(2)}, u32[]{:S(2)}) collective-permute-start(f32[128,128]{1,0:T(8,128)S(1)} %add.32), channel_id=1, source_target_pairs={{0,16},{8,24},{16,0},{24,8},{32,48},{40,56},{48,32},{56,40},{64,80... | collective-permute-start | bytes 196616 | tf_op jit(solution)/shard_map/ppermute | solution.py:20
  201.8 6.8 %collective-permute-start.22 = (f32[128,128]{1,0:T(8,128)S(1)}, f32[128,128]{1,0:T(8,128)S(1)}, u32[]{:S(2)}, u32[]{:S(2)}) collective-permute-start(f32[128,128]{1,0:T(8,128)S(1)} %add.32), channel_id=1, source_target_pairs={{0,8},{8,16},{16,24},{24,0},{32,40},{40,48},{48,56},{56,32},{64,72... | collective-permute-start | bytes 196616 | tf_op jit(solution)/shard_map/ppermute | solution.py:20
  208.6 6.3 %collective-permute-start.27 = (f32[128,128]{1,0:T(8,128)S(1)}, f32[128,128]{1,0:T(8,128)S(1)}, u32[]{:S(2)}, u32[]{:S(2)}) collective-permute-start(f32[128,128]{1,0:T(8,128)S(1)} %add_add_fusion.1), channel_id=1, source_target_pairs={{0,96},{8,104},{16,112},{24,120},{32,0},{40,8},{48,16},{56,24},{64... | collective-permute-start | bytes 196616 | tf_op jit(solution)/shard_map/ppermute | solution.py:20
  212.4 5.9 %collective-permute-start.26 = (f32[128,128]{1,0:T(8,128)S(1)}, f32[128,128]{1,0:T(8,128)S(1)}, u32[]{:S(2)}, u32[]{:S(2)}) collective-permute-start(f32[128,128]{1,0:T(8,128)S(1)} %add_add_fusion.1), channel_id=1, source_target_pairs={{0,64},{8,72},{16,80},{24,88},{32,96},{40,104},{48,112},{56,120},{... | collective-permute-start | bytes 196616 | tf_op jit(solution)/shard_map/ppermute | solution.py:20
  212.4 6.2 %collective-permute-start.25 = (f32[128,128]{1,0:T(8,128)S(1)}, f32[128,128]{1,0:T(8,128)S(1)}, u32[]{:S(2)}, u32[]{:S(2)}) collective-permute-start(f32[128,128]{1,0:T(8,128)S(1)} %add_add_fusion.1), channel_id=1, source_target_pairs={{0,32},{8,40},{16,48},{24,56},{32,64},{40,72},{48,80},{56,88},{64,... | collective-permute-start | bytes 196616 | tf_op jit(solution)/shard_map/ppermute | solution.py:20
  218.6 8.3 %collective-permute-start.28 = (f32[128,128]{1,0:T(8,128)S(1)}, f32[128,128]{1,0:T(8,128)S(1)}, u32[]{:S(2)}, u32[]{:S(2)}) collective-permute-start(f32[128,128]{1,0:T(8,128)S(1)} %add_add_fusion), channel_id=1, source_target_pairs={{0,128},{8,136},{16,144},{24,152},{32,160},{40,168},{48,176},{56,1... | collective-permute-start | bytes 196616 | tf_op jit(solution)/shard_map/ppermute | solution.py:20

commit v3 on v2

--- a/solution.py
+++ b/solution.py
@@ -12,7 +12,7 @@
 PARTS = 1
 PANEL = 32
 SIDE = 4
-SHARES = (6, 4, 3, 3)
+SHARES = (7, 5, 4)
 
 
 def permuted(block, axis, target):
@@ -26,20 +26,21 @@
     return beside + pltpu.roll(plane, 1, 1) + pltpu.roll(plane, lanes - 1, 1)
 
 
-def filter_kernel(shares, stripes, field, low, high, pot, pot_low, pot_high, pot_seam, *rest):
+def filter_kernel(shares, stripes, field, pot, low, high, *rest):
     routes = len(shares)
     seams, outs = rest[:routes], rest[routes : routes + stripes]
     zero, one, two, three, local = rest[routes + stripes :]
     me = lax.axis_index("band")
     at = lax.rem(lax.axis_index("domain"), SIDE * SIDE)
     at_low, at_high = at == 0, at == SIDE * SIDE - 1
-    planes = field.shape[1]
+    count, planes = field.shape[:2]
     top = planes + 2 * DEPTH
     width = outs[0].shape[2]
     own = pl.ds(DEPTH, planes)
+    seam = seams[0][shares[0]]
     local[own] = 0.8 * pot[...] - 1.2
-    local[:DEPTH] = 0.8 * jnp.where(at_low, pot_seam[...], pot_low[...]) - 1.2
-    local[planes + DEPTH :] = 0.8 * jnp.where(at_high, pot_seam[...], pot_high[...]) - 1.2
+    local[:DEPTH] = 0.8 * jnp.where(at_low, seam, low[count]) - 1.2
+    local[planes + DEPTH :] = 0.8 * jnp.where(at_high, seam, high[count]) - 1.2
 
     def one_orbital(orbital, seam_plane):
         zero[own] = field[orbital]
@@ -70,14 +71,13 @@
         first += share
 
 
-def filtered_stripes(field, low, high, pots, seams, stripes):
+def filtered_stripes(field, pot, low, high, seams, stripes):
     count, planes, rows, lanes = field.shape
     width = rows // stripes
     top = planes + 2 * DEPTH
-    shares = [seam.shape[0] for seam in seams]
     shape = jax.ShapeDtypeStruct((count, planes, width, lanes), jnp.float32)
     return pl.pallas_call(
-        functools.partial(filter_kernel, shares, stripes),
+        functools.partial(filter_kernel, SHARES, stripes),
         out_shape=[shape] * stripes,
         scratch_shapes=[
             pltpu.VMEM((top, rows, lanes), jnp.float32),
@@ -87,7 +87,7 @@
             pltpu.VMEM((top, rows, lanes), jnp.float32),
         ],
         compiler_params=pltpu.CompilerParams(vmem_limit_bytes=40 * 1024 * 1024),
-    )(field, low, high, *pots, *seams)
+    )(field, pot, low, high, *seams)
 
 
 def inner_pairs(step):
@@ -116,12 +116,24 @@
     return out, back
 
 
-def halos(block):
-    lows, highs = block[..., :DEPTH, :, :], block[..., block.shape[-3] - DEPTH :, :, :]
+def halos(field, pot):
+    planes = field.shape[1]
+    both = jnp.concatenate([field, pot[None]])
+    lows, highs = both[:, :DEPTH], both[:, planes - DEPTH :]
+    at = lax.rem(lax.axis_index("domain"), SIDE * SIDE)
+    across = jnp.where(at == 0, lows, highs)
+    blocks, first = [], 0
+    for share in SHARES:
+        blocks.append(across[first : first + share])
+        first += share
+    blocks[0] = jnp.concatenate([blocks[0], across[first:]])
+    seams = [lax.ppermute(blocks[0], "domain", seam_pairs())]
+    for route, block in enumerate(blocks[1:]):
+        out, back = detour_pairs(route)
+        seams.append(lax.ppermute(lax.ppermute(block, "domain", out), "domain", back))
     low = lax.ppermute(highs, "domain", inner_pairs(1))
     high = lax.ppermute(lows, "domain", inner_pairs(-1))
-    at = lax.rem(lax.axis_index("domain"), SIDE * SIDE)
-    return low, high, jnp.where(at == 0, lows, highs)
+    return low, high, seams
 
 
 def gram_kernel(pieces, cells, *rest):
@@ -257,23 +269,12 @@
     orb_total = own * stripes
     cell_total = planes * lax.axis_size("domain") * ny_all * nx_all
 
-    pot_low, pot_high, pot_seam = halos(potential)
-    pots = (potential, pot_low, pot_high, lax.ppermute(pot_seam, "domain", seam_pairs()))
     share = own // PARTS
     pieces = []
     for part in range(PARTS):
         field = orbitals[part * share : (part + 1) * share]
-        low, high, across = halos(field)
-        seams, first = [], 0
-        for route, width in enumerate(SHARES):
-            block = across[first : first + width]
-            first += width
-            if route == 0:
-                seams.append(lax.ppermute(block, "domain", seam_pairs()))
-            else:
-                out, back = detour_pairs(route - 1)
-                seams.append(lax.ppermute(lax.ppermute(block, "domain", out), "domain", back))
-        slots = filtered_stripes(field, low, high, pots, seams, stripes)
+        low, high, seams = halos(field, potential)
+        slots = filtered_stripes(field, potential, low, high, seams, stripes)
         pieces.append(
             [slots[0]]
             + [permuted(slots[k], "band", lambda i: i ^ k) for k in range(1, stripes)]

time: 236 us -> 213 us (0.903)
  starting transfers between devices: 82.4 us -> 63 us
  waiting for transfers between devices: 132 us -> 128 us
    ppermute x8 -> x5, starting transfers between devices: 38.1 us -> 20.6 us  [the longest x2 13 us: halos(): lax.ppermute(block, 'domain', out)]
    ppermute x2 -> x1, waiting for transfers between devices: 13.2 us -> 0.01 us  [halos(): low = lax.ppermute(highs, 'domain', inner_pairs(1))]
    ppermute x8 -> x5, waiting for transfers between devices: 53.4 us -> 65.4 us  [the longest x2 39 us: halos(): lax.ppermute(block, 'domain', out)]
    ppermute x2 -> x1, starting transfers between devices: 4.88 us -> 4.65 us  [halos(): low = lax.ppermute(highs, 'domain', inner_pairs(1))]
  transfers between devices with their start and end apart: 29 -> 24, of which waited for: 21 -> 18; matrix products, arithmetic and copies ran while one was open for 0% -> 0% of each run, Pallas kernels for 0% -> 0%
where the time goes in v3:
time: 213 us
  waiting for transfers between devices  128 us (60%)
  starting transfers between devices  63 us (30%)
  Pallas kernels  18.1 us (8%)
  other arithmetic  2.88 us (1%)
    ppermute x17, waiting for transfers between devices, permuted(): return lax.ppermute(block, axis, [(i, target(i)) for i in range(count)])  62.9 us
    ppermute x2, waiting for transfers between devices, halos(): lax.ppermute(block, 'domain', out)  39 us
    ppermute x17, starting transfers between devices, permuted(): return lax.ppermute(block, axis, [(i, target(i)) for i in range(count)])  36.4 us
    ppermute x1, waiting for transfers between devices, halos(): seams = [lax.ppermute(blocks[0], 'domain', seam_pairs())]  13.2 us
    ppermute x2, waiting for transfers between devices, halos(): lax.ppermute(lax.ppermute(block, 'domain', out), 'domain', back)  13.2 us
    ppermute x2, starting transfers between devices, halos(): lax.ppermute(block, 'domain', out)  13 us
    pallas_call x1, Pallas kernels, filtered_stripes(): pl.pallas_call(functools.partial(filter_kernel, SHARES, stripes), out_sha...  6.63 us
    ppermute x1, starting transfers between devices, halos(): seams = [lax.ppermute(blocks[0], 'domain', seam_pairs())]  5.06 us
  transfers between devices with their start and end apart: 24, of which 18 were waited for; matrix products, arithmetic and copies ran while one was open for 0% of the time, Pallas kernels for 0%

profile of v3, /device:TPU:32, one launch (start us, length us, event | category | flops | bytes accessed | tf_op | source)
XLA Modules:
  0.0 212.6 jit_solution(11046879395801305547)
XLA Ops:
  0.0 2.7 %broadcast_select_fusion = (f32[17,3,64,128]{3,2,1,0:T(8,128)S(1)}, f32[17,3,64,128]{3,2,1,0:T(8,128)S(1)}, f32[17,3,64,128]{3,2,1,0:T(8,128)S(1)}) fusion(pred[]{:T(512)S(6)} %eq.3, f32[1,4,64,128]{3,2,1,0:T(8,128)} %bitcast.10, f32[16,4,64,128]{3,2,1,0:T(8,128)} %field.1), kind=kLoop, calls=%fused_computation.4 | loop fusion | flops 1253376 | bytes 7241729 | tf_op jit(solution)/shard_map/jit(_where)/select_n | solution.py:124
  2.7 1.3 collective-permute-start.1
  4.0 4.7 %collective-permute-start = (f32[17,3,64,128]{3,2,1,0:T(8,128)S(1)}, f32[17,3,64,128]{3,2,1,0:T(8,128)S(1)}, u32[]{:S(2)}, u32[]{:S(2)}) collective-permute-start(f32[17,3,64,128]{3,2,1,0:T(8,128)S(1)} %get-tuple-element.27), channel_id=1, source_target_pairs={{0,8},{8,16},{16,24},{24,32},{32,40},{40,48},{48,56},{56,64},{64,7... | collective-permute-start | bytes 5013512 | tf_op jit(solution)/shard_map/ppermute | solution.py:134
  8.8 11.6 %collective-permute-start.3 = (f32[5,3,64,128]{3,2,1,0:T(8,128)S(1)}, f32[5,3,64,128]{3,2,1,0:T(8,128)S(1)}, u32[]{:S(2)}, u32[]{:S(2)}) collective-permute-start(f32[5,3,64,128]{3,2,1,0:T(8,128)S(1)} %slice.28), channel_id=1, source_target_pairs={{120,152},{0,224},{248,24},{128,96},{121,153},{1,225},{249,25},{12... | collective-permute-start | bytes 1474568 | tf_op jit(solution)/shard_map/ppermute | solution.py:133
  20.4 0.0 copy-start
  20.4 0.0 copy-start.1
  20.4 1.4 collective-permute-start.5
  21.9 0.1 slice.26
  21.9 0.1 pad_maximum_fusion.1
  22.0 5.1 %collective-permute-start.2 = (f32[8,3,64,128]{3,2,1,0:T(8,128)S(1)}, f32[8,3,64,128]{3,2,1,0:T(8,128)S(1)}, u32[]{:S(2)}, u32[]{:S(2)}) collective-permute-start(f32[8,3,64,128]{3,2,1,0:T(8,128)S(1)} %pad_maximum_fusion.1), channel_id=1, source_target_pairs={{120,128},{0,248},{248,0},{128,120},{121,129},{1,249},{249,1},{129... | collective-permute-start | bytes 2359304 | tf_op jit(solution)/shard_map/ppermute | solution.py:130
  27.1 20.2 %collective-permute-done.3 = f32[5,3,64,128]{3,2,1,0:T(8,128)S(1)} collective-permute-done((f32[5,3,64,128]{3,2,1,0:T(8,128)S(1)}, f32[5,3,64,128]{3,2,1,0:T(8,128)S(1)}, u32[]{:S(2)}, u32[]{:S(2)}) %collective-permute-start.3) | collective-permute-done | bytes 491552 | tf_op jit(solution)/shard_map/ppermute | solution.py:133
  47.3 1.3 collective-permute-start.4
  48.6 18.8 %collective-permute-done.5 = f32[4,3,64,128]{3,2,1,0:T(8,128)S(1)} collective-permute-done((f32[4,3,64,128]{3,2,1,0:T(8,128)S(1)}, f32[4,3,64,128]{3,2,1,0:T(8,128)S(1)}, u32[]{:S(2)}, u32[]{:S(2)}) %collective-permute-start.5) | collective-permute-done | bytes 393248 | tf_op jit(solution)/shard_map/ppermute | solution.py:133
  67.4 1.3 collective-permute-start.6
  68.7 13.2 %collective-permute-done.6.rest_2_ = f32[4,3,64,128]{3,2,1,0:T(8,128)S(1)} collective-permute-done((f32[4,3,64,128]{3,2,1,0:T(8,128)S(1)}, f32[4,3,64,128]{3,2,1,0:T(8,128)S(1)}, u32[]{:S(2)}, u32[]{:S(2)}) %collective-permute-start.6) | collective-permute-done | bytes 393248 | tf_op jit(solution)/shard_map/ppermute | solution.py:133
  81.9 13.2 %collective-permute-done.2.rest_0_ = f32[8,3,64,128]{3,2,1,0:T(8,128)S(1)} collective-permute-done((f32[8,3,64,128]{3,2,1,0:T(8,128)S(1)}, f32[8,3,64,128]{3,2,1,0:T(8,128)S(1)}, u32[]{:S(2)}, u32[]{:S(2)}) %collective-permute-start.2) | collective-permute-done | bytes 786464 | tf_op jit(solution)/shard_map/ppermute | solution.py:130
  95.0 0.0 collective-permute-done.4.rest_1_
  95.0 0.0 collective-permute-done.1.high
  95.0 0.0 collective-permute-done.low
  95.0 0.0 copy-done
  95.1 0.0 copy-done.1
  95.1 6.6 %shard_map.28 = (f32[16,4,8,128]{3,2,1,0:T(8,128)S(1)}, f32[16,4,8,128]{3,2,1,0:T(8,128)S(1)}, f32[16,4,8,128]{3,2,1,0:T(8,128)S(1)}, f32[16,4,8,128]{3,2,1,0:T(...) custom-call(f32[16,4,64,128]{3,2,1,0:T(8,128)S(1)} %copy-done, ...), custom_call_target="tpu_custom_call" | custom-call | tf_op jit(solution)/shard_map/pallas_call | solution.py:79
  101.7 0.1 collective-permute-start.7
  101.8 5.2 %collective-permute-start.8 = (f32[16,4,8,128]{3,2,1,0:T(8,128)S(1)}, f32[16,4,8,128]{3,2,1,0:T(8,128)S(1)}, u32[]{:S(2)}, u32[]{:S(2)}) collective-permute-start(f32[16,4,8,128]{3,2,1,0:T(8,128)S(1)} %get-tuple-element.17), channel_id=1, source_target_pairs={{0,2},{1,3},{2,0},{3,1},{4,6},{5,7},{6,4},{7,5},{8,10},{9,11},{10,... | collective-permute-start | bytes 786440 | tf_op jit(solution)/shard_map/ppermute | solution.py:20
  107.0 0.1 collective-permute-start.9
  107.0 13.5 %collective-permute-start.10 = (f32[16,4,8,128]{3,2,1,0:T(8,128)S(1)}, f32[16,4,8,128]{3,2,1,0:T(8,128)S(1)}, u32[]{:S(2)}, u32[]{:S(2)}) collective-permute-start(f32[16,4,8,128]{3,2,1,0:T(8,128)S(1)} %get-tuple-element.19), channel_id=1, source_target_pairs={{0,4},{1,5},{2,6},{3,7},{4,0},{5,1},{6,2},{7,3},{8,12},{9,13},{10,... | collective-permute-start | bytes 786440 | tf_op jit(solution)/shard_map/ppermute | solution.py:20
  120.5 0.0 collective-permute-start.11
  120.5 0.0 collective-permute-done.7
  120.5 2.9 %collective-permute-start.12 = (f32[16,4,8,128]{3,2,1,0:T(8,128)S(1)}, f32[16,4,8,128]{3,2,1,0:T(8,128)S(1)}, u32[]{:S(2)}, u32[]{:S(2)}) collective-permute-start(f32[16,4,8,128]{3,2,1,0:T(8,128)S(1)} %get-tuple-element.21), channel_id=1, source_target_pairs={{0,6},{1,7},{2,4},{3,5},{4,2},{5,3},{6,0},{7,1},{8,14},{9,15},{10,... | collective-permute-start | bytes 786440 | tf_op jit(solution)/shard_map/ppermute | solution.py:20
  123.4 0.0 collective-permute-done.8
  123.4 3.5 %collective-permute-start.13 = (f32[16,4,8,128]{3,2,1,0:T(8,128)S(1)}, f32[16,4,8,128]{3,2,1,0:T(8,128)S(1)}, u32[]{:S(2)}, u32[]{:S(2)}) collective-permute-start(f32[16,4,8,128]{3,2,1,0:T(8,128)S(1)} %get-tuple-element.22), channel_id=1, source_target_pairs={{0,7},{1,6},{2,5},{3,4},{4,3},{5,2},{6,1},{7,0},{8,15},{9,14},{10,... | collective-permute-start | bytes 786440 | tf_op jit(solution)/shard_map/ppermute | solution.py:20
  126.9 0.0 collective-permute-done.9
  126.9 22.8 %collective-permute-done.10 = f32[16,4,8,128]{3,2,1,0:T(8,128)S(1)} collective-permute-done((f32[16,4,8,128]{3,2,1,0:T(8,128)S(1)}, f32[16,4,8,128]{3,2,1,0:T(8,128)S(1)}, u32[]{:S(2)}, u32[]{:S(2)}) %collective-permute-start.10) | collective-permute-done | bytes 262176 | tf_op jit(solution)/shard_map/ppermute | solution.py:20
  149.7 5.6 %collective-permute-done.11 = f32[16,4,8,128]{3,2,1,0:T(8,128)S(1)} collective-permute-done((f32[16,4,8,128]{3,2,1,0:T(8,128)S(1)}, f32[16,4,8,128]{3,2,1,0:T(8,128)S(1)}, u32[]{:S(2)}, u32[]{:S(2)}) %collective-permute-start.11) | collective-permute-done | bytes 262176 | tf_op jit(solution)/shard_map/ppermute | solution.py:20
  155.3 6.3 %collective-permute-done.12 = f32[16,4,8,128]{3,2,1,0:T(8,128)S(1)} collective-permute-done((f32[16,4,8,128]{3,2,1,0:T(8,128)S(1)}, f32[16,4,8,128]{3,2,1,0:T(8,128)S(1)}, u32[]{:S(2)}, u32[]{:S(2)}) %collective-permute-start.12) | collective-permute-done | bytes 262176 | tf_op jit(solution)/shard_map/ppermute | solution.py:20
  161.6 5.0 %collective-permute-done.13 = f32[16,4,8,128]{3,2,1,0:T(8,128)S(1)} collective-permute-done((f32[16,4,8,128]{3,2,1,0:T(8,128)S(1)}, f32[16,4,8,128]{3,2,1,0:T(8,128)S(1)}, u32[]{:S(2)}, u32[]{:S(2)}) %collective-permute-start.13) | collective-permute-done | bytes 262176 | tf_op jit(solution)/shard_map/ppermute | solution.py:20
  166.6 3.1 %shard_map.29 = (f32[128,4096]{1,0:T(8,128)S(1)}, f32[128,128]{1,0:T(8,128)S(1)}) custom-call(f32[512,128]{1,0:T(8,128)S(1)} %bitcast.11, f32[512,128]{1,0:T(8,128)S(1)} %bitcast.12, f32[512,128]{1,0:T(8,128)S(1)} %bitcast.13, f32[512,128]{1,0:T(8,128)S(1)} %bitcast.14, f32[512,128]{1,0:T(8,128)S(1)} %bitcast.15, f32[512,128]{1,0:T(8,128)S(1)} %bitcast.16, ...), custom_call_target="tpu_custom_call" | custom-call | tf_op jit(solution)/shard_map/pallas_call | solution.py:165
  169.7 0.2 collective-permute-start.14
  169.9 1.1 collective-permute-done.14
  171.1 0.1 collective-permute-start.15
  171.2 4.3 %collective-permute-done.15 = f32[128,128]{1,0:T(8,128)S(1)} collective-permute-done((f32[128,128]{1,0:T(8,128)S(1)}, f32[128,128]{1,0:T(8,128)S(1)}, u32[]{:S(2)}, u32[]{:S(2)}) %collective-permute-start.15) | collective-permute-done | bytes 65568 | tf_op jit(solution)/shard_map/ppermute | solution.py:20
  175.4 1.0 collective-permute-start.16
  176.4 4.2 %collective-permute-done.16 = f32[128,128]{1,0:T(8,128)S(1)} collective-permute-done((f32[128,128]{1,0:T(8,128)S(1)}, f32[128,128]{1,0:T(8,128)S(1)}, u32[]{:S(2)}, u32[]{:S(2)}) %collective-permute-start.16) | collective-permute-done | bytes 65568 | tf_op jit(solution)/shard_map/ppermute | solution.py:20
  180.7 0.3 collective-permute-start.19
  181.0 0.1 collective-permute-start.18
  181.1 1.9 collective-permute-start.17
  183.0 2.2 %collective-permute-done.19 = f32[128,128]{1,0:T(8,128)S(1)} collective-permute-done((f32[128,128]{1,0:T(8,128)S(1)}, f32[128,128]{1,0:T(8,128)S(1)}, u32[]{:S(2)}, u32[]{:S(2)}) %collective-permute-start.19) | collective-permute-done | bytes 65568 | tf_op jit(solution)/shard_map/ppermute | solution.py:20
  185.2 1.6 collective-permute-done.18
  186.8 1.1 collective-permute-done.17
  187.9 1.8 collective-permute-start.22
  189.7 0.0 collective-permute-start.21
  189.7 1.0 collective-permute-start.20
  190.7 1.6 collective-permute-done.22
  192.3 3.3 %collective-permute-done.21 = f32[128,128]{1,0:T(8,128)S(1)} collective-permute-done((f32[128,128]{1,0:T(8,128)S(1)}, f32[128,128]{1,0:T(8,128)S(1)}, u32[]{:S(2)}, u32[]{:S(2)}) %collective-permute-start.21) | collective-permute-done | bytes 65568 | tf_op jit(solution)/shard_map/ppermute | solution.py:20
  195.6 0.3 collective-permute-done.20
  195.9 4.9 %collective-permute-start.23 = (f32[128,128]{1,0:T(8,128)S(1)}, f32[128,128]{1,0:T(8,128)S(1)}, u32[]{:S(2)}, u32[]{:S(2)}) collective-permute-start(f32[128,128]{1,0:T(8,128)S(1)} %add_add_fusion), channel_id=1, source_target_pairs={{0,128},{8,136},{16,144},{24,152},{32,160},{40,168},{48,176},{56,1... | collective-permute-start | bytes 196616 | tf_op jit(solution)/shard_map/ppermute | solution.py:20
  200.8 3.4 %collective-permute-done.23 = f32[128,128]{1,0:T(8,128)S(1)} collective-permute-done((f32[128,128]{1,0:T(8,128)S(1)}, f32[128,128]{1,0:T(8,128)S(1)}, u32[]{:S(2)}, u32[]{:S(2)}) %collective-permute-start.23) | collective-permute-done | bytes 65568 | tf_op jit(solution)/shard_map/ppermute | solution.py:20
  204.2 4.2 %shard_map.30.inverse = f32[128,128]{1,0:T(8,128)S(1)} custom-call(f32[128,128]{1,0:T(8,128)S(1)} %add.39.gram), custom_call_target="tpu_custom_call" | custom-call | tf_op jit(solution)/shard_map/pallas_call | solution.py:218
  208.4 4.2 %shard_map.31 = f32[4096,128]{1,0:T(8,128)} custom-call(f32[128,128]{1,0:T(8,128)S(1)} %shard_map.30.inverse, f32[128,4096]{1,0:T(8,128)S(1)} %get-tuple-element.24.flat), custom_call_target="tpu_custom_call" | custom-call | tf_op jit(solution)/shard_map/pallas_call | solution.py:242
  (9 shorter events, 0.1 us)
Async XLA Ops:
  2.7 92.3 %collective-permute-start.1 = (f32[17,3,64,128]{3,2,1,0:T(8,128)S(1)}, f32[17,3,64,128]{3,2,1,0:T(8,128)S(1)}, u32[]{:S(2)}, u32[]{:S(2)}) collective-permute-start(f32[17,3,64,128]{3,2,1,0:T(8,128)S(1)} %get-tuple-element.26), channel_id=1, source_target_pairs={{8,0},{16,8},{24,16},{32,24},{40,32},{48,40},{56,48},{64,56},{72,6... | collective-permute-start | bytes 5013512 | tf_op jit(solution)/shard_map/ppermute | solution.py:135
  4.0 91.0 %collective-permute-start = (f32[17,3,64,128]{3,2,1,0:T(8,128)S(1)}, f32[17,3,64,128]{3,2,1,0:T(8,128)S(1)}, u32[]{:S(2)}, u32[]{:S(2)}) collective-permute-start(f32[17,3,64,128]{3,2,1,0:T(8,128)S(1)} %get-tuple-element.27), channel_id=1, source_target_pairs={{0,8},{8,16},{16,24},{24,32},{32,40},{40,48},{48,56},{56,64},{64,7... | collective-permute-start | bytes 5013512 | tf_op jit(solution)/shard_map/ppermute | solution.py:134
  8.8 38.5 %collective-permute-start.3 = (f32[5,3,64,128]{3,2,1,0:T(8,128)S(1)}, f32[5,3,64,128]{3,2,1,0:T(8,128)S(1)}, u32[]{:S(2)}, u32[]{:S(2)}) collective-permute-start(f32[5,3,64,128]{3,2,1,0:T(8,128)S(1)} %slice.28), channel_id=1, source_target_pairs={{120,152},{0,224},{248,24},{128,96},{121,153},{1,225},{249,25},{12... | collective-permute-start | bytes 1474568 | tf_op jit(solution)/shard_map/ppermute | solution.py:133
  20.4 74.7 %copy-start = (f32[16,4,64,128]{3,2,1,0:T(8,128)S(1)}, f32[16,4,64,128]{3,2,1,0:T(8,128)}, u32[]{:S(2)}) copy-start(f32[16,4,64,128]{3,2,1,0:T(8,128)} %field.1) | copy-start | bytes 6291460
  20.4 74.7 %copy-start.1 = (f32[4,64,128]{2,1,0:T(8,128)S(1)}, f32[4,64,128]{2,1,0:T(8,128)}, u32[]{:S(2)}) copy-start(f32[4,64,128]{2,1,0:T(8,128)} %pot.1) | copy-start | bytes 393220
  20.4 47.0 %collective-permute-start.5 = (f32[4,3,64,128]{3,2,1,0:T(8,128)S(1)}, f32[4,3,64,128]{3,2,1,0:T(8,128)S(1)}, u32[]{:S(2)}, u32[]{:S(2)}) collective-permute-start(f32[4,3,64,128]{3,2,1,0:T(8,128)S(1)} %slice.29), channel_id=1, source_target_pairs={{120,184},{0,192},{248,56},{128,64},{121,185},{1,193},{249,57},{12... | collective-permute-start | bytes 1179656 | tf_op jit(solution)/shard_map/ppermute | solution.py:133
  22.0 73.0 %collective-permute-start.2 = (f32[8,3,64,128]{3,2,1,0:T(8,128)S(1)}, f32[8,3,64,128]{3,2,1,0:T(8,128)S(1)}, u32[]{:S(2)}, u32[]{:S(2)}) collective-permute-start(f32[8,3,64,128]{3,2,1,0:T(8,128)S(1)} %pad_maximum_fusion.1), channel_id=1, source_target_pairs={{120,128},{0,248},{248,0},{128,120},{121,129},{1,249},{249,1},{129... | collective-permute-start | bytes 2359304 | tf_op jit(solution)/shard_map/ppermute | solution.py:130
  47.3 47.8 %collective-permute-start.4 = (f32[5,3,64,128]{3,2,1,0:T(8,128)S(1)}, f32[5,3,64,128]{3,2,1,0:T(8,128)S(1)}, u32[]{:S(2)}, u32[]{:S(2)}) collective-permute-start(f32[5,3,64,128]{3,2,1,0:T(8,128)S(1)} %collective-permute-done.3), channel_id=1, source_target_pairs={{152,128},{224,248},{24,0},{96,120},{153,129},{225,249},{25,1},{97... | collective-permute-start | bytes 1474568 | tf_op jit(solution)/shard_map/ppermute | solution.py:133
  67.4 14.5 %collective-permute-start.6 = (f32[4,3,64,128]{3,2,1,0:T(8,128)S(1)}, f32[4,3,64,128]{3,2,1,0:T(8,128)S(1)}, u32[]{:S(2)}, u32[]{:S(2)}) collective-permute-start(f32[4,3,64,128]{3,2,1,0:T(8,128)S(1)} %collective-permute-done.5), channel_id=1, source_target_pairs={{184,128},{192,248},{56,0},{64,120},{185,129},{193,249},{57,1},{65... | collective-permute-start | bytes 1179656 | tf_op jit(solution)/shard_map/ppermute | solution.py:133
  101.7 18.8 %collective-permute-start.7 = (f32[16,4,8,128]{3,2,1,0:T(8,128)S(1)}, f32[16,4,8,128]{3,2,1,0:T(8,128)S(1)}, u32[]{:S(2)}, u32[]{:S(2)}) collective-permute-start(f32[16,4,8,128]{3,2,1,0:T(8,128)S(1)} %get-tuple-element.16), channel_id=1, source_target_pairs={{0,1},{1,0},{2,3},{3,2},{4,5},{5,4},{6,7},{7,6},{8,9},{9,8},{10,11... | collective-permute-start | bytes 786440 | tf_op jit(solution)/shard_map/ppermute | solution.py:20
  101.8 21.6 %collective-permute-start.8 = (f32[16,4,8,128]{3,2,1,0:T(8,128)S(1)}, f32[16,4,8,128]{3,2,1,0:T(8,128)S(1)}, u32[]{:S(2)}, u32[]{:S(2)}) collective-permute-start(f32[16,4,8,128]{3,2,1,0:T(8,128)S(1)} %get-tuple-element.17), channel_id=1, source_target_pairs={{0,2},{1,3},{2,0},{3,1},{4,6},{5,7},{6,4},{7,5},{8,10},{9,11},{10,... | collective-permute-start | bytes 786440 | tf_op jit(solution)/shard_map/ppermute | solution.py:20
  107.0 19.9 %collective-permute-start.9 = (f32[16,4,8,128]{3,2,1,0:T(8,128)S(1)}, f32[16,4,8,128]{3,2,1,0:T(8,128)S(1)}, u32[]{:S(2)}, u32[]{:S(2)}) collective-permute-start(f32[16,4,8,128]{3,2,1,0:T(8,128)S(1)} %get-tuple-element.18), channel_id=1, source_target_pairs={{0,3},{1,2},{2,1},{3,0},{4,7},{5,6},{6,5},{7,4},{8,11},{9,10},{10,... | collective-permute-start | bytes 786440 | tf_op jit(solution)/shard_map/ppermute | solution.py:20
  107.0 42.7 %collective-permute-start.10 = (f32[16,4,8,128]{3,2,1,0:T(8,128)S(1)}, f32[16,4,8,128]{3,2,1,0:T(8,128)S(1)}, u32[]{:S(2)}, u32[]{:S(2)}) collective-permute-start(f32[16,4,8,128]{3,2,1,0:T(8,128)S(1)} %get-tuple-element.19), channel_id=1, source_target_pairs={{0,4},{1,5},{2,6},{3,7},{4,0},{5,1},{6,2},{7,3},{8,12},{9,13},{10,... | collective-permute-start | bytes 786440 | tf_op jit(solution)/shard_map/ppermute | solution.py:20
  120.5 34.8 %collective-permute-start.11 = (f32[16,4,8,128]{3,2,1,0:T(8,128)S(1)}, f32[16,4,8,128]{3,2,1,0:T(8,128)S(1)}, u32[]{:S(2)}, u32[]{:S(2)}) collective-permute-start(f32[16,4,8,128]{3,2,1,0:T(8,128)S(1)} %get-tuple-element.20), channel_id=1, source_target_pairs={{0,5},{1,4},{2,7},{3,6},{4,1},{5,0},{6,3},{7,2},{8,13},{9,12},{10,... | collective-permute-start | bytes 786440 | tf_op jit(solution)/shard_map/ppermute | solution.py:20
  120.5 41.1 %collective-permute-start.12 = (f32[16,4,8,128]{3,2,1,0:T(8,128)S(1)}, f32[16,4,8,128]{3,2,1,0:T(8,128)S(1)}, u32[]{:S(2)}, u32[]{:S(2)}) collective-permute-start(f32[16,4,8,128]{3,2,1,0:T(8,128)S(1)} %get-tuple-element.21), channel_id=1, source_target_pairs={{0,6},{1,7},{2,4},{3,5},{4,2},{5,3},{6,0},{7,1},{8,14},{9,15},{10,... | collective-permute-start | bytes 786440 | tf_op jit(solution)/shard_map/ppermute | solution.py:20
  123.4 43.2 %collective-permute-start.13 = (f32[16,4,8,128]{3,2,1,0:T(8,128)S(1)}, f32[16,4,8,128]{3,2,1,0:T(8,128)S(1)}, u32[]{:S(2)}, u32[]{:S(2)}) collective-permute-start(f32[16,4,8,128]{3,2,1,0:T(8,128)S(1)} %get-tuple-element.22), channel_id=1, source_target_pairs={{0,7},{1,6},{2,5},{3,4},{4,3},{5,2},{6,1},{7,0},{8,15},{9,14},{10,... | collective-permute-start | bytes 786440 | tf_op jit(solution)/shard_map/ppermute | solution.py:20
  169.7 1.3 collective-permute-start.14
  171.1 4.4 %collective-permute-start.15 = (f32[128,128]{1,0:T(8,128)S(1)}, f32[128,128]{1,0:T(8,128)S(1)}, u32[]{:S(2)}, u32[]{:S(2)}) collective-permute-start(f32[128,128]{1,0:T(8,128)S(1)} %add.30), channel_id=1, source_target_pairs={{0,2},{1,3},{2,0},{3,1},{4,6},{5,7},{6,4},{7,5},{8,10},{9,11},{10,... | collective-permute-start | bytes 196616 | tf_op jit(solution)/shard_map/ppermute | solution.py:20
  175.4 5.3 %collective-permute-start.16 = (f32[128,128]{1,0:T(8,128)S(1)}, f32[128,128]{1,0:T(8,128)S(1)}, u32[]{:S(2)}, u32[]{:S(2)}) collective-permute-start(f32[128,128]{1,0:T(8,128)S(1)} %add.31), channel_id=1, source_target_pairs={{0,4},{1,5},{2,6},{3,7},{4,0},{5,1},{6,2},{7,3},{8,12},{9,13},{10,... | collective-permute-start | bytes 196616 | tf_op jit(solution)/shard_map/ppermute | solution.py:20
  180.7 4.5 %collective-permute-start.19 = (f32[128,128]{1,0:T(8,128)S(1)}, f32[128,128]{1,0:T(8,128)S(1)}, u32[]{:S(2)}, u32[]{:S(2)}) collective-permute-start(f32[128,128]{1,0:T(8,128)S(1)} %add.32), channel_id=1, source_target_pairs={{0,24},{8,0},{16,8},{24,16},{32,56},{40,32},{48,40},{56,48},{64,88... | collective-permute-start | bytes 196616 | tf_op jit(solution)/shard_map/ppermute | solution.py:20
  181.0 5.9 %collective-permute-start.18 = (f32[128,128]{1,0:T(8,128)S(1)}, f32[128,128]{1,0:T(8,128)S(1)}, u32[]{:S(2)}, u32[]{:S(2)}) collective-permute-start(f32[128,128]{1,0:T(8,128)S(1)} %add.32), channel_id=1, source_target_pairs={{0,16},{8,24},{16,0},{24,8},{32,48},{40,56},{48,32},{56,40},{64,80... | collective-permute-start | bytes 196616 | tf_op jit(solution)/shard_map/ppermute | solution.py:20
  181.1 6.8 %collective-permute-start.17 = (f32[128,128]{1,0:T(8,128)S(1)}, f32[128,128]{1,0:T(8,128)S(1)}, u32[]{:S(2)}, u32[]{:S(2)}) collective-permute-start(f32[128,128]{1,0:T(8,128)S(1)} %add.32), channel_id=1, source_target_pairs={{0,8},{8,16},{16,24},{24,0},{32,40},{40,48},{48,56},{56,32},{64,72... | collective-permute-start | bytes 196616 | tf_op jit(solution)/shard_map/ppermute | solution.py:20
  187.9 4.3 %collective-permute-start.22 = (f32[128,128]{1,0:T(8,128)S(1)}, f32[128,128]{1,0:T(8,128)S(1)}, u32[]{:S(2)}, u32[]{:S(2)}) collective-permute-start(f32[128,128]{1,0:T(8,128)S(1)} %add_add_fusion.1), channel_id=1, source_target_pairs={{0,96},{8,104},{16,112},{24,120},{32,0},{40,8},{48,16},{56,24},{64... | collective-permute-start | bytes 196616 | tf_op jit(solution)/shard_map/ppermute | solution.py:20
  189.7 5.9 %collective-permute-start.21 = (f32[128,128]{1,0:T(8,128)S(1)}, f32[128,128]{1,0:T(8,128)S(1)}, u32[]{:S(2)}, u32[]{:S(2)}) collective-permute-start(f32[128,128]{1,0:T(8,128)S(1)} %add_add_fusion.1), channel_id=1, source_target_pairs={{0,64},{8,72},{16,80},{24,88},{32,96},{40,104},{48,112},{56,120},{... | collective-permute-start | bytes 196616 | tf_op jit(solution)/shard_map/ppermute | solution.py:20
  189.7 6.2 %collective-permute-start.20 = (f32[128,128]{1,0:T(8,128)S(1)}, f32[128,128]{1,0:T(8,128)S(1)}, u32[]{:S(2)}, u32[]{:S(2)}) collective-permute-start(f32[128,128]{1,0:T(8,128)S(1)} %add_add_fusion.1), channel_id=1, source_target_pairs={{0,32},{8,40},{16,48},{24,56},{32,64},{40,72},{48,80},{56,88},{64,... | collective-permute-start | bytes 196616 | tf_op jit(solution)/shard_map/ppermute | solution.py:20
  195.9 8.3 %collective-permute-start.23 = (f32[128,128]{1,0:T(8,128)S(1)}, f32[128,128]{1,0:T(8,128)S(1)}, u32[]{:S(2)}, u32[]{:S(2)}) collective-permute-start(f32[128,128]{1,0:T(8,128)S(1)} %add_add_fusion), channel_id=1, source_target_pairs={{0,128},{8,136},{16,144},{24,152},{32,160},{40,168},{48,176},{56,1... | collective-permute-start | bytes 196616 | tf_op jit(solution)/shard_map/ppermute | solution.py:20

commit v4 on v3

--- a/solution.py
+++ b/solution.py
@@ -13,6 +13,7 @@
 PANEL = 32
 SIDE = 4
 SHARES = (7, 5, 4)
+DETOURS = (0, 2)
 
 
 def permuted(block, axis, target):
@@ -107,12 +108,12 @@
 
 def detour_pairs(route):
     half, last = SIDE * SIDE, SIDE - 1
-    up, down = route * SIDE + last, (last - route) * SIDE
+    up, down = DETOURS[route] * SIDE + last, (last - DETOURS[route]) * SIDE
     out, back = [], []
     for h in (0, 1):
-        other = (1 - h) * half
-        out += [(h * half + half - 1, other + up), (h * half, other + down)]
-        back += [(other + up, other), (other + down, other + half - 1)]
+        own, other = h * half, (1 - h) * half
+        out += [(own + half - 1, own + up), (own, own + down)]
+        back += [(own + up, other), (own + down, other + half - 1)]
     return out, back
 
 

time: 213 us -> 190 us (0.89)
  waiting for transfers between devices: 128 us -> 106 us
    ppermute x2, waiting for transfers between devices: 39 us -> 0.01 us  [halos(): lax.ppermute(block, 'domain', out)]
    ppermute x2, waiting for transfers between devices: 13.2 us -> 36.1 us  [halos(): lax.ppermute(lax.ppermute(block, 'domain', out), 'domain', back)]
    ppermute x1, starting transfers between devices: 5.06 us -> 11.4 us  [halos(): seams = [lax.ppermute(blocks[0], 'domain', seam_pairs())]]
    ppermute x2, starting transfers between devices: 13 us -> 7.3 us  [halos(): lax.ppermute(block, 'domain', out)]
    ppermute x1, waiting for transfers between devices: 13.2 us -> 9.34 us  [halos(): seams = [lax.ppermute(blocks[0], 'domain', seam_pairs())]]
    ppermute x17, waiting for transfers between devices: 62.9 us -> 60.7 us  [permuted(): return lax.ppermute(block, axis, [(i, target(i)) for i in range(count)])]
  transfers between devices with their start and end apart: 24 -> 24, of which waited for: 18 -> 17; matrix products, arithmetic and copies ran while one was open for 0% -> 0% of each run, Pallas kernels for 0% -> 0%
where the time goes in v4:
time: 190 us
  waiting for transfers between devices  106 us (56%)
  starting transfers between devices  62.4 us (33%)
  Pallas kernels  18.1 us (10%)
  other arithmetic  2.88 us (2%)
    ppermute x17, waiting for transfers between devices, permuted(): return lax.ppermute(block, axis, [(i, target(i)) for i in range(count)])  60.7 us
    ppermute x2, waiting for transfers between devices, halos(): lax.ppermute(lax.ppermute(block, 'domain', out), 'domain', back)  36.1 us
    ppermute x17, starting transfers between devices, permuted(): return lax.ppermute(block, axis, [(i, target(i)) for i in range(count)])  35.2 us
    ppermute x1, starting transfers between devices, halos(): seams = [lax.ppermute(blocks[0], 'domain', seam_pairs())]  11.4 us
    ppermute x1, waiting for transfers between devices, halos(): seams = [lax.ppermute(blocks[0], 'domain', seam_pairs())]  9.34 us
    ppermute x2, starting transfers between devices, halos(): lax.ppermute(block, 'domain', out)  7.3 us
    pallas_call x1, Pallas kernels, filtered_stripes(): pl.pallas_call(functools.partial(filter_kernel, SHARES, stripes), out_sha...  6.63 us
    ppermute x1, starting transfers between devices, halos(): low = lax.ppermute(highs, 'domain', inner_pairs(1))  4.65 us
  transfers between devices with their start and end apart: 24, of which 17 were waited for; matrix products, arithmetic and copies ran while one was open for 0% of the time, Pallas kernels for 0%

profile of v4, /device:TPU:32, one launch (start us, length us, event | category | flops | bytes accessed | tf_op | source)
XLA Modules:
  0.0 189.9 jit_solution(758902609720853635)
XLA Ops:
  0.0 2.7 %broadcast_select_fusion = (f32[17,3,64,128]{3,2,1,0:T(8,128)S(1)}, f32[17,3,64,128]{3,2,1,0:T(8,128)S(1)}, f32[17,3,64,128]{3,2,1,0:T(8,128)S(1)}) fusion(pred[]{:T(512)S(6)} %eq.3, f32[1,4,64,128]{3,2,1,0:T(8,128)} %bitcast.10, f32[16,4,64,128]{3,2,1,0:T(8,128)} %field.1), kind=kLoop, calls=%fused_computation.4 | loop fusion | flops 1253376 | bytes 7241729 | tf_op jit(solution)/shard_map/jit(_where)/select_n | solution.py:125
  2.7 1.3 collective-permute-start.1
  4.0 4.7 %collective-permute-start = (f32[17,3,64,128]{3,2,1,0:T(8,128)S(1)}, f32[17,3,64,128]{3,2,1,0:T(8,128)S(1)}, u32[]{:S(2)}, u32[]{:S(2)}) collective-permute-start(f32[17,3,64,128]{3,2,1,0:T(8,128)S(1)} %get-tuple-element.27), channel_id=1, source_target_pairs={{0,8},{8,16},{16,24},{24,32},{32,40},{40,48},{48,56},{56,64},{64,7... | collective-permute-start | bytes 5013512 | tf_op jit(solution)/shard_map/ppermute | solution.py:135
  8.8 5.9 %collective-permute-start.3 = (f32[5,3,64,128]{3,2,1,0:T(8,128)S(1)}, f32[5,3,64,128]{3,2,1,0:T(8,128)S(1)}, u32[]{:S(2)}, u32[]{:S(2)}) collective-permute-start(f32[5,3,64,128]{3,2,1,0:T(8,128)S(1)} %slice.28), channel_id=1, source_target_pairs={{120,24},{0,96},{248,152},{128,224},{121,25},{1,97},{249,153},{129... | collective-permute-start | bytes 1474568 | tf_op jit(solution)/shard_map/ppermute | solution.py:134
  14.7 0.0 copy-start
  14.7 0.0 copy-start.1
  14.7 1.4 collective-permute-start.5
  16.1 0.1 slice.26
  16.2 0.1 pad_maximum_fusion.1
  16.3 11.4 %collective-permute-start.2 = (f32[8,3,64,128]{3,2,1,0:T(8,128)S(1)}, f32[8,3,64,128]{3,2,1,0:T(8,128)S(1)}, u32[]{:S(2)}, u32[]{:S(2)}) collective-permute-start(f32[8,3,64,128]{3,2,1,0:T(8,128)S(1)} %pad_maximum_fusion.1), channel_id=1, source_target_pairs={{120,128},{0,248},{248,0},{128,120},{121,129},{1,249},{249,1},{129... | collective-permute-start | bytes 2359304 | tf_op jit(solution)/shard_map/ppermute | solution.py:131
  27.7 0.0 collective-permute-done.3
  27.7 1.3 collective-permute-start.4
  29.0 0.0 collective-permute-done.5
  29.0 1.3 collective-permute-start.6
  30.3 36.1 %collective-permute-done.6.rest_2_ = f32[4,3,64,128]{3,2,1,0:T(8,128)S(1)} collective-permute-done((f32[4,3,64,128]{3,2,1,0:T(8,128)S(1)}, f32[4,3,64,128]{3,2,1,0:T(8,128)S(1)}, u32[]{:S(2)}, u32[]{:S(2)}) %collective-permute-start.6) | collective-permute-done | bytes 393248 | tf_op jit(solution)/shard_map/ppermute | solution.py:134
  66.4 9.3 %collective-permute-done.2.rest_0_ = f32[8,3,64,128]{3,2,1,0:T(8,128)S(1)} collective-permute-done((f32[8,3,64,128]{3,2,1,0:T(8,128)S(1)}, f32[8,3,64,128]{3,2,1,0:T(8,128)S(1)}, u32[]{:S(2)}, u32[]{:S(2)}) %collective-permute-start.2) | collective-permute-done | bytes 786464 | tf_op jit(solution)/shard_map/ppermute | solution.py:131
  75.8 0.0 collective-permute-done.4.rest_1_
  75.8 0.0 collective-permute-done.1.high
  75.8 0.0 collective-permute-done.low
  75.8 0.0 copy-done
  75.8 0.0 copy-done.1
  75.8 6.6 %shard_map.28 = (f32[16,4,8,128]{3,2,1,0:T(8,128)S(1)}, f32[16,4,8,128]{3,2,1,0:T(8,128)S(1)}, f32[16,4,8,128]{3,2,1,0:T(8,128)S(1)}, f32[16,4,8,128]{3,2,1,0:T(...) custom-call(f32[16,4,64,128]{3,2,1,0:T(8,128)S(1)} %copy-done, ...), custom_call_target="tpu_custom_call" | custom-call | tf_op jit(solution)/shard_map/pallas_call | solution.py:80
  82.4 0.1 collective-permute-start.7
  82.5 0.1 collective-permute-start.8
  82.6 1.8 collective-permute-start.9
  84.4 7.5 %collective-permute-start.10 = (f32[16,4,8,128]{3,2,1,0:T(8,128)S(1)}, f32[16,4,8,128]{3,2,1,0:T(8,128)S(1)}, u32[]{:S(2)}, u32[]{:S(2)}) collective-permute-start(f32[16,4,8,128]{3,2,1,0:T(8,128)S(1)} %get-tuple-element.19), channel_id=1, source_target_pairs={{0,4},{1,5},{2,6},{3,7},{4,0},{5,1},{6,2},{7,3},{8,12},{9,13},{10,... | collective-permute-start | bytes 786440 | tf_op jit(solution)/shard_map/ppermute | solution.py:21
  92.0 0.0 collective-permute-start.11
  92.0 0.0 collective-permute-done.7
  92.0 2.9 %collective-permute-start.12 = (f32[16,4,8,128]{3,2,1,0:T(8,128)S(1)}, f32[16,4,8,128]{3,2,1,0:T(8,128)S(1)}, u32[]{:S(2)}, u32[]{:S(2)}) collective-permute-start(f32[16,4,8,128]{3,2,1,0:T(8,128)S(1)} %get-tuple-element.21), channel_id=1, source_target_pairs={{0,6},{1,7},{2,4},{3,5},{4,2},{5,3},{6,0},{7,1},{8,14},{9,15},{10,... | collective-permute-start | bytes 786440 | tf_op jit(solution)/shard_map/ppermute | solution.py:21
  94.8 0.0 collective-permute-done.8
  94.8 5.1 %collective-permute-start.13 = (f32[16,4,8,128]{3,2,1,0:T(8,128)S(1)}, f32[16,4,8,128]{3,2,1,0:T(8,128)S(1)}, u32[]{:S(2)}, u32[]{:S(2)}) collective-permute-start(f32[16,4,8,128]{3,2,1,0:T(8,128)S(1)} %get-tuple-element.22), channel_id=1, source_target_pairs={{0,7},{1,6},{2,5},{3,4},{4,3},{5,2},{6,1},{7,0},{8,15},{9,14},{10,... | collective-permute-start | bytes 786440 | tf_op jit(solution)/shard_map/ppermute | solution.py:21
  100.0 5.4 %collective-permute-done.9 = f32[16,4,8,128]{3,2,1,0:T(8,128)S(1)} collective-permute-done((f32[16,4,8,128]{3,2,1,0:T(8,128)S(1)}, f32[16,4,8,128]{3,2,1,0:T(8,128)S(1)}, u32[]{:S(2)}, u32[]{:S(2)}) %collective-permute-start.9) | collective-permute-done | bytes 262176 | tf_op jit(solution)/shard_map/ppermute | solution.py:21
  105.4 15.7 %collective-permute-done.10 = f32[16,4,8,128]{3,2,1,0:T(8,128)S(1)} collective-permute-done((f32[16,4,8,128]{3,2,1,0:T(8,128)S(1)}, f32[16,4,8,128]{3,2,1,0:T(8,128)S(1)}, u32[]{:S(2)}, u32[]{:S(2)}) %collective-permute-start.10) | collective-permute-done | bytes 262176 | tf_op jit(solution)/shard_map/ppermute | solution.py:21
  121.1 5.6 %collective-permute-done.11 = f32[16,4,8,128]{3,2,1,0:T(8,128)S(1)} collective-permute-done((f32[16,4,8,128]{3,2,1,0:T(8,128)S(1)}, f32[16,4,8,128]{3,2,1,0:T(8,128)S(1)}, u32[]{:S(2)}, u32[]{:S(2)}) %collective-permute-start.11) | collective-permute-done | bytes 262176 | tf_op jit(solution)/shard_map/ppermute | solution.py:21
  126.8 6.4 %collective-permute-done.12 = f32[16,4,8,128]{3,2,1,0:T(8,128)S(1)} collective-permute-done((f32[16,4,8,128]{3,2,1,0:T(8,128)S(1)}, f32[16,4,8,128]{3,2,1,0:T(8,128)S(1)}, u32[]{:S(2)}, u32[]{:S(2)}) %collective-permute-start.12) | collective-permute-done | bytes 262176 | tf_op jit(solution)/shard_map/ppermute | solution.py:21
  133.1 5.0 %collective-permute-done.13 = f32[16,4,8,128]{3,2,1,0:T(8,128)S(1)} collective-permute-done((f32[16,4,8,128]{3,2,1,0:T(8,128)S(1)}, f32[16,4,8,128]{3,2,1,0:T(8,128)S(1)}, u32[]{:S(2)}, u32[]{:S(2)}) %collective-permute-start.13) | collective-permute-done | bytes 262176 | tf_op jit(solution)/shard_map/ppermute | solution.py:21
  138.1 3.1 %shard_map.29 = (f32[128,4096]{1,0:T(8,128)S(1)}, f32[128,128]{1,0:T(8,128)S(1)}) custom-call(f32[512,128]{1,0:T(8,128)S(1)} %bitcast.11, f32[512,128]{1,0:T(8,128)S(1)} %bitcast.12, f32[512,128]{1,0:T(8,128)S(1)} %bitcast.13, f32[512,128]{1,0:T(8,128)S(1)} %bitcast.14, f32[512,128]{1,0:T(8,128)S(1)} %bitcast.15, f32[512,128]{1,0:T(8,128)S(1)} %bitcast.16, ...), custom_call_target="tpu_custom_call" | custom-call | tf_op jit(solution)/shard_map/pallas_call | solution.py:166
  141.2 0.2 collective-permute-start.14
  141.4 1.1 collective-permute-done.14
  142.5 0.1 collective-permute-start.15
  142.6 4.3 %collective-permute-done.15 = f32[128,128]{1,0:T(8,128)S(1)} collective-permute-done((f32[128,128]{1,0:T(8,128)S(1)}, f32[128,128]{1,0:T(8,128)S(1)}, u32[]{:S(2)}, u32[]{:S(2)}) %collective-permute-start.15) | collective-permute-done | bytes 65568 | tf_op jit(solution)/shard_map/ppermute | solution.py:21
  146.9 1.0 collective-permute-start.16
  147.9 4.3 %collective-permute-done.16 = f32[128,128]{1,0:T(8,128)S(1)} collective-permute-done((f32[128,128]{1,0:T(8,128)S(1)}, f32[128,128]{1,0:T(8,128)S(1)}, u32[]{:S(2)}, u32[]{:S(2)}) %collective-permute-start.16) | collective-permute-done | bytes 65568 | tf_op jit(solution)/shard_map/ppermute | solution.py:21
  152.2 0.3 collective-permute-start.19
  152.4 0.1 collective-permute-start.18
  152.5 1.9 %collective-permute-start.17 = (f32[128,128]{1,0:T(8,128)S(1)}, f32[128,128]{1,0:T(8,128)S(1)}, u32[]{:S(2)}, u32[]{:S(2)}) collective-permute-start(f32[128,128]{1,0:T(8,128)S(1)} %add.32), channel_id=1, source_target_pairs={{0,8},{8,16},{16,24},{24,0},{32,40},{40,48},{48,56},{56,32},{64,72... | collective-permute-start | bytes 196616 | tf_op jit(solution)/shard_map/ppermute | solution.py:21
  154.5 2.2 %collective-permute-done.19 = f32[128,128]{1,0:T(8,128)S(1)} collective-permute-done((f32[128,128]{1,0:T(8,128)S(1)}, f32[128,128]{1,0:T(8,128)S(1)}, u32[]{:S(2)}, u32[]{:S(2)}) %collective-permute-start.19) | collective-permute-done | bytes 65568 | tf_op jit(solution)/shard_map/ppermute | solution.py:21
  156.7 1.6 collective-permute-done.18
  158.3 1.1 collective-permute-done.17
  159.4 7.6 %collective-permute-start.22 = (f32[128,128]{1,0:T(8,128)S(1)}, f32[128,128]{1,0:T(8,128)S(1)}, u32[]{:S(2)}, u32[]{:S(2)}) collective-permute-start(f32[128,128]{1,0:T(8,128)S(1)} %add_add_fusion.1), channel_id=1, source_target_pairs={{0,96},{8,104},{16,112},{24,120},{32,0},{40,8},{48,16},{56,24},{64... | collective-permute-start | bytes 196616 | tf_op jit(solution)/shard_map/ppermute | solution.py:21
  167.0 0.0 collective-permute-start.21
  167.0 1.0 collective-permute-start.20
  167.9 1.6 collective-permute-done.22
  169.5 3.4 %collective-permute-done.21 = f32[128,128]{1,0:T(8,128)S(1)} collective-permute-done((f32[128,128]{1,0:T(8,128)S(1)}, f32[128,128]{1,0:T(8,128)S(1)}, u32[]{:S(2)}, u32[]{:S(2)}) %collective-permute-start.21) | collective-permute-done | bytes 65568 | tf_op jit(solution)/shard_map/ppermute | solution.py:21
  172.8 0.3 collective-permute-done.20
  173.2 5.6 %collective-permute-start.23 = (f32[128,128]{1,0:T(8,128)S(1)}, f32[128,128]{1,0:T(8,128)S(1)}, u32[]{:S(2)}, u32[]{:S(2)}) collective-permute-start(f32[128,128]{1,0:T(8,128)S(1)} %add_add_fusion), channel_id=1, source_target_pairs={{0,128},{8,136},{16,144},{24,152},{32,160},{40,168},{48,176},{56,1... | collective-permute-start | bytes 196616 | tf_op jit(solution)/shard_map/ppermute | solution.py:21
  178.7 2.8 %collective-permute-done.23 = f32[128,128]{1,0:T(8,128)S(1)} collective-permute-done((f32[128,128]{1,0:T(8,128)S(1)}, f32[128,128]{1,0:T(8,128)S(1)}, u32[]{:S(2)}, u32[]{:S(2)}) %collective-permute-start.23) | collective-permute-done | bytes 65568 | tf_op jit(solution)/shard_map/ppermute | solution.py:21
  181.5 4.2 %shard_map.30.inverse = f32[128,128]{1,0:T(8,128)S(1)} custom-call(f32[128,128]{1,0:T(8,128)S(1)} %add.39.gram), custom_call_target="tpu_custom_call" | custom-call | tf_op jit(solution)/shard_map/pallas_call | solution.py:219
  185.7 4.2 %shard_map.31 = f32[4096,128]{1,0:T(8,128)} custom-call(f32[128,128]{1,0:T(8,128)S(1)} %shard_map.30.inverse, f32[128,4096]{1,0:T(8,128)S(1)} %get-tuple-element.24.flat), custom_call_target="tpu_custom_call" | custom-call | tf_op jit(solution)/shard_map/pallas_call | solution.py:243
  (9 shorter events, 0.1 us)
Async XLA Ops:
  2.7 73.0 %collective-permute-start.1 = (f32[17,3,64,128]{3,2,1,0:T(8,128)S(1)}, f32[17,3,64,128]{3,2,1,0:T(8,128)S(1)}, u32[]{:S(2)}, u32[]{:S(2)}) collective-permute-start(f32[17,3,64,128]{3,2,1,0:T(8,128)S(1)} %get-tuple-element.26), channel_id=1, source_target_pairs={{8,0},{16,8},{24,16},{32,24},{40,32},{48,40},{56,48},{64,56},{72,6... | collective-permute-start | bytes 5013512 | tf_op jit(solution)/shard_map/ppermute | solution.py:136
  4.0 71.7 %collective-permute-start = (f32[17,3,64,128]{3,2,1,0:T(8,128)S(1)}, f32[17,3,64,128]{3,2,1,0:T(8,128)S(1)}, u32[]{:S(2)}, u32[]{:S(2)}) collective-permute-start(f32[17,3,64,128]{3,2,1,0:T(8,128)S(1)} %get-tuple-element.27), channel_id=1, source_target_pairs={{0,8},{8,16},{16,24},{24,32},{32,40},{40,48},{48,56},{56,64},{64,7... | collective-permute-start | bytes 5013512 | tf_op jit(solution)/shard_map/ppermute | solution.py:135
  8.8 19.0 %collective-permute-start.3 = (f32[5,3,64,128]{3,2,1,0:T(8,128)S(1)}, f32[5,3,64,128]{3,2,1,0:T(8,128)S(1)}, u32[]{:S(2)}, u32[]{:S(2)}) collective-permute-start(f32[5,3,64,128]{3,2,1,0:T(8,128)S(1)} %slice.28), channel_id=1, source_target_pairs={{120,24},{0,96},{248,152},{128,224},{121,25},{1,97},{249,153},{129... | collective-permute-start | bytes 1474568 | tf_op jit(solution)/shard_map/ppermute | solution.py:134
  14.7 61.1 %copy-start = (f32[16,4,64,128]{3,2,1,0:T(8,128)S(1)}, f32[16,4,64,128]{3,2,1,0:T(8,128)}, u32[]{:S(2)}) copy-start(f32[16,4,64,128]{3,2,1,0:T(8,128)} %field.1) | copy-start | bytes 6291460
  14.7 61.1 %copy-start.1 = (f32[4,64,128]{2,1,0:T(8,128)S(1)}, f32[4,64,128]{2,1,0:T(8,128)}, u32[]{:S(2)}) copy-start(f32[4,64,128]{2,1,0:T(8,128)} %pot.1) | copy-start | bytes 393220
  14.7 14.3 %collective-permute-start.5 = (f32[4,3,64,128]{3,2,1,0:T(8,128)S(1)}, f32[4,3,64,128]{3,2,1,0:T(8,128)S(1)}, u32[]{:S(2)}, u32[]{:S(2)}) collective-permute-start(f32[4,3,64,128]{3,2,1,0:T(8,128)S(1)} %slice.29), channel_id=1, source_target_pairs={{120,88},{0,32},{248,216},{128,160},{121,89},{1,33},{249,217},{129... | collective-permute-start | bytes 1179656 | tf_op jit(solution)/shard_map/ppermute | solution.py:134
  16.3 59.5 %collective-permute-start.2 = (f32[8,3,64,128]{3,2,1,0:T(8,128)S(1)}, f32[8,3,64,128]{3,2,1,0:T(8,128)S(1)}, u32[]{:S(2)}, u32[]{:S(2)}) collective-permute-start(f32[8,3,64,128]{3,2,1,0:T(8,128)S(1)} %pad_maximum_fusion.1), channel_id=1, source_target_pairs={{120,128},{0,248},{248,0},{128,120},{121,129},{1,249},{249,1},{129... | collective-permute-start | bytes 2359304 | tf_op jit(solution)/shard_map/ppermute | solution.py:131
  27.7 48.1 %collective-permute-start.4 = (f32[5,3,64,128]{3,2,1,0:T(8,128)S(1)}, f32[5,3,64,128]{3,2,1,0:T(8,128)S(1)}, u32[]{:S(2)}, u32[]{:S(2)}) collective-permute-start(f32[5,3,64,128]{3,2,1,0:T(8,128)S(1)} %collective-permute-done.3), channel_id=1, source_target_pairs={{24,128},{96,248},{152,0},{224,120},{25,129},{97,249},{153,1},{225... | collective-permute-start | bytes 1474568 | tf_op jit(solution)/shard_map/ppermute | solution.py:134
  29.0 37.4 %collective-permute-start.6 = (f32[4,3,64,128]{3,2,1,0:T(8,128)S(1)}, f32[4,3,64,128]{3,2,1,0:T(8,128)S(1)}, u32[]{:S(2)}, u32[]{:S(2)}) collective-permute-start(f32[4,3,64,128]{3,2,1,0:T(8,128)S(1)} %collective-permute-done.5), channel_id=1, source_target_pairs={{88,128},{32,248},{216,0},{160,120},{89,129},{33,249},{217,1},{161... | collective-permute-start | bytes 1179656 | tf_op jit(solution)/shard_map/ppermute | solution.py:134
  82.4 9.5 %collective-permute-start.7 = (f32[16,4,8,128]{3,2,1,0:T(8,128)S(1)}, f32[16,4,8,128]{3,2,1,0:T(8,128)S(1)}, u32[]{:S(2)}, u32[]{:S(2)}) collective-permute-start(f32[16,4,8,128]{3,2,1,0:T(8,128)S(1)} %get-tuple-element.16), channel_id=1, source_target_pairs={{0,1},{1,0},{2,3},{3,2},{4,5},{5,4},{6,7},{7,6},{8,9},{9,8},{10,11... | collective-permute-start | bytes 786440 | tf_op jit(solution)/shard_map/ppermute | solution.py:21
  82.5 12.3 %collective-permute-start.8 = (f32[16,4,8,128]{3,2,1,0:T(8,128)S(1)}, f32[16,4,8,128]{3,2,1,0:T(8,128)S(1)}, u32[]{:S(2)}, u32[]{:S(2)}) collective-permute-start(f32[16,4,8,128]{3,2,1,0:T(8,128)S(1)} %get-tuple-element.17), channel_id=1, source_target_pairs={{0,2},{1,3},{2,0},{3,1},{4,6},{5,7},{6,4},{7,5},{8,10},{9,11},{10,... | collective-permute-start | bytes 786440 | tf_op jit(solution)/shard_map/ppermute | solution.py:21
  82.6 22.8 %collective-permute-start.9 = (f32[16,4,8,128]{3,2,1,0:T(8,128)S(1)}, f32[16,4,8,128]{3,2,1,0:T(8,128)S(1)}, u32[]{:S(2)}, u32[]{:S(2)}) collective-permute-start(f32[16,4,8,128]{3,2,1,0:T(8,128)S(1)} %get-tuple-element.18), channel_id=1, source_target_pairs={{0,3},{1,2},{2,1},{3,0},{4,7},{5,6},{6,5},{7,4},{8,11},{9,10},{10,... | collective-permute-start | bytes 786440 | tf_op jit(solution)/shard_map/ppermute | solution.py:21
  84.4 36.7 %collective-permute-start.10 = (f32[16,4,8,128]{3,2,1,0:T(8,128)S(1)}, f32[16,4,8,128]{3,2,1,0:T(8,128)S(1)}, u32[]{:S(2)}, u32[]{:S(2)}) collective-permute-start(f32[16,4,8,128]{3,2,1,0:T(8,128)S(1)} %get-tuple-element.19), channel_id=1, source_target_pairs={{0,4},{1,5},{2,6},{3,7},{4,0},{5,1},{6,2},{7,3},{8,12},{9,13},{10,... | collective-permute-start | bytes 786440 | tf_op jit(solution)/shard_map/ppermute | solution.py:21
  92.0 34.8 %collective-permute-start.11 = (f32[16,4,8,128]{3,2,1,0:T(8,128)S(1)}, f32[16,4,8,128]{3,2,1,0:T(8,128)S(1)}, u32[]{:S(2)}, u32[]{:S(2)}) collective-permute-start(f32[16,4,8,128]{3,2,1,0:T(8,128)S(1)} %get-tuple-element.20), channel_id=1, source_target_pairs={{0,5},{1,4},{2,7},{3,6},{4,1},{5,0},{6,3},{7,2},{8,13},{9,12},{10,... | collective-permute-start | bytes 786440 | tf_op jit(solution)/shard_map/ppermute | solution.py:21
  92.0 41.2 %collective-permute-start.12 = (f32[16,4,8,128]{3,2,1,0:T(8,128)S(1)}, f32[16,4,8,128]{3,2,1,0:T(8,128)S(1)}, u32[]{:S(2)}, u32[]{:S(2)}) collective-permute-start(f32[16,4,8,128]{3,2,1,0:T(8,128)S(1)} %get-tuple-element.21), channel_id=1, source_target_pairs={{0,6},{1,7},{2,4},{3,5},{4,2},{5,3},{6,0},{7,1},{8,14},{9,15},{10,... | collective-permute-start | bytes 786440 | tf_op jit(solution)/shard_map/ppermute | solution.py:21
  94.8 43.3 %collective-permute-start.13 = (f32[16,4,8,128]{3,2,1,0:T(8,128)S(1)}, f32[16,4,8,128]{3,2,1,0:T(8,128)S(1)}, u32[]{:S(2)}, u32[]{:S(2)}) collective-permute-start(f32[16,4,8,128]{3,2,1,0:T(8,128)S(1)} %get-tuple-element.22), channel_id=1, source_target_pairs={{0,7},{1,6},{2,5},{3,4},{4,3},{5,2},{6,1},{7,0},{8,15},{9,14},{10,... | collective-permute-start | bytes 786440 | tf_op jit(solution)/shard_map/ppermute | solution.py:21
  141.2 1.3 collective-permute-start.14
  142.5 4.4 %collective-permute-start.15 = (f32[128,128]{1,0:T(8,128)S(1)}, f32[128,128]{1,0:T(8,128)S(1)}, u32[]{:S(2)}, u32[]{:S(2)}) collective-permute-start(f32[128,128]{1,0:T(8,128)S(1)} %add.30), channel_id=1, source_target_pairs={{0,2},{1,3},{2,0},{3,1},{4,6},{5,7},{6,4},{7,5},{8,10},{9,11},{10,... | collective-permute-start | bytes 196616 | tf_op jit(solution)/shard_map/ppermute | solution.py:21
  146.9 5.3 %collective-permute-start.16 = (f32[128,128]{1,0:T(8,128)S(1)}, f32[128,128]{1,0:T(8,128)S(1)}, u32[]{:S(2)}, u32[]{:S(2)}) collective-permute-start(f32[128,128]{1,0:T(8,128)S(1)} %add.31), channel_id=1, source_target_pairs={{0,4},{1,5},{2,6},{3,7},{4,0},{5,1},{6,2},{7,3},{8,12},{9,13},{10,... | collective-permute-start | bytes 196616 | tf_op jit(solution)/shard_map/ppermute | solution.py:21
  152.2 4.5 %collective-permute-start.19 = (f32[128,128]{1,0:T(8,128)S(1)}, f32[128,128]{1,0:T(8,128)S(1)}, u32[]{:S(2)}, u32[]{:S(2)}) collective-permute-start(f32[128,128]{1,0:T(8,128)S(1)} %add.32), channel_id=1, source_target_pairs={{0,24},{8,0},{16,8},{24,16},{32,56},{40,32},{48,40},{56,48},{64,88... | collective-permute-start | bytes 196616 | tf_op jit(solution)/shard_map/ppermute | solution.py:21
  152.4 5.9 %collective-permute-start.18 = (f32[128,128]{1,0:T(8,128)S(1)}, f32[128,128]{1,0:T(8,128)S(1)}, u32[]{:S(2)}, u32[]{:S(2)}) collective-permute-start(f32[128,128]{1,0:T(8,128)S(1)} %add.32), channel_id=1, source_target_pairs={{0,16},{8,24},{16,0},{24,8},{32,48},{40,56},{48,32},{56,40},{64,80... | collective-permute-start | bytes 196616 | tf_op jit(solution)/shard_map/ppermute | solution.py:21
  152.5 6.8 %collective-permute-start.17 = (f32[128,128]{1,0:T(8,128)S(1)}, f32[128,128]{1,0:T(8,128)S(1)}, u32[]{:S(2)}, u32[]{:S(2)}) collective-permute-start(f32[128,128]{1,0:T(8,128)S(1)} %add.32), channel_id=1, source_target_pairs={{0,8},{8,16},{16,24},{24,0},{32,40},{40,48},{48,56},{56,32},{64,72... | collective-permute-start | bytes 196616 | tf_op jit(solution)/shard_map/ppermute | solution.py:21
  159.4 10.1 %collective-permute-start.22 = (f32[128,128]{1,0:T(8,128)S(1)}, f32[128,128]{1,0:T(8,128)S(1)}, u32[]{:S(2)}, u32[]{:S(2)}) collective-permute-start(f32[128,128]{1,0:T(8,128)S(1)} %add_add_fusion.1), channel_id=1, source_target_pairs={{0,96},{8,104},{16,112},{24,120},{32,0},{40,8},{48,16},{56,24},{64... | collective-permute-start | bytes 196616 | tf_op jit(solution)/shard_map/ppermute | solution.py:21
  167.0 5.9 %collective-permute-start.21 = (f32[128,128]{1,0:T(8,128)S(1)}, f32[128,128]{1,0:T(8,128)S(1)}, u32[]{:S(2)}, u32[]{:S(2)}) collective-permute-start(f32[128,128]{1,0:T(8,128)S(1)} %add_add_fusion.1), channel_id=1, source_target_pairs={{0,64},{8,72},{16,80},{24,88},{32,96},{40,104},{48,112},{56,120},{... | collective-permute-start | bytes 196616 | tf_op jit(solution)/shard_map/ppermute | solution.py:21
  167.0 6.2 %collective-permute-start.20 = (f32[128,128]{1,0:T(8,128)S(1)}, f32[128,128]{1,0:T(8,128)S(1)}, u32[]{:S(2)}, u32[]{:S(2)}) collective-permute-start(f32[128,128]{1,0:T(8,128)S(1)} %add_add_fusion.1), channel_id=1, source_target_pairs={{0,32},{8,40},{16,48},{24,56},{32,64},{40,72},{48,80},{56,88},{64,... | collective-permute-start | bytes 196616 | tf_op jit(solution)/shard_map/ppermute | solution.py:21
  173.2 8.4 %collective-permute-start.23 = (f32[128,128]{1,0:T(8,128)S(1)}, f32[128,128]{1,0:T(8,128)S(1)}, u32[]{:S(2)}, u32[]{:S(2)}) collective-permute-start(f32[128,128]{1,0:T(8,128)S(1)} %add_add_fusion), channel_id=1, source_target_pairs={{0,128},{8,136},{16,144},{24,152},{32,160},{40,168},{48,176},{56,1... | collective-permute-start | bytes 196616 | tf_op jit(solution)/shard_map/ppermute | solution.py:21

commit v5 on v2

--- a/solution.py
+++ b/solution.py
@@ -9,10 +9,10 @@
 from jax.sharding import PartitionSpec as P
 
 DEPTH = 3
-PARTS = 1
+PARTS = 2
 PANEL = 32
 SIDE = 4
-SHARES = (6, 4, 3, 3)
+DETOURS = ((3, 2), (0, 1))
 
 
 def permuted(block, axis, target):
@@ -26,16 +26,14 @@
     return beside + pltpu.roll(plane, 1, 1) + pltpu.roll(plane, lanes - 1, 1)
 
 
-def filter_kernel(shares, stripes, field, low, high, pot, pot_low, pot_high, pot_seam, *rest):
+def filter_kernel(shares, stripes, field, pot, pot_low, pot_high, pot_seam, low, high, *rest):
     routes = len(shares)
-    seams, outs = rest[:routes], rest[routes : routes + stripes]
-    zero, one, two, three, local = rest[routes + stripes :]
-    me = lax.axis_index("band")
+    seams, (out, zero, one, two, local) = rest[:routes], rest[routes:]
     at = lax.rem(lax.axis_index("domain"), SIDE * SIDE)
     at_low, at_high = at == 0, at == SIDE * SIDE - 1
     planes = field.shape[1]
     top = planes + 2 * DEPTH
-    width = outs[0].shape[2]
+    width = out.shape[3]
     own = pl.ds(DEPTH, planes)
     local[own] = 0.8 * pot[...] - 1.2
     local[:DEPTH] = 0.8 * jnp.where(at_low, pot_seam[...], pot_low[...]) - 1.2
@@ -54,10 +52,9 @@
             two[k] = local[k] * one[k] - 0.4 * beside - zero[k]
         for k in range(3, top - 3):
             beside = two[k - 1] + two[k + 1] + neighbours(two[k])
-            three[k - 3] = local[k] * two[k] - 0.4 * beside - one[k]
-        for slot in range(stripes):
-            start = pl.multiple_of(jnp.bitwise_xor(me, slot) * width, width)
-            outs[slot][orbital] = three[:, pl.ds(start, width), :]
+            three = local[k] * two[k] - 0.4 * beside - one[k]
+            for stripe in range(stripes):
+                out[stripe, orbital, k - 3] = three[stripe * width : (stripe + 1) * width]
 
     first = 0
     for share, seam in zip(shares, seams):
@@ -70,24 +67,22 @@
         first += share
 
 
-def filtered_stripes(field, low, high, pots, seams, stripes):
+def filtered_stripes(field, pots, low, high, seams, stripes):
     count, planes, rows, lanes = field.shape
     width = rows // stripes
     top = planes + 2 * DEPTH
-    shares = [seam.shape[0] for seam in seams]
-    shape = jax.ShapeDtypeStruct((count, planes, width, lanes), jnp.float32)
+    shares = [count // len(seams)] * len(seams)
     return pl.pallas_call(
         functools.partial(filter_kernel, shares, stripes),
-        out_shape=[shape] * stripes,
+        out_shape=jax.ShapeDtypeStruct((stripes, count, planes, width, lanes), jnp.float32),
         scratch_shapes=[
             pltpu.VMEM((top, rows, lanes), jnp.float32),
             pltpu.VMEM((top, rows, lanes), jnp.float32),
             pltpu.VMEM((top, rows, lanes), jnp.float32),
-            pltpu.VMEM((planes, rows, lanes), jnp.float32),
             pltpu.VMEM((top, rows, lanes), jnp.float32),
         ],
         compiler_params=pltpu.CompilerParams(vmem_limit_bytes=40 * 1024 * 1024),
-    )(field, low, high, *pots, *seams)
+    )(field, *pots, low, high, *seams)
 
 
 def inner_pairs(step):
@@ -96,45 +91,53 @@
     return [(i, i + step) for i in range(2 * half) if i % half != seam]
 
 
-def seam_pairs():
-    half = SIDE * SIDE
-    pairs = []
-    for h in (0, 1):
-        other = (1 - h) * half
-        pairs += [(h * half + half - 1, other), (h * half, other + half - 1)]
-    return pairs
-
-
-def detour_pairs(route):
+def detour_pairs(route, bands):
     half, last = SIDE * SIDE, SIDE - 1
-    up, down = route * SIDE + last, (last - route) * SIDE
     out, back = [], []
     for h in (0, 1):
-        other = (1 - h) * half
-        out += [(h * half + half - 1, other + up), (h * half, other + down)]
-        back += [(other + up, other), (other + down, other + half - 1)]
+        own, other = h * half, (1 - h) * half
+        for band in range(bands):
+            column = DETOURS[route][band // 2 % 2]
+            up, down = column * SIDE, (last - column) * SIDE + last
+            for start, middle, end in (
+                (own + half - 1, own + up, other),
+                (own, own + down, other + half - 1),
+            ):
+                out.append((start * bands + band, middle * bands + band))
+                back.append((middle * bands + band, end * bands + band))
     return out, back
 
 
 def halos(block):
-    lows, highs = block[..., :DEPTH, :, :], block[..., block.shape[-3] - DEPTH :, :, :]
+    bands = lax.axis_size("band")
+    planes = block.shape[1]
+    lows, highs = block[:, :DEPTH], block[:, planes - DEPTH :]
+    at = lax.rem(lax.axis_index("domain"), SIDE * SIDE)
+    across = jnp.where(at == 0, lows, highs)
+    share = block.shape[0] // len(DETOURS)
+    seams = []
+    for route in range(len(DETOURS)):
+        out, back = detour_pairs(route, bands)
+        piece = across[route * share :][: share if route + 1 < len(DETOURS) else None]
+        piece = lax.ppermute(piece, ("domain", "band"), out)
+        seams.append(lax.ppermute(piece, ("domain", "band"), back))
     low = lax.ppermute(highs, "domain", inner_pairs(1))
     high = lax.ppermute(lows, "domain", inner_pairs(-1))
-    at = lax.rem(lax.axis_index("domain"), SIDE * SIDE)
-    return low, high, jnp.where(at == 0, lows, highs)
-
-
-def gram_kernel(pieces, cells, *rest):
+    return low, high, seams
+
+
+def gram_kernel(cells, *rest):
     refs, (flat, gram) = rest[:-2], rest[-2:]
-    me = lax.axis_index("band")
-    lanes = refs[0].shape[1]
-    share = refs[0].shape[0] // cells
-    for index, ref in enumerate(refs):
-        slot, piece = divmod(index, pieces)
-        first = jnp.bitwise_xor(me, slot) * (share * pieces) + piece * share
-        rows = pl.ds(pl.multiple_of(first, share), share)
-        for r in range(cells):
-            flat[rows, r * lanes : (r + 1) * lanes] = ref[pl.ds(r, share, stride=cells), :]
+    lanes = refs[0].shape[2]
+    share = refs[0].shape[1] // cells
+    own = share * len(refs)
+    for piece, ref in enumerate(refs):
+        for band in range(ref.shape[0]):
+            first = band * own + piece * share
+            for r in range(cells):
+                flat[first : first + share, r * lanes : (r + 1) * lanes] = ref[
+                    band, pl.ds(r, share, stride=cells), :
+                ]
     whole = flat[...]
     gram[...] = lax.dot_general(
         whole,
@@ -145,13 +148,12 @@
     )
 
 
-def flat_and_gram(slots, orbitals):
-    pieces = len(slots[0])
-    _, planes, width, lanes = slots[0][0].shape
+def flat_and_gram(pieces, orbitals):
+    bands, _, planes, width, lanes = pieces[0].shape
     cells = planes * width
-    refs = [piece.reshape(-1, lanes) for slot in slots for piece in slot]
-    return pl.pallas_call(
-        functools.partial(gram_kernel, pieces, cells),
+    refs = [piece.reshape(bands, -1, lanes) for piece in pieces]
+    return pl.pallas_call(
+        functools.partial(gram_kernel, cells),
         out_shape=[
             jax.ShapeDtypeStruct((orbitals, cells * lanes), jnp.float32),
             jax.ShapeDtypeStruct((orbitals, orbitals), jnp.float32),
@@ -257,29 +259,18 @@
     orb_total = own * stripes
     cell_total = planes * lax.axis_size("domain") * ny_all * nx_all
 
-    pot_low, pot_high, pot_seam = halos(potential)
-    pots = (potential, pot_low, pot_high, lax.ppermute(pot_seam, "domain", seam_pairs()))
     share = own // PARTS
     pieces = []
     for part in range(PARTS):
         field = orbitals[part * share : (part + 1) * share]
-        low, high, across = halos(field)
-        seams, first = [], 0
-        for route, width in enumerate(SHARES):
-            block = across[first : first + width]
-            first += width
-            if route == 0:
-                seams.append(lax.ppermute(block, "domain", seam_pairs()))
-            else:
-                out, back = detour_pairs(route - 1)
-                seams.append(lax.ppermute(lax.ppermute(block, "domain", out), "domain", back))
-        slots = filtered_stripes(field, low, high, pots, seams, stripes)
-        pieces.append(
-            [slots[0]]
-            + [permuted(slots[k], "band", lambda i: i ^ k) for k in range(1, stripes)]
-        )
-    slots = [[piece[k] for piece in pieces] for k in range(stripes)]
-    flat, partial_gram = flat_and_gram(slots, orb_total)
+        if part == 0:
+            low, high, seams = halos(jnp.concatenate([field, potential[None]]))
+            pots = (potential, low[share], high[share], seams[-1][-1])
+        else:
+            low, high, seams = halos(field)
+        striped = filtered_stripes(field, pots, low, high, seams, stripes)
+        pieces.append(lax.all_to_all(striped, "band", 0, 0, tiled=True))
+    flat, partial_gram = flat_and_gram(pieces, orb_total)
     gram = summed(partial_gram)
     inverse = scaled_inverse(gram, math.sqrt(cell_total))
     return rotated(inverse, flat, nx_all).reshape(

time: 236 us -> 212 us (0.90)
  starting transfers between devices: 82.4 us -> 45.7 us
  blocking collectives: 0 us -> 35.5 us
  waiting for transfers between devices: 132 us -> 107 us
    ppermute x17 -> x10, waiting for transfers between devices: 65 us -> 21.1 us  [permuted(): return lax.ppermute(block, axis, [(i, target(i)) for i in range(count)])]
    all_to_all x0 -> x1, blocking collectives: none -> 35.5 us  [body(): pieces.append(lax.all_to_all(striped, 'band', 0, 0, tiled=True))]
    ppermute x8, waiting for transfers between devices: 53.4 us -> 85.4 us  [the longest x4 44.6 us: halos(): seams.append(lax.ppermute(piece, ('domain', 'band'), back))]
    ppermute x17 -> x10, starting transfers between devices: 36.9 us -> 13 us  [permuted(): return lax.ppermute(block, axis, [(i, target(i)) for i in range(count)])]
    ppermute x8, starting transfers between devices: 38.1 us -> 21.8 us  [the longest x4 16.6 us: halos(): piece = lax.ppermute(piece, ('domain', 'band'), out)]
    ppermute x2, waiting for transfers between devices: 13.2 us -> 0.01 us  [halos(): low = lax.ppermute(highs, 'domain', inner_pairs(1))]
    all_to_all x0 -> x1, starting transfers between devices: none -> 3.51 us  [body(): pieces.append(lax.all_to_all(striped, 'band', 0, 0, tiled=True))]
    pallas_call x1 -> x2, Pallas kernels: 6.61 us -> 7.29 us  [filtered_stripes(): pl.pallas_call(functools.partial(filter_kernel, shares, stripes), out_sha...]
  transfers between devices with their start and end apart: 29 -> 23, of which waited for: 21 -> 17; matrix products, arithmetic and copies ran while one was open for 0% -> 1% of each run, Pallas kernels for 0% -> 1%
where the time goes in v5:
time: 212 us; the launch traced here: 211 us
  waiting for transfers between devices  107 us (50%)
  starting transfers between devices  45.7 us (22%)
  blocking collectives  35.5 us (17%)
  Pallas kernels  18.4 us (9%)
  other arithmetic  2.12 us (1%)
    ppermute x4, waiting for transfers between devices, halos(): seams.append(lax.ppermute(piece, ('domain', 'band'), back))  44.6 us
    ppermute x4, waiting for transfers between devices, halos(): piece = lax.ppermute(piece, ('domain', 'band'), out)  40.8 us
    all_to_all x1, blocking collectives, body(): pieces.append(lax.all_to_all(striped, 'band', 0, 0, tiled=True))  35.5 us
    ppermute x10, waiting for transfers between devices, permuted(): return lax.ppermute(block, axis, [(i, target(i)) for i in range(count)])  21.1 us
    ppermute x4, starting transfers between devices, halos(): piece = lax.ppermute(piece, ('domain', 'band'), out)  16.6 us
    ppermute x10, starting transfers between devices, permuted(): return lax.ppermute(block, axis, [(i, target(i)) for i in range(count)])  13 us
    pallas_call x2, Pallas kernels, filtered_stripes(): pl.pallas_call(functools.partial(filter_kernel, shares, stripes), out_sha...  7.29 us
    ppermute x4, starting transfers between devices, halos(): seams.append(lax.ppermute(piece, ('domain', 'band'), back))  5.12 us
  transfers between devices with their start and end apart: 23, of which 17 were waited for; matrix products, arithmetic and copies ran while one was open for 1% of the time, Pallas kernels for 1%

profile of v5, /device:TPU:32, one launch (start us, length us, event | category | flops | bytes accessed | tf_op | source)
XLA Modules:
  0.0 210.6 jit_solution(3478696587782765004)
XLA Ops:
  0.0 0.0 copy-start
  0.0 1.8 fusion.2
  1.8 0.0 copy-done
  1.8 0.3 broadcast_select_fusion
  2.1 3.5 %collective-permute-start = (f32[9,3,64,128]{3,2,1,0:T(8,128)S(1)}, f32[9,3,64,128]{3,2,1,0:T(8,128)S(1)}, u32[]{:S(2)}, u32[]{:S(2)}) collective-permute-start(f32[9,3,64,128]{3,2,1,0:T(8,128)S(1)} %get-tuple-element.11), channel_id=1, source_target_pairs={{0,8},{8,16},{16,24},{24,32},{32,40},{40,48},{48,56},{56,64},{64,7... | collective-permute-start | bytes 2654216 | tf_op jit(solution)/shard_map/ppermute | solution.py:124
  5.7 1.3 collective-permute-start.1
  7.0 8.4 %collective-permute-start.2 = (f32[5,3,64,128]{3,2,1,0:T(8,128)S(1)}, f32[5,3,64,128]{3,2,1,0:T(8,128)S(1)}, u32[]{:S(2)}, u32[]{:S(2)}) collective-permute-start(f32[5,3,64,128]{3,2,1,0:T(8,128)S(1)} %slice.58), channel_id=1, source_target_pairs={{120,0},{0,120},{121,1},{1,121},{122,34},{2,90},{123,35},{3,91},{1... | collective-permute-start | bytes 1474568 | tf_op jit(solution)/shard_map/ppermute | solution.py:122
  15.5 1.3 collective-permute-start.4
  16.8 15.9 %collective-permute-done.2 = f32[5,3,64,128]{3,2,1,0:T(8,128)S(1)} collective-permute-done((f32[5,3,64,128]{3,2,1,0:T(8,128)S(1)}, f32[5,3,64,128]{3,2,1,0:T(8,128)S(1)}, u32[]{:S(2)}, u32[]{:S(2)}) %collective-permute-start.2) | collective-permute-done | bytes 491552 | tf_op jit(solution)/shard_map/ppermute | solution.py:122
  32.6 1.3 collective-permute-start.3
  33.9 5.4 %collective-permute-done.4 = f32[4,3,64,128]{3,2,1,0:T(8,128)S(1)} collective-permute-done((f32[4,3,64,128]{3,2,1,0:T(8,128)S(1)}, f32[4,3,64,128]{3,2,1,0:T(8,128)S(1)}, u32[]{:S(2)}, u32[]{:S(2)}) %collective-permute-start.4) | collective-permute-done | bytes 393248 | tf_op jit(solution)/shard_map/ppermute | solution.py:122
  39.3 1.3 collective-permute-start.5
  40.6 0.0 collective-permute-done.low
  40.6 0.0 collective-permute-done.1.high
  40.7 23.1 %collective-permute-done.3.rest_1_ = f32[5,3,64,128]{3,2,1,0:T(8,128)S(1)} collective-permute-done((f32[5,3,64,128]{3,2,1,0:T(8,128)S(1)}, f32[5,3,64,128]{3,2,1,0:T(8,128)S(1)}, u32[]{:S(2)}, u32[]{:S(2)}) %collective-permute-start.3) | collective-permute-done | bytes 491552 | tf_op jit(solution)/shard_map/ppermute | solution.py:123
  63.7 0.0 copy-start.1
  63.7 3.5 %collective-permute-done.5.rest_0_ = f32[4,3,64,128]{3,2,1,0:T(8,128)S(1)} collective-permute-done((f32[4,3,64,128]{3,2,1,0:T(8,128)S(1)}, f32[4,3,64,128]{3,2,1,0:T(8,128)S(1)}, u32[]{:S(2)}, u32[]{:S(2)}) %collective-permute-start.5) | collective-permute-done | bytes 393248 | tf_op jit(solution)/shard_map/ppermute | solution.py:123
  67.2 4.1 %shard_map.28 = f32[8,8,4,8,128]{4,3,2,1,0:T(8,128)} custom-call(f32[8,4,64,128]{3,2,1,0:T(8,128)S(1)} %get-tuple-element.16.field, f32[4,64,128]{2,1,0:T(8,128)S(1)} %copy-done, f32[3,64,128]{2,1,0:T(8,128)S(1)} %slice_bitcast_fusion.2.pot_low, f32[3,64,128]{2,1,0:T(8,128)S(1)} %slice_bitcast_fusion.1.pot_high, ...), custom_call_target="tpu_custom_call" | custom-call | tf_op jit(solution)/shard_map/pallas_call | solution.py:75
  71.3 0.0 copy-done.1
  71.4 3.5 %all-to-all-start = ((f32[8,8,4,8,128]{4,3,2,1,0:T(8,128)}), f32[8,8,4,8,128]{4,3,2,1,0:T(8,128)S(1)}, u32[]{:S(2)}, u32[]{:S(2)}) async-start(f32[8,8,4,8,128]{4,3,2,1,0:T(8,128)} %shard_map.28), calls=%async_computation | async-start | bytes 2097152 | tf_op jit(solution)/shard_map/all_to_all | solution.py:272
  74.9 0.0 copy-start.2
  74.9 1.7 broadcast_select_fusion.1
  76.6 1.3 collective-permute-start.6
  78.0 1.3 collective-permute-start.7
  79.3 0.1 fusion.3
  79.3 3.9 %collective-permute-start.8 = (f32[4,3,64,128]{3,2,1,0:T(8,128)S(1)}, f32[4,3,64,128]{3,2,1,0:T(8,128)S(1)}, u32[]{:S(2)}, u32[]{:S(2)}) collective-permute-start(f32[4,3,64,128]{3,2,1,0:T(8,128)S(1)} %get-tuple-element.18), channel_id=1, source_target_pairs={{120,96},{0,24},{121,97},{1,25},{122,66},{2,58},{123,67},{3,59},{1... | collective-permute-start | bytes 1179656 | tf_op jit(solution)/shard_map/ppermute | solution.py:122
  83.3 3.0 %collective-permute-start.10 = (f32[4,3,64,128]{3,2,1,0:T(8,128)S(1)}, f32[4,3,64,128]{3,2,1,0:T(8,128)S(1)}, u32[]{:S(2)}, u32[]{:S(2)}) collective-permute-start(f32[4,3,64,128]{3,2,1,0:T(8,128)S(1)} %get-tuple-element.17), channel_id=1, source_target_pairs={{120,0},{0,120},{121,1},{1,121},{122,34},{2,90},{123,35},{3,91},{1... | collective-permute-start | bytes 1179656 | tf_op jit(solution)/shard_map/ppermute | solution.py:122
  86.3 12.4 %collective-permute-done.8 = f32[4,3,64,128]{3,2,1,0:T(8,128)S(1)} collective-permute-done((f32[4,3,64,128]{3,2,1,0:T(8,128)S(1)}, f32[4,3,64,128]{3,2,1,0:T(8,128)S(1)}, u32[]{:S(2)}, u32[]{:S(2)}) %collective-permute-start.8) | collective-permute-done | bytes 393248 | tf_op jit(solution)/shard_map/ppermute | solution.py:122
  98.6 1.3 collective-permute-start.9
  99.9 7.2 %collective-permute-done.10 = f32[4,3,64,128]{3,2,1,0:T(8,128)S(1)} collective-permute-done((f32[4,3,64,128]{3,2,1,0:T(8,128)S(1)}, f32[4,3,64,128]{3,2,1,0:T(8,128)S(1)}, u32[]{:S(2)}, u32[]{:S(2)}) %collective-permute-start.10) | collective-permute-done | bytes 393248 | tf_op jit(solution)/shard_map/ppermute | solution.py:122
  107.2 1.3 collective-permute-start.11
  108.5 0.0 collective-permute-done.6.low
  108.5 0.0 collective-permute-done.7.high
  108.5 11.6 %collective-permute-done.9.rest_0_ = f32[4,3,64,128]{3,2,1,0:T(8,128)S(1)} collective-permute-done((f32[4,3,64,128]{3,2,1,0:T(8,128)S(1)}, f32[4,3,64,128]{3,2,1,0:T(8,128)S(1)}, u32[]{:S(2)}, u32[]{:S(2)}) %collective-permute-start.9) | collective-permute-done | bytes 393248 | tf_op jit(solution)/shard_map/ppermute | solution.py:123
  120.1 6.4 %collective-permute-done.11.rest_1_ = f32[4,3,64,128]{3,2,1,0:T(8,128)S(1)} collective-permute-done((f32[4,3,64,128]{3,2,1,0:T(8,128)S(1)}, f32[4,3,64,128]{3,2,1,0:T(8,128)S(1)}, u32[]{:S(2)}, u32[]{:S(2)}) %collective-permute-start.11) | collective-permute-done | bytes 393248 | tf_op jit(solution)/shard_map/ppermute | solution.py:123
  126.5 0.0 copy-done.2
  126.5 3.2 %shard_map.29 = f32[8,8,4,8,128]{4,3,2,1,0:T(8,128)S(1)} custom-call(f32[8,4,64,128]{3,2,1,0:T(8,128)S(1)} %get-tuple-element.15.field, f32[4,64,128]{2,1,0:T(8,128)S(1)} %copy-done, f32[3,64,128]{2,1,0:T(8,128)S(1)} %slice_bitcast_fusion.2.pot_low, f32[3,64,128]{2,1,0:T(8,128)S(1)} %slice_bitcast_fusion.1.pot_high, f32[3,64,128]{2,1,0:T(8,128)S(1)} %copy-done.2, ...), custom_call_target="tpu_custom_call" | custom-call | tf_op jit(solution)/shard_map/pallas_call | solution.py:75
  129.7 0.0 all-to-all-done
  129.7 35.5 %all_to_all.10 = f32[8,8,4,8,128]{4,3,2,1,0:T(8,128)S(1)} all-to-all(f32[8,8,4,8,128]{4,3,2,1,0:T(8,128)S(1)} %shard_map.29), channel_id=1, replica_groups=mesh['domain'=32,'band'=8] {'band'}, dimensions={0} | all-to-all | bytes 2097152 | tf_op jit(solution)/shard_map/all_to_all | solution.py:272
  165.2 2.7 %shard_map.30 = (f32[128,4096]{1,0:T(8,128)S(1)}, f32[128,128]{1,0:T(8,128)S(1)}) custom-call(f32[8,256,128]{2,1,0:T(8,128)S(1)} %bitcast.10, f32[8,256,128]{2,1,0:T(8,128)S(1)} %bitcast.11), custom_call_target="tpu_custom_call" | custom-call | tf_op jit(solution)/shard_map/pallas_call | solution.py:155
  168.0 0.1 collective-permute-start.12
  168.1 1.2 collective-permute-done.12
  169.3 2.5 %collective-permute-start.13 = (f32[128,128]{1,0:T(8,128)S(1)}, f32[128,128]{1,0:T(8,128)S(1)}, u32[]{:S(2)}, u32[]{:S(2)}) collective-permute-start(f32[128,128]{1,0:T(8,128)S(1)} %add.30), channel_id=1, source_target_pairs={{0,2},{1,3},{2,0},{3,1},{4,6},{5,7},{6,4},{7,5},{8,10},{9,11},{10,... | collective-permute-start | bytes 196616 | tf_op jit(solution)/shard_map/ppermute | solution.py:20
  171.8 2.4 %collective-permute-done.13 = f32[128,128]{1,0:T(8,128)S(1)} collective-permute-done((f32[128,128]{1,0:T(8,128)S(1)}, f32[128,128]{1,0:T(8,128)S(1)}, u32[]{:S(2)}, u32[]{:S(2)}) %collective-permute-start.13) | collective-permute-done | bytes 65568 | tf_op jit(solution)/shard_map/ppermute | solution.py:20
  174.2 1.7 collective-permute-start.14
  175.9 3.6 %collective-permute-done.14 = f32[128,128]{1,0:T(8,128)S(1)} collective-permute-done((f32[128,128]{1,0:T(8,128)S(1)}, f32[128,128]{1,0:T(8,128)S(1)}, u32[]{:S(2)}, u32[]{:S(2)}) %collective-permute-start.14) | collective-permute-done | bytes 65568 | tf_op jit(solution)/shard_map/ppermute | solution.py:20
  179.5 0.1 collective-permute-start.16
  179.6 0.1 collective-permute-start.17
  179.7 2.0 collective-permute-start.15
  181.7 3.7 %collective-permute-done.16 = f32[128,128]{1,0:T(8,128)S(1)} collective-permute-done((f32[128,128]{1,0:T(8,128)S(1)}, f32[128,128]{1,0:T(8,128)S(1)}, u32[]{:S(2)}, u32[]{:S(2)}) %collective-permute-start.16) | collective-permute-done | bytes 65568 | tf_op jit(solution)/shard_map/ppermute | solution.py:20
  185.4 0.0 collective-permute-done.17
  185.4 0.7 collective-permute-done.15
  186.1 0.1 collective-permute-start.19
  186.2 2.1 %collective-permute-start.20 = (f32[128,128]{1,0:T(8,128)S(1)}, f32[128,128]{1,0:T(8,128)S(1)}, u32[]{:S(2)}, u32[]{:S(2)}) collective-permute-start(f32[128,128]{1,0:T(8,128)S(1)} %add_add_fusion.1), channel_id=1, source_target_pairs={{0,96},{8,104},{16,112},{24,120},{32,0},{40,8},{48,16},{56,24},{64... | collective-permute-start | bytes 196616 | tf_op jit(solution)/shard_map/ppermute | solution.py:20
  188.3 0.8 collective-permute-start.18
  189.1 2.9 %collective-permute-done.19 = f32[128,128]{1,0:T(8,128)S(1)} collective-permute-done((f32[128,128]{1,0:T(8,128)S(1)}, f32[128,128]{1,0:T(8,128)S(1)}, u32[]{:S(2)}, u32[]{:S(2)}) %collective-permute-start.19) | collective-permute-done | bytes 65568 | tf_op jit(solution)/shard_map/ppermute | solution.py:20
  191.9 0.1 collective-permute-done.20
  192.0 1.8 collective-permute-done.18
  193.8 3.5 %collective-permute-start.21 = (f32[128,128]{1,0:T(8,128)S(1)}, f32[128,128]{1,0:T(8,128)S(1)}, u32[]{:S(2)}, u32[]{:S(2)}) collective-permute-start(f32[128,128]{1,0:T(8,128)S(1)} %add_add_fusion), channel_id=1, source_target_pairs={{0,128},{8,136},{16,144},{24,152},{32,160},{40,168},{48,176},{56,1... | collective-permute-start | bytes 196616 | tf_op jit(solution)/shard_map/ppermute | solution.py:20
  197.3 4.9 %collective-permute-done.21 = f32[128,128]{1,0:T(8,128)S(1)} collective-permute-done((f32[128,128]{1,0:T(8,128)S(1)}, f32[128,128]{1,0:T(8,128)S(1)}, u32[]{:S(2)}, u32[]{:S(2)}) %collective-permute-start.21) | collective-permute-done | bytes 65568 | tf_op jit(solution)/shard_map/ppermute | solution.py:20
  202.2 4.2 %shard_map.31.inverse = f32[128,128]{1,0:T(8,128)S(1)} custom-call(f32[128,128]{1,0:T(8,128)S(1)} %add.39.gram), custom_call_target="tpu_custom_call" | custom-call | tf_op jit(solution)/shard_map/pallas_call | solution.py:208
  206.4 4.2 %shard_map.32 = f32[4096,128]{1,0:T(8,128)} custom-call(f32[128,128]{1,0:T(8,128)S(1)} %shard_map.31.inverse, f32[128,4096]{1,0:T(8,128)S(1)} %get-tuple-element.8.flat), custom_call_target="tpu_custom_call" | custom-call | tf_op jit(solution)/shard_map/pallas_call | solution.py:232
  (11 shorter events, 0.2 us)
Async XLA Ops:
  0.0 1.8 copy-start
  2.1 38.5 %collective-permute-start = (f32[9,3,64,128]{3,2,1,0:T(8,128)S(1)}, f32[9,3,64,128]{3,2,1,0:T(8,128)S(1)}, u32[]{:S(2)}, u32[]{:S(2)}) collective-permute-start(f32[9,3,64,128]{3,2,1,0:T(8,128)S(1)} %get-tuple-element.11), channel_id=1, source_target_pairs={{0,8},{8,16},{16,24},{24,32},{32,40},{40,48},{48,56},{56,64},{64,7... | collective-permute-start | bytes 2654216 | tf_op jit(solution)/shard_map/ppermute | solution.py:124
  5.7 35.0 %collective-permute-start.1 = (f32[9,3,64,128]{3,2,1,0:T(8,128)S(1)}, f32[9,3,64,128]{3,2,1,0:T(8,128)S(1)}, u32[]{:S(2)}, u32[]{:S(2)}) collective-permute-start(f32[9,3,64,128]{3,2,1,0:T(8,128)S(1)} %get-tuple-element.10), channel_id=1, source_target_pairs={{8,0},{16,8},{24,16},{32,24},{40,32},{48,40},{56,48},{64,56},{72,6... | collective-permute-start | bytes 2654216 | tf_op jit(solution)/shard_map/ppermute | solution.py:125
  7.0 25.6 %collective-permute-start.2 = (f32[5,3,64,128]{3,2,1,0:T(8,128)S(1)}, f32[5,3,64,128]{3,2,1,0:T(8,128)S(1)}, u32[]{:S(2)}, u32[]{:S(2)}) collective-permute-start(f32[5,3,64,128]{3,2,1,0:T(8,128)S(1)} %slice.58), channel_id=1, source_target_pairs={{120,0},{0,120},{121,1},{1,121},{122,34},{2,90},{123,35},{3,91},{1... | collective-permute-start | bytes 1474568 | tf_op jit(solution)/shard_map/ppermute | solution.py:122
  15.5 23.8 %collective-permute-start.4 = (f32[4,3,64,128]{3,2,1,0:T(8,128)S(1)}, f32[4,3,64,128]{3,2,1,0:T(8,128)S(1)}, u32[]{:S(2)}, u32[]{:S(2)}) collective-permute-start(f32[4,3,64,128]{3,2,1,0:T(8,128)S(1)} %slice.60), channel_id=1, source_target_pairs={{120,96},{0,24},{121,97},{1,25},{122,66},{2,58},{123,67},{3,59},{1... | collective-permute-start | bytes 1179656 | tf_op jit(solution)/shard_map/ppermute | solution.py:122
  32.6 31.1 %collective-permute-start.3 = (f32[5,3,64,128]{3,2,1,0:T(8,128)S(1)}, f32[5,3,64,128]{3,2,1,0:T(8,128)S(1)}, u32[]{:S(2)}, u32[]{:S(2)}) collective-permute-start(f32[5,3,64,128]{3,2,1,0:T(8,128)S(1)} %collective-permute-done.2), channel_id=1, source_target_pairs={{0,128},{120,248},{1,129},{121,249},{34,130},{90,250},{35,131},{91... | collective-permute-start | bytes 1474568 | tf_op jit(solution)/shard_map/ppermute | solution.py:123
  39.3 27.9 %collective-permute-start.5 = (f32[4,3,64,128]{3,2,1,0:T(8,128)S(1)}, f32[4,3,64,128]{3,2,1,0:T(8,128)S(1)}, u32[]{:S(2)}, u32[]{:S(2)}) collective-permute-start(f32[4,3,64,128]{3,2,1,0:T(8,128)S(1)} %collective-permute-done.4), channel_id=1, source_target_pairs={{96,128},{24,248},{97,129},{25,249},{66,130},{58,250},{67,131},{59... | collective-permute-start | bytes 1179656 | tf_op jit(solution)/shard_map/ppermute | solution.py:123
  63.7 7.6 %copy-start.1 = (f32[3,64,128]{2,1,0:T(8,128)}, f32[3,64,128]{2,1,0:T(8,128)S(1)}, u32[]{:S(2)}) copy-start(f32[3,64,128]{2,1,0:T(8,128)S(1)} %slice_bitcast_fusion.pot_seam) | copy-start | bytes 294916
  71.4 58.3 %all-to-all-start = ((f32[8,8,4,8,128]{4,3,2,1,0:T(8,128)}), f32[8,8,4,8,128]{4,3,2,1,0:T(8,128)S(1)}, u32[]{:S(2)}, u32[]{:S(2)}) async-start(f32[8,8,4,8,128]{4,3,2,1,0:T(8,128)} %shard_map.28), calls=%async_computation | async-start | bytes 2097152 | tf_op jit(solution)/shard_map/all_to_all | solution.py:272
  74.9 51.6 %copy-start.2 = (f32[3,64,128]{2,1,0:T(8,128)S(1)}, f32[3,64,128]{2,1,0:T(8,128)}, u32[]{:S(2)}) copy-start(f32[3,64,128]{2,1,0:T(8,128)} %copy-done.1) | copy-start | bytes 294916
  76.6 31.8 %collective-permute-start.6 = (f32[8,3,64,128]{3,2,1,0:T(8,128)S(1)}, f32[8,3,64,128]{3,2,1,0:T(8,128)S(1)}, u32[]{:S(2)}, u32[]{:S(2)}) collective-permute-start(f32[8,3,64,128]{3,2,1,0:T(8,128)S(1)} %get-tuple-element.14), channel_id=1, source_target_pairs={{0,8},{8,16},{16,24},{24,32},{32,40},{40,48},{48,56},{56,64},{64,7... | collective-permute-start | bytes 2359304 | tf_op jit(solution)/shard_map/ppermute | solution.py:124
  78.0 30.5 %collective-permute-start.7 = (f32[8,3,64,128]{3,2,1,0:T(8,128)S(1)}, f32[8,3,64,128]{3,2,1,0:T(8,128)S(1)}, u32[]{:S(2)}, u32[]{:S(2)}) collective-permute-start(f32[8,3,64,128]{3,2,1,0:T(8,128)S(1)} %get-tuple-element.13), channel_id=1, source_target_pairs={{8,0},{16,8},{24,16},{32,24},{40,32},{48,40},{56,48},{64,56},{72,6... | collective-permute-start | bytes 2359304 | tf_op jit(solution)/shard_map/ppermute | solution.py:125
  79.3 19.3 %collective-permute-start.8 = (f32[4,3,64,128]{3,2,1,0:T(8,128)S(1)}, f32[4,3,64,128]{3,2,1,0:T(8,128)S(1)}, u32[]{:S(2)}, u32[]{:S(2)}) collective-permute-start(f32[4,3,64,128]{3,2,1,0:T(8,128)S(1)} %get-tuple-element.18), channel_id=1, source_target_pairs={{120,96},{0,24},{121,97},{1,25},{122,66},{2,58},{123,67},{3,59},{1... | collective-permute-start | bytes 1179656 | tf_op jit(solution)/shard_map/ppermute | solution.py:122
  83.3 23.9 %collective-permute-start.10 = (f32[4,3,64,128]{3,2,1,0:T(8,128)S(1)}, f32[4,3,64,128]{3,2,1,0:T(8,128)S(1)}, u32[]{:S(2)}, u32[]{:S(2)}) collective-permute-start(f32[4,3,64,128]{3,2,1,0:T(8,128)S(1)} %get-tuple-element.17), channel_id=1, source_target_pairs={{120,0},{0,120},{121,1},{1,121},{122,34},{2,90},{123,35},{3,91},{1... | collective-permute-start | bytes 1179656 | tf_op jit(solution)/shard_map/ppermute | solution.py:122
  98.6 21.4 %collective-permute-start.9 = (f32[4,3,64,128]{3,2,1,0:T(8,128)S(1)}, f32[4,3,64,128]{3,2,1,0:T(8,128)S(1)}, u32[]{:S(2)}, u32[]{:S(2)}) collective-permute-start(f32[4,3,64,128]{3,2,1,0:T(8,128)S(1)} %collective-permute-done.8), channel_id=1, source_target_pairs={{96,128},{24,248},{97,129},{25,249},{66,130},{58,250},{67,131},{59... | collective-permute-start | bytes 1179656 | tf_op jit(solution)/shard_map/ppermute | solution.py:123
  107.2 19.3 %collective-permute-start.11 = (f32[4,3,64,128]{3,2,1,0:T(8,128)S(1)}, f32[4,3,64,128]{3,2,1,0:T(8,128)S(1)}, u32[]{:S(2)}, u32[]{:S(2)}) collective-permute-start(f32[4,3,64,128]{3,2,1,0:T(8,128)S(1)} %collective-permute-done.10), channel_id=1, source_target_pairs={{0,128},{120,248},{1,129},{121,249},{34,130},{90,250},{35,131},{91... | collective-permute-start | bytes 1179656 | tf_op jit(solution)/shard_map/ppermute | solution.py:123
  168.0 1.3 collective-permute-start.12
  169.3 4.9 %collective-permute-start.13 = (f32[128,128]{1,0:T(8,128)S(1)}, f32[128,128]{1,0:T(8,128)S(1)}, u32[]{:S(2)}, u32[]{:S(2)}) collective-permute-start(f32[128,128]{1,0:T(8,128)S(1)} %add.30), channel_id=1, source_target_pairs={{0,2},{1,3},{2,0},{3,1},{4,6},{5,7},{6,4},{7,5},{8,10},{9,11},{10,... | collective-permute-start | bytes 196616 | tf_op jit(solution)/shard_map/ppermute | solution.py:20
  174.2 5.3 %collective-permute-start.14 = (f32[128,128]{1,0:T(8,128)S(1)}, f32[128,128]{1,0:T(8,128)S(1)}, u32[]{:S(2)}, u32[]{:S(2)}) collective-permute-start(f32[128,128]{1,0:T(8,128)S(1)} %add.31), channel_id=1, source_target_pairs={{0,4},{1,5},{2,6},{3,7},{4,0},{5,1},{6,2},{7,3},{8,12},{9,13},{10,... | collective-permute-start | bytes 196616 | tf_op jit(solution)/shard_map/ppermute | solution.py:20
  179.5 5.9 %collective-permute-start.16 = (f32[128,128]{1,0:T(8,128)S(1)}, f32[128,128]{1,0:T(8,128)S(1)}, u32[]{:S(2)}, u32[]{:S(2)}) collective-permute-start(f32[128,128]{1,0:T(8,128)S(1)} %add.32), channel_id=1, source_target_pairs={{0,16},{8,24},{16,0},{24,8},{32,48},{40,56},{48,32},{56,40},{64,80... | collective-permute-start | bytes 196616 | tf_op jit(solution)/shard_map/ppermute | solution.py:20
  179.6 5.8 %collective-permute-start.17 = (f32[128,128]{1,0:T(8,128)S(1)}, f32[128,128]{1,0:T(8,128)S(1)}, u32[]{:S(2)}, u32[]{:S(2)}) collective-permute-start(f32[128,128]{1,0:T(8,128)S(1)} %add.32), channel_id=1, source_target_pairs={{0,24},{8,0},{16,8},{24,16},{32,56},{40,32},{48,40},{56,48},{64,88... | collective-permute-start | bytes 196616 | tf_op jit(solution)/shard_map/ppermute | solution.py:20
  179.7 6.4 %collective-permute-start.15 = (f32[128,128]{1,0:T(8,128)S(1)}, f32[128,128]{1,0:T(8,128)S(1)}, u32[]{:S(2)}, u32[]{:S(2)}) collective-permute-start(f32[128,128]{1,0:T(8,128)S(1)} %add.32), channel_id=1, source_target_pairs={{0,8},{8,16},{16,24},{24,0},{32,40},{40,48},{48,56},{56,32},{64,72... | collective-permute-start | bytes 196616 | tf_op jit(solution)/shard_map/ppermute | solution.py:20
  186.1 5.9 %collective-permute-start.19 = (f32[128,128]{1,0:T(8,128)S(1)}, f32[128,128]{1,0:T(8,128)S(1)}, u32[]{:S(2)}, u32[]{:S(2)}) collective-permute-start(f32[128,128]{1,0:T(8,128)S(1)} %add_add_fusion.1), channel_id=1, source_target_pairs={{0,64},{8,72},{16,80},{24,88},{32,96},{40,104},{48,112},{56,120},{... | collective-permute-start | bytes 196616 | tf_op jit(solution)/shard_map/ppermute | solution.py:20
  186.2 5.8 %collective-permute-start.20 = (f32[128,128]{1,0:T(8,128)S(1)}, f32[128,128]{1,0:T(8,128)S(1)}, u32[]{:S(2)}, u32[]{:S(2)}) collective-permute-start(f32[128,128]{1,0:T(8,128)S(1)} %add_add_fusion.1), channel_id=1, source_target_pairs={{0,96},{8,104},{16,112},{24,120},{32,0},{40,8},{48,16},{56,24},{64... | collective-permute-start | bytes 196616 | tf_op jit(solution)/shard_map/ppermute | solution.py:20
  188.3 5.5 %collective-permute-start.18 = (f32[128,128]{1,0:T(8,128)S(1)}, f32[128,128]{1,0:T(8,128)S(1)}, u32[]{:S(2)}, u32[]{:S(2)}) collective-permute-start(f32[128,128]{1,0:T(8,128)S(1)} %add_add_fusion.1), channel_id=1, source_target_pairs={{0,32},{8,40},{16,48},{24,56},{32,64},{40,72},{48,80},{56,88},{64,... | collective-permute-start | bytes 196616 | tf_op jit(solution)/shard_map/ppermute | solution.py:20
  193.8 8.4 %collective-permute-start.21 = (f32[128,128]{1,0:T(8,128)S(1)}, f32[128,128]{1,0:T(8,128)S(1)}, u32[]{:S(2)}, u32[]{:S(2)}) collective-permute-start(f32[128,128]{1,0:T(8,128)S(1)} %add_add_fusion), channel_id=1, source_target_pairs={{0,128},{8,136},{16,144},{24,152},{32,160},{40,168},{48,176},{56,1... | collective-permute-start | bytes 196616 | tf_op jit(solution)/shard_map/ppermute | solution.py:20

commit v6 on v4

--- a/solution.py
+++ b/solution.py
@@ -12,7 +12,7 @@
 PARTS = 1
 PANEL = 32
 SIDE = 4
-SHARES = (7, 5, 4)
+SHARES = (8, 4, 4)
 DETOURS = (0, 2)
 
 
@@ -119,21 +119,26 @@
 
 def halos(field, pot):
     planes = field.shape[1]
-    both = jnp.concatenate([field, pot[None]])
-    lows, highs = both[:, :DEPTH], both[:, planes - DEPTH :]
     at = lax.rem(lax.axis_index("domain"), SIDE * SIDE)
-    across = jnp.where(at == 0, lows, highs)
+
+    def across(first, stop):
+        block = field[first:stop]
+        return jnp.where(at == 0, block[:, :DEPTH], block[:, planes - DEPTH :])
+
     blocks, first = [], 0
     for share in SHARES:
-        blocks.append(across[first : first + share])
+        blocks.append(across(first, first + share))
         first += share
-    blocks[0] = jnp.concatenate([blocks[0], across[first:]])
+    last = jnp.where(at == 0, pot[:DEPTH], pot[planes - DEPTH :])
+    blocks[0] = jnp.concatenate([blocks[0], last[None]])
     seams = [lax.ppermute(blocks[0], "domain", seam_pairs())]
     for route, block in enumerate(blocks[1:]):
         out, back = detour_pairs(route)
         seams.append(lax.ppermute(lax.ppermute(block, "domain", out), "domain", back))
-    low = lax.ppermute(highs, "domain", inner_pairs(1))
-    high = lax.ppermute(lows, "domain", inner_pairs(-1))
+    field, pot, *_ = lax.optimization_barrier((field, pot, *blocks))
+    both = jnp.concatenate([field, pot[None]])
+    low = lax.ppermute(both[:, planes - DEPTH :], "domain", inner_pairs(1))
+    high = lax.ppermute(both[:, :DEPTH], "domain", inner_pairs(-1))
     return low, high, seams
 
 

time: 190 us -> 180 us (0.947)
  starting transfers between devices: 62.4 us -> 46.4 us
  waiting for transfers between devices: 106 us -> 110 us
    ppermute x17, starting transfers between devices: 35.2 us -> 24.4 us  [permuted(): return lax.ppermute(block, axis, [(i, target(i)) for i in range(count)])]
    ppermute x2, waiting for transfers between devices: 0.01 us -> 10.8 us  [halos(): lax.ppermute(block, 'domain', out)]
    ppermute x1, waiting for transfers between devices: 9.34 us -> 0.01 us  [halos(): seams = [lax.ppermute(blocks[0], 'domain', seam_pairs())]]
    ppermute x17, waiting for transfers between devices: 60.7 us -> 67.2 us  [permuted(): return lax.ppermute(block, axis, [(i, target(i)) for i in range(count)])]
    ppermute x2, starting transfers between devices: 7.3 us -> 2.63 us  [halos(): lax.ppermute(block, 'domain', out)]
    ppermute x2, waiting for transfers between devices: 36.1 us -> 32.4 us  [halos(): lax.ppermute(lax.ppermute(block, 'domain', out), 'domain', back)]
  transfers between devices with their start and end apart: 24 -> 24, of which waited for: 17 -> 20; matrix products, arithmetic and copies ran while one was open for 0% -> 0% of each run, Pallas kernels for 0% -> 0%
where the time goes in v6:
time: 180 us; the launch traced here: 179 us
  waiting for transfers between devices  110 us (61%)
  starting transfers between devices  46.4 us (26%)
  Pallas kernels  18.1 us (10%)
  other arithmetic  2.26 us (1%)
    ppermute x17, waiting for transfers between devices, permuted(): return lax.ppermute(block, axis, [(i, target(i)) for i in range(count)])  67.2 us
    ppermute x2, waiting for transfers between devices, halos(): lax.ppermute(lax.ppermute(block, 'domain', out), 'domain', back)  32.4 us
    ppermute x17, starting transfers between devices, permuted(): return lax.ppermute(block, axis, [(i, target(i)) for i in range(count)])  24.4 us
    ppermute x1, starting transfers between devices, halos(): seams = [lax.ppermute(blocks[0], 'domain', seam_pairs())]  10.9 us
    ppermute x2, waiting for transfers between devices, halos(): lax.ppermute(block, 'domain', out)  10.8 us
    pallas_call x1, Pallas kernels, filtered_stripes(): pl.pallas_call(functools.partial(filter_kernel, SHARES, stripes), out_sha...  6.63 us
    ppermute x1, starting transfers between devices, halos(): low = lax.ppermute(both[:, planes - DEPTH:], 'domain', inner_pairs(1))  4.65 us
    pallas_call x1, Pallas kernels, rotated(): pl.pallas_call(functools.partial(rotate_kernel, cells), out_shape=jax.Sha...  4.19 us
  transfers between devices with their start and end apart: 24, of which 20 were waited for; matrix products, arithmetic and copies ran while one was open for 0% of the time, Pallas kernels for 0%

profile of v6, /device:TPU:32, one launch (start us, length us, event | category | flops | bytes accessed | tf_op | source)
XLA Modules:
  0.0 178.6 jit_solution(1045954555130910674)
XLA Ops:
  0.0 0.0 copy-start
  0.0 1.6 slice_select_fusion
  1.6 0.4 copy-done
  2.1 0.0 copy-start.1
  2.1 0.1 slice_select_fusion.1
  2.1 0.8 copy-done.1
  3.0 0.1 pad_maximum_fusion.1
  3.1 0.4 pad_maximum_fusion
  3.5 1.3 collective-permute-start.1
  4.8 4.7 %collective-permute-start = (f32[17,3,64,128]{3,2,1,0:T(8,128)S(1)}, f32[17,3,64,128]{3,2,1,0:T(8,128)S(1)}, u32[]{:S(2)}, u32[]{:S(2)}) collective-permute-start(f32[17,3,64,128]{3,2,1,0:T(8,128)S(1)} %get-tuple-element.30), channel_id=1, source_target_pairs={{0,8},{8,16},{16,24},{24,32},{32,40},{40,48},{48,56},{56,64},{64,7... | collective-permute-start | bytes 5013512 | tf_op jit(solution)/shard_map/ppermute | solution.py:140
  9.4 10.9 %collective-permute-start.2 = (f32[9,3,64,128]{3,2,1,0:T(8,128)S(1)}, f32[9,3,64,128]{3,2,1,0:T(8,128)S(1)}, u32[]{:S(2)}, u32[]{:S(2)}) collective-permute-start(f32[9,3,64,128]{3,2,1,0:T(8,128)S(1)} %pad_maximum_fusion.1), channel_id=1, source_target_pairs={{120,128},{0,248},{248,0},{128,120},{121,129},{1,249},{249,1},{129... | collective-permute-start | bytes 2654216 | tf_op jit(solution)/shard_map/ppermute | solution.py:134
  20.4 1.3 collective-permute-start.5
  21.7 1.3 collective-permute-start.3
  23.0 6.7 %collective-permute-done.5 = f32[4,3,64,128]{3,2,1,0:T(8,128)S(1)} collective-permute-done((f32[4,3,64,128]{3,2,1,0:T(8,128)S(1)}, f32[4,3,64,128]{3,2,1,0:T(8,128)S(1)}, u32[]{:S(2)}, u32[]{:S(2)}) %collective-permute-start.5) | collective-permute-done | bytes 393248 | tf_op jit(solution)/shard_map/ppermute | solution.py:137
  29.8 1.3 collective-permute-start.6
  31.1 4.0 %collective-permute-done.3 = f32[4,3,64,128]{3,2,1,0:T(8,128)S(1)} collective-permute-done((f32[4,3,64,128]{3,2,1,0:T(8,128)S(1)}, f32[4,3,64,128]{3,2,1,0:T(8,128)S(1)}, u32[]{:S(2)}, u32[]{:S(2)}) %collective-permute-start.3) | collective-permute-done | bytes 393248 | tf_op jit(solution)/shard_map/ppermute | solution.py:137
  35.1 1.3 collective-permute-start.4
  36.4 31.9 %collective-permute-done.6.rest_2_ = f32[4,3,64,128]{3,2,1,0:T(8,128)S(1)} collective-permute-done((f32[4,3,64,128]{3,2,1,0:T(8,128)S(1)}, f32[4,3,64,128]{3,2,1,0:T(8,128)S(1)}, u32[]{:S(2)}, u32[]{:S(2)}) %collective-permute-start.6) | collective-permute-done | bytes 393248 | tf_op jit(solution)/shard_map/ppermute | solution.py:137
  68.3 0.4 collective-permute-done.4.rest_1_
  68.7 0.0 collective-permute-done.2.rest_0_
  68.8 0.0 collective-permute-done.1.high
  68.8 0.0 collective-permute-done.low
  68.8 6.6 %shard_map.28 = (f32[16,4,8,128]{3,2,1,0:T(8,128)S(1)}, f32[16,4,8,128]{3,2,1,0:T(8,128)S(1)}, f32[16,4,8,128]{3,2,1,0:T(8,128)S(1)}, f32[16,4,8,128]{3,2,1,0:T(...) custom-call(f32[16,4,64,128]{3,2,1,0:T(8,128)S(1)} %copy-done, ...), custom_call_target="tpu_custom_call" | custom-call | tf_op jit(solution)/shard_map/pallas_call | solution.py:80
  75.4 0.1 collective-permute-start.7
  75.5 5.4 %collective-permute-start.8 = (f32[16,4,8,128]{3,2,1,0:T(8,128)S(1)}, f32[16,4,8,128]{3,2,1,0:T(8,128)S(1)}, u32[]{:S(2)}, u32[]{:S(2)}) collective-permute-start(f32[16,4,8,128]{3,2,1,0:T(8,128)S(1)} %get-tuple-element.21), channel_id=1, source_target_pairs={{0,2},{1,3},{2,0},{3,1},{4,6},{5,7},{6,4},{7,5},{8,10},{9,11},{10,... | collective-permute-start | bytes 786440 | tf_op jit(solution)/shard_map/ppermute | solution.py:21
  80.9 0.1 collective-permute-start.9
  81.0 7.1 %collective-permute-start.10 = (f32[16,4,8,128]{3,2,1,0:T(8,128)S(1)}, f32[16,4,8,128]{3,2,1,0:T(8,128)S(1)}, u32[]{:S(2)}, u32[]{:S(2)}) collective-permute-start(f32[16,4,8,128]{3,2,1,0:T(8,128)S(1)} %get-tuple-element.23), channel_id=1, source_target_pairs={{0,4},{1,5},{2,6},{3,7},{4,0},{5,1},{6,2},{7,3},{8,12},{9,13},{10,... | collective-permute-start | bytes 786440 | tf_op jit(solution)/shard_map/ppermute | solution.py:21
  88.1 0.0 collective-permute-start.11
  88.1 0.0 collective-permute-done.7
  88.1 1.2 collective-permute-start.12
  89.3 8.9 %collective-permute-done.8 = f32[16,4,8,128]{3,2,1,0:T(8,128)S(1)} collective-permute-done((f32[16,4,8,128]{3,2,1,0:T(8,128)S(1)}, f32[16,4,8,128]{3,2,1,0:T(8,128)S(1)}, u32[]{:S(2)}, u32[]{:S(2)}) %collective-permute-start.8) | collective-permute-done | bytes 262176 | tf_op jit(solution)/shard_map/ppermute | solution.py:21
  98.2 0.0 collective-permute-start.13
  98.2 5.4 %collective-permute-done.9 = f32[16,4,8,128]{3,2,1,0:T(8,128)S(1)} collective-permute-done((f32[16,4,8,128]{3,2,1,0:T(8,128)S(1)}, f32[16,4,8,128]{3,2,1,0:T(8,128)S(1)}, u32[]{:S(2)}, u32[]{:S(2)}) %collective-permute-start.9) | collective-permute-done | bytes 262176 | tf_op jit(solution)/shard_map/ppermute | solution.py:21
  103.5 13.7 %collective-permute-done.10 = f32[16,4,8,128]{3,2,1,0:T(8,128)S(1)} collective-permute-done((f32[16,4,8,128]{3,2,1,0:T(8,128)S(1)}, f32[16,4,8,128]{3,2,1,0:T(8,128)S(1)}, u32[]{:S(2)}, u32[]{:S(2)}) %collective-permute-start.10) | collective-permute-done | bytes 262176 | tf_op jit(solution)/shard_map/ppermute | solution.py:21
  117.3 5.6 %collective-permute-done.11 = f32[16,4,8,128]{3,2,1,0:T(8,128)S(1)} collective-permute-done((f32[16,4,8,128]{3,2,1,0:T(8,128)S(1)}, f32[16,4,8,128]{3,2,1,0:T(8,128)S(1)}, u32[]{:S(2)}, u32[]{:S(2)}) %collective-permute-start.11) | collective-permute-done | bytes 262176 | tf_op jit(solution)/shard_map/ppermute | solution.py:21
  122.9 5.6 %collective-permute-done.12 = f32[16,4,8,128]{3,2,1,0:T(8,128)S(1)} collective-permute-done((f32[16,4,8,128]{3,2,1,0:T(8,128)S(1)}, f32[16,4,8,128]{3,2,1,0:T(8,128)S(1)}, u32[]{:S(2)}, u32[]{:S(2)}) %collective-permute-start.12) | collective-permute-done | bytes 262176 | tf_op jit(solution)/shard_map/ppermute | solution.py:21
  128.5 5.0 %collective-permute-done.13 = f32[16,4,8,128]{3,2,1,0:T(8,128)S(1)} collective-permute-done((f32[16,4,8,128]{3,2,1,0:T(8,128)S(1)}, f32[16,4,8,128]{3,2,1,0:T(8,128)S(1)}, u32[]{:S(2)}, u32[]{:S(2)}) %collective-permute-start.13) | collective-permute-done | bytes 262176 | tf_op jit(solution)/shard_map/ppermute | solution.py:21
  133.5 3.1 %shard_map.29 = (f32[128,4096]{1,0:T(8,128)S(1)}, f32[128,128]{1,0:T(8,128)S(1)}) custom-call(f32[512,128]{1,0:T(8,128)S(1)} %bitcast.13, f32[512,128]{1,0:T(8,128)S(1)} %bitcast.14, f32[512,128]{1,0:T(8,128)S(1)} %bitcast.15, f32[512,128]{1,0:T(8,128)S(1)} %bitcast.16, f32[512,128]{1,0:T(8,128)S(1)} %bitcast.17, f32[512,128]{1,0:T(8,128)S(1)} %bitcast.18, ...), custom_call_target="tpu_custom_call" | custom-call | tf_op jit(solution)/shard_map/pallas_call | solution.py:171
  136.6 0.1 collective-permute-start.14
  136.7 1.2 collective-permute-done.14
  138.0 0.1 collective-permute-start.15
  138.1 4.3 %collective-permute-done.15 = f32[128,128]{1,0:T(8,128)S(1)} collective-permute-done((f32[128,128]{1,0:T(8,128)S(1)}, f32[128,128]{1,0:T(8,128)S(1)}, u32[]{:S(2)}, u32[]{:S(2)}) %collective-permute-start.15) | collective-permute-done | bytes 65568 | tf_op jit(solution)/shard_map/ppermute | solution.py:21
  142.4 1.8 %collective-permute-start.16 = (f32[128,128]{1,0:T(8,128)S(1)}, f32[128,128]{1,0:T(8,128)S(1)}, u32[]{:S(2)}, u32[]{:S(2)}) collective-permute-start(f32[128,128]{1,0:T(8,128)S(1)} %add.31), channel_id=1, source_target_pairs={{0,4},{1,5},{2,6},{3,7},{4,0},{5,1},{6,2},{7,3},{8,12},{9,13},{10,... | collective-permute-start | bytes 196616 | tf_op jit(solution)/shard_map/ppermute | solution.py:21
  144.2 3.5 %collective-permute-done.16 = f32[128,128]{1,0:T(8,128)S(1)} collective-permute-done((f32[128,128]{1,0:T(8,128)S(1)}, f32[128,128]{1,0:T(8,128)S(1)}, u32[]{:S(2)}, u32[]{:S(2)}) %collective-permute-start.16) | collective-permute-done | bytes 65568 | tf_op jit(solution)/shard_map/ppermute | solution.py:21
  147.7 0.3 collective-permute-start.19
  148.0 0.1 collective-permute-start.18
  148.1 1.9 %collective-permute-start.17 = (f32[128,128]{1,0:T(8,128)S(1)}, f32[128,128]{1,0:T(8,128)S(1)}, u32[]{:S(2)}, u32[]{:S(2)}) collective-permute-start(f32[128,128]{1,0:T(8,128)S(1)} %add.32), channel_id=1, source_target_pairs={{0,8},{8,16},{16,24},{24,0},{32,40},{40,48},{48,56},{56,32},{64,72... | collective-permute-start | bytes 196616 | tf_op jit(solution)/shard_map/ppermute | solution.py:21
  150.0 2.2 %collective-permute-done.19 = f32[128,128]{1,0:T(8,128)S(1)} collective-permute-done((f32[128,128]{1,0:T(8,128)S(1)}, f32[128,128]{1,0:T(8,128)S(1)}, u32[]{:S(2)}, u32[]{:S(2)}) %collective-permute-start.19) | collective-permute-done | bytes 65568 | tf_op jit(solution)/shard_map/ppermute | solution.py:21
  152.2 1.6 collective-permute-done.18
  153.8 1.1 collective-permute-done.17
  154.9 0.1 collective-permute-start.22
  155.0 0.1 collective-permute-start.21
  155.1 1.9 %collective-permute-start.20 = (f32[128,128]{1,0:T(8,128)S(1)}, f32[128,128]{1,0:T(8,128)S(1)}, u32[]{:S(2)}, u32[]{:S(2)}) collective-permute-start(f32[128,128]{1,0:T(8,128)S(1)} %add_add_fusion.1), channel_id=1, source_target_pairs={{0,32},{8,40},{16,48},{24,56},{32,64},{40,72},{48,80},{56,88},{64,... | collective-permute-start | bytes 196616 | tf_op jit(solution)/shard_map/ppermute | solution.py:21
  157.0 2.2 %collective-permute-done.22 = f32[128,128]{1,0:T(8,128)S(1)} collective-permute-done((f32[128,128]{1,0:T(8,128)S(1)}, f32[128,128]{1,0:T(8,128)S(1)}, u32[]{:S(2)}, u32[]{:S(2)}) %collective-permute-start.22) | collective-permute-done | bytes 65568 | tf_op jit(solution)/shard_map/ppermute | solution.py:21
  159.3 1.6 collective-permute-done.21
  160.9 1.1 collective-permute-done.20
  162.0 4.0 %collective-permute-start.23 = (f32[128,128]{1,0:T(8,128)S(1)}, f32[128,128]{1,0:T(8,128)S(1)}, u32[]{:S(2)}, u32[]{:S(2)}) collective-permute-start(f32[128,128]{1,0:T(8,128)S(1)} %add_add_fusion), channel_id=1, source_target_pairs={{0,128},{8,136},{16,144},{24,152},{32,160},{40,168},{48,176},{56,1... | collective-permute-start | bytes 196616 | tf_op jit(solution)/shard_map/ppermute | solution.py:21
  166.0 4.2 %collective-permute-done.23 = f32[128,128]{1,0:T(8,128)S(1)} collective-permute-done((f32[128,128]{1,0:T(8,128)S(1)}, f32[128,128]{1,0:T(8,128)S(1)}, u32[]{:S(2)}, u32[]{:S(2)}) %collective-permute-start.23) | collective-permute-done | bytes 65568 | tf_op jit(solution)/shard_map/ppermute | solution.py:21
  170.2 4.2 %shard_map.30.inverse = f32[128,128]{1,0:T(8,128)S(1)} custom-call(f32[128,128]{1,0:T(8,128)S(1)} %add.39.gram), custom_call_target="tpu_custom_call" | custom-call | tf_op jit(solution)/shard_map/pallas_call | solution.py:224
  174.4 4.2 %shard_map.31 = f32[4096,128]{1,0:T(8,128)} custom-call(f32[128,128]{1,0:T(8,128)S(1)} %shard_map.30.inverse, f32[128,4096]{1,0:T(8,128)S(1)} %get-tuple-element.28.flat), custom_call_target="tpu_custom_call" | custom-call | tf_op jit(solution)/shard_map/pallas_call | solution.py:248
  (7 shorter events, 0.1 us)
Async XLA Ops:
  0.0 2.1 %copy-start = (f32[16,4,64,128]{3,2,1,0:T(8,128)S(1)}, f32[16,4,64,128]{3,2,1,0:T(8,128)}, u32[]{:S(2)}) copy-start(f32[16,4,64,128]{3,2,1,0:T(8,128)} %field.1) | copy-start | bytes 6291460
  2.1 0.9 copy-start.1
  3.5 65.3 %collective-permute-start.1 = (f32[17,3,64,128]{3,2,1,0:T(8,128)S(1)}, f32[17,3,64,128]{3,2,1,0:T(8,128)S(1)}, u32[]{:S(2)}, u32[]{:S(2)}) collective-permute-start(f32[17,3,64,128]{3,2,1,0:T(8,128)S(1)} %get-tuple-element.29), channel_id=1, source_target_pairs={{8,0},{16,8},{24,16},{32,24},{40,32},{48,40},{56,48},{64,56},{72,6... | collective-permute-start | bytes 5013512 | tf_op jit(solution)/shard_map/ppermute | solution.py:141
  4.8 64.0 %collective-permute-start = (f32[17,3,64,128]{3,2,1,0:T(8,128)S(1)}, f32[17,3,64,128]{3,2,1,0:T(8,128)S(1)}, u32[]{:S(2)}, u32[]{:S(2)}) collective-permute-start(f32[17,3,64,128]{3,2,1,0:T(8,128)S(1)} %get-tuple-element.30), channel_id=1, source_target_pairs={{0,8},{8,16},{16,24},{24,32},{32,40},{40,48},{48,56},{56,64},{64,7... | collective-permute-start | bytes 5013512 | tf_op jit(solution)/shard_map/ppermute | solution.py:140
  9.4 59.3 %collective-permute-start.2 = (f32[9,3,64,128]{3,2,1,0:T(8,128)S(1)}, f32[9,3,64,128]{3,2,1,0:T(8,128)S(1)}, u32[]{:S(2)}, u32[]{:S(2)}) collective-permute-start(f32[9,3,64,128]{3,2,1,0:T(8,128)S(1)} %pad_maximum_fusion.1), channel_id=1, source_target_pairs={{120,128},{0,248},{248,0},{128,120},{121,129},{1,249},{249,1},{129... | collective-permute-start | bytes 2654216 | tf_op jit(solution)/shard_map/ppermute | solution.py:134
  20.4 9.4 %collective-permute-start.5 = (f32[4,3,64,128]{3,2,1,0:T(8,128)S(1)}, f32[4,3,64,128]{3,2,1,0:T(8,128)S(1)}, u32[]{:S(2)}, u32[]{:S(2)}) collective-permute-start(f32[4,3,64,128]{3,2,1,0:T(8,128)S(1)} %get-tuple-element.31), channel_id=1, source_target_pairs={{120,88},{0,32},{248,216},{128,160},{121,89},{1,33},{249,217},{129... | collective-permute-start | bytes 1179656 | tf_op jit(solution)/shard_map/ppermute | solution.py:137
  21.7 13.4 %collective-permute-start.3 = (f32[4,3,64,128]{3,2,1,0:T(8,128)S(1)}, f32[4,3,64,128]{3,2,1,0:T(8,128)S(1)}, u32[]{:S(2)}, u32[]{:S(2)}) collective-permute-start(f32[4,3,64,128]{3,2,1,0:T(8,128)S(1)} %get-tuple-element.32), channel_id=1, source_target_pairs={{120,24},{0,96},{248,152},{128,224},{121,25},{1,97},{249,153},{129... | collective-permute-start | bytes 1179656 | tf_op jit(solution)/shard_map/ppermute | solution.py:137
  29.8 38.6 %collective-permute-start.6 = (f32[4,3,64,128]{3,2,1,0:T(8,128)S(1)}, f32[4,3,64,128]{3,2,1,0:T(8,128)S(1)}, u32[]{:S(2)}, u32[]{:S(2)}) collective-permute-start(f32[4,3,64,128]{3,2,1,0:T(8,128)S(1)} %collective-permute-done.5), channel_id=1, source_target_pairs={{88,128},{32,248},{216,0},{160,120},{89,129},{33,249},{217,1},{161... | collective-permute-start | bytes 1179656 | tf_op jit(solution)/shard_map/ppermute | solution.py:137
  35.1 33.6 %collective-permute-start.4 = (f32[4,3,64,128]{3,2,1,0:T(8,128)S(1)}, f32[4,3,64,128]{3,2,1,0:T(8,128)S(1)}, u32[]{:S(2)}, u32[]{:S(2)}) collective-permute-start(f32[4,3,64,128]{3,2,1,0:T(8,128)S(1)} %collective-permute-done.3), channel_id=1, source_target_pairs={{24,128},{96,248},{152,0},{224,120},{25,129},{97,249},{153,1},{225... | collective-permute-start | bytes 1179656 | tf_op jit(solution)/shard_map/ppermute | solution.py:137
  75.4 12.7 %collective-permute-start.7 = (f32[16,4,8,128]{3,2,1,0:T(8,128)S(1)}, f32[16,4,8,128]{3,2,1,0:T(8,128)S(1)}, u32[]{:S(2)}, u32[]{:S(2)}) collective-permute-start(f32[16,4,8,128]{3,2,1,0:T(8,128)S(1)} %get-tuple-element.20), channel_id=1, source_target_pairs={{0,1},{1,0},{2,3},{3,2},{4,5},{5,4},{6,7},{7,6},{8,9},{9,8},{10,11... | collective-permute-start | bytes 786440 | tf_op jit(solution)/shard_map/ppermute | solution.py:21
  75.5 22.7 %collective-permute-start.8 = (f32[16,4,8,128]{3,2,1,0:T(8,128)S(1)}, f32[16,4,8,128]{3,2,1,0:T(8,128)S(1)}, u32[]{:S(2)}, u32[]{:S(2)}) collective-permute-start(f32[16,4,8,128]{3,2,1,0:T(8,128)S(1)} %get-tuple-element.21), channel_id=1, source_target_pairs={{0,2},{1,3},{2,0},{3,1},{4,6},{5,7},{6,4},{7,5},{8,10},{9,11},{10,... | collective-permute-start | bytes 786440 | tf_op jit(solution)/shard_map/ppermute | solution.py:21
  80.9 22.6 %collective-permute-start.9 = (f32[16,4,8,128]{3,2,1,0:T(8,128)S(1)}, f32[16,4,8,128]{3,2,1,0:T(8,128)S(1)}, u32[]{:S(2)}, u32[]{:S(2)}) collective-permute-start(f32[16,4,8,128]{3,2,1,0:T(8,128)S(1)} %get-tuple-element.22), channel_id=1, source_target_pairs={{0,3},{1,2},{2,1},{3,0},{4,7},{5,6},{6,5},{7,4},{8,11},{9,10},{10,... | collective-permute-start | bytes 786440 | tf_op jit(solution)/shard_map/ppermute | solution.py:21
  81.0 36.3 %collective-permute-start.10 = (f32[16,4,8,128]{3,2,1,0:T(8,128)S(1)}, f32[16,4,8,128]{3,2,1,0:T(8,128)S(1)}, u32[]{:S(2)}, u32[]{:S(2)}) collective-permute-start(f32[16,4,8,128]{3,2,1,0:T(8,128)S(1)} %get-tuple-element.23), channel_id=1, source_target_pairs={{0,4},{1,5},{2,6},{3,7},{4,0},{5,1},{6,2},{7,3},{8,12},{9,13},{10,... | collective-permute-start | bytes 786440 | tf_op jit(solution)/shard_map/ppermute | solution.py:21
  88.1 34.8 %collective-permute-start.11 = (f32[16,4,8,128]{3,2,1,0:T(8,128)S(1)}, f32[16,4,8,128]{3,2,1,0:T(8,128)S(1)}, u32[]{:S(2)}, u32[]{:S(2)}) collective-permute-start(f32[16,4,8,128]{3,2,1,0:T(8,128)S(1)} %get-tuple-element.24), channel_id=1, source_target_pairs={{0,5},{1,4},{2,7},{3,6},{4,1},{5,0},{6,3},{7,2},{8,13},{9,12},{10,... | collective-permute-start | bytes 786440 | tf_op jit(solution)/shard_map/ppermute | solution.py:21
  88.1 40.4 %collective-permute-start.12 = (f32[16,4,8,128]{3,2,1,0:T(8,128)S(1)}, f32[16,4,8,128]{3,2,1,0:T(8,128)S(1)}, u32[]{:S(2)}, u32[]{:S(2)}) collective-permute-start(f32[16,4,8,128]{3,2,1,0:T(8,128)S(1)} %get-tuple-element.25), channel_id=1, source_target_pairs={{0,6},{1,7},{2,4},{3,5},{4,2},{5,3},{6,0},{7,1},{8,14},{9,15},{10,... | collective-permute-start | bytes 786440 | tf_op jit(solution)/shard_map/ppermute | solution.py:21
  98.2 35.4 %collective-permute-start.13 = (f32[16,4,8,128]{3,2,1,0:T(8,128)S(1)}, f32[16,4,8,128]{3,2,1,0:T(8,128)S(1)}, u32[]{:S(2)}, u32[]{:S(2)}) collective-permute-start(f32[16,4,8,128]{3,2,1,0:T(8,128)S(1)} %get-tuple-element.26), channel_id=1, source_target_pairs={{0,7},{1,6},{2,5},{3,4},{4,3},{5,2},{6,1},{7,0},{8,15},{9,14},{10,... | collective-permute-start | bytes 786440 | tf_op jit(solution)/shard_map/ppermute | solution.py:21
  136.6 1.3 collective-permute-start.14
  138.0 4.4 %collective-permute-start.15 = (f32[128,128]{1,0:T(8,128)S(1)}, f32[128,128]{1,0:T(8,128)S(1)}, u32[]{:S(2)}, u32[]{:S(2)}) collective-permute-start(f32[128,128]{1,0:T(8,128)S(1)} %add.30), channel_id=1, source_target_pairs={{0,2},{1,3},{2,0},{3,1},{4,6},{5,7},{6,4},{7,5},{8,10},{9,11},{10,... | collective-permute-start | bytes 196616 | tf_op jit(solution)/shard_map/ppermute | solution.py:21
  142.4 5.3 %collective-permute-start.16 = (f32[128,128]{1,0:T(8,128)S(1)}, f32[128,128]{1,0:T(8,128)S(1)}, u32[]{:S(2)}, u32[]{:S(2)}) collective-permute-start(f32[128,128]{1,0:T(8,128)S(1)} %add.31), channel_id=1, source_target_pairs={{0,4},{1,5},{2,6},{3,7},{4,0},{5,1},{6,2},{7,3},{8,12},{9,13},{10,... | collective-permute-start | bytes 196616 | tf_op jit(solution)/shard_map/ppermute | solution.py:21
  147.7 4.5 %collective-permute-start.19 = (f32[128,128]{1,0:T(8,128)S(1)}, f32[128,128]{1,0:T(8,128)S(1)}, u32[]{:S(2)}, u32[]{:S(2)}) collective-permute-start(f32[128,128]{1,0:T(8,128)S(1)} %add.32), channel_id=1, source_target_pairs={{0,24},{8,0},{16,8},{24,16},{32,56},{40,32},{48,40},{56,48},{64,88... | collective-permute-start | bytes 196616 | tf_op jit(solution)/shard_map/ppermute | solution.py:21
  148.0 5.9 %collective-permute-start.18 = (f32[128,128]{1,0:T(8,128)S(1)}, f32[128,128]{1,0:T(8,128)S(1)}, u32[]{:S(2)}, u32[]{:S(2)}) collective-permute-start(f32[128,128]{1,0:T(8,128)S(1)} %add.32), channel_id=1, source_target_pairs={{0,16},{8,24},{16,0},{24,8},{32,48},{40,56},{48,32},{56,40},{64,80... | collective-permute-start | bytes 196616 | tf_op jit(solution)/shard_map/ppermute | solution.py:21
  148.1 6.8 %collective-permute-start.17 = (f32[128,128]{1,0:T(8,128)S(1)}, f32[128,128]{1,0:T(8,128)S(1)}, u32[]{:S(2)}, u32[]{:S(2)}) collective-permute-start(f32[128,128]{1,0:T(8,128)S(1)} %add.32), channel_id=1, source_target_pairs={{0,8},{8,16},{16,24},{24,0},{32,40},{40,48},{48,56},{56,32},{64,72... | collective-permute-start | bytes 196616 | tf_op jit(solution)/shard_map/ppermute | solution.py:21
  154.9 4.3 %collective-permute-start.22 = (f32[128,128]{1,0:T(8,128)S(1)}, f32[128,128]{1,0:T(8,128)S(1)}, u32[]{:S(2)}, u32[]{:S(2)}) collective-permute-start(f32[128,128]{1,0:T(8,128)S(1)} %add_add_fusion.1), channel_id=1, source_target_pairs={{0,96},{8,104},{16,112},{24,120},{32,0},{40,8},{48,16},{56,24},{64... | collective-permute-start | bytes 196616 | tf_op jit(solution)/shard_map/ppermute | solution.py:21
  155.0 5.9 %collective-permute-start.21 = (f32[128,128]{1,0:T(8,128)S(1)}, f32[128,128]{1,0:T(8,128)S(1)}, u32[]{:S(2)}, u32[]{:S(2)}) collective-permute-start(f32[128,128]{1,0:T(8,128)S(1)} %add_add_fusion.1), channel_id=1, source_target_pairs={{0,64},{8,72},{16,80},{24,88},{32,96},{40,104},{48,112},{56,120},{... | collective-permute-start | bytes 196616 | tf_op jit(solution)/shard_map/ppermute | solution.py:21
  155.1 6.8 %collective-permute-start.20 = (f32[128,128]{1,0:T(8,128)S(1)}, f32[128,128]{1,0:T(8,128)S(1)}, u32[]{:S(2)}, u32[]{:S(2)}) collective-permute-start(f32[128,128]{1,0:T(8,128)S(1)} %add_add_fusion.1), channel_id=1, source_target_pairs={{0,32},{8,40},{16,48},{24,56},{32,64},{40,72},{48,80},{56,88},{64,... | collective-permute-start | bytes 196616 | tf_op jit(solution)/shard_map/ppermute | solution.py:21
  162.0 8.3 %collective-permute-start.23 = (f32[128,128]{1,0:T(8,128)S(1)}, f32[128,128]{1,0:T(8,128)S(1)}, u32[]{:S(2)}, u32[]{:S(2)}) collective-permute-start(f32[128,128]{1,0:T(8,128)S(1)} %add_add_fusion), channel_id=1, source_target_pairs={{0,128},{8,136},{16,144},{24,152},{32,160},{40,168},{48,176},{56,1... | collective-permute-start | bytes 196616 | tf_op jit(solution)/shard_map/ppermute | solution.py:21

commit v7 on v6

--- a/solution.py
+++ b/solution.py
@@ -9,7 +9,8 @@
 from jax.sharding import PartitionSpec as P
 
 DEPTH = 3
-PARTS = 1
+TIED = True
+EARLY = (7, 6, 5)
 PANEL = 32
 SIDE = 4
 SHARES = (8, 4, 4)
@@ -27,27 +28,26 @@
     return beside + pltpu.roll(plane, 1, 1) + pltpu.roll(plane, lanes - 1, 1)
 
 
-def filter_kernel(shares, stripes, field, pot, low, high, *rest):
+def filter_kernel(begin, shares, stripes, field, pot, pot_low, pot_high, pot_seam, low, high, *rest):
     routes = len(shares)
     seams, outs = rest[:routes], rest[routes : routes + stripes]
     zero, one, two, three, local = rest[routes + stripes :]
     me = lax.axis_index("band")
     at = lax.rem(lax.axis_index("domain"), SIDE * SIDE)
     at_low, at_high = at == 0, at == SIDE * SIDE - 1
-    count, planes = field.shape[:2]
+    planes = field.shape[1]
     top = planes + 2 * DEPTH
     width = outs[0].shape[2]
     own = pl.ds(DEPTH, planes)
-    seam = seams[0][shares[0]]
     local[own] = 0.8 * pot[...] - 1.2
-    local[:DEPTH] = 0.8 * jnp.where(at_low, seam, low[count]) - 1.2
-    local[planes + DEPTH :] = 0.8 * jnp.where(at_high, seam, high[count]) - 1.2
+    local[:DEPTH] = 0.8 * jnp.where(at_low, pot_seam[...], pot_low[...]) - 1.2
+    local[planes + DEPTH :] = 0.8 * jnp.where(at_high, pot_seam[...], pot_high[...]) - 1.2
 
     def one_orbital(orbital, seam_plane):
         zero[own] = field[orbital]
         for k in range(DEPTH):
-            zero[k] = jnp.where(at_low, seam_plane(k), low[orbital, k])
-            zero[planes + DEPTH + k] = jnp.where(at_high, seam_plane(k), high[orbital, k])
+            zero[k] = jnp.where(at_low, seam_plane(k), low[begin + orbital, k])
+            zero[planes + DEPTH + k] = jnp.where(at_high, seam_plane(k), high[begin + orbital, k])
         for k in range(1, top - 1):
             beside = zero[k - 1] + zero[k + 1] + neighbours(zero[k])
             one[k] = (0.5 * local[k]) * zero[k] - 0.2 * beside
@@ -72,13 +72,14 @@
         first += share
 
 
-def filtered_stripes(field, pot, low, high, seams, stripes):
+def filtered_stripes(field, pots, low, high, begin, seams, stripes):
     count, planes, rows, lanes = field.shape
     width = rows // stripes
     top = planes + 2 * DEPTH
+    shares = [min(seam.shape[0], count) for seam in seams]
     shape = jax.ShapeDtypeStruct((count, planes, width, lanes), jnp.float32)
     return pl.pallas_call(
-        functools.partial(filter_kernel, SHARES, stripes),
+        functools.partial(filter_kernel, begin, shares, stripes),
         out_shape=[shape] * stripes,
         scratch_shapes=[
             pltpu.VMEM((top, rows, lanes), jnp.float32),
@@ -88,7 +89,7 @@
             pltpu.VMEM((top, rows, lanes), jnp.float32),
         ],
         compiler_params=pltpu.CompilerParams(vmem_limit_bytes=40 * 1024 * 1024),
-    )(field, pot, low, high, *seams)
+    )(field, *pots, low, high, *seams)
 
 
 def inner_pairs(step):
@@ -143,7 +144,7 @@
 
 
 def gram_kernel(pieces, cells, *rest):
-    refs, (flat, gram) = rest[:-2], rest[-2:]
+    refs, (flat, own, other, gram) = rest[:-4], rest[-4:]
     me = lax.axis_index("band")
     lanes = refs[0].shape[1]
     share = refs[0].shape[0] // cells
@@ -161,6 +162,10 @@
         precision=lax.Precision.HIGHEST,
         preferred_element_type=jnp.float32,
     )
+    half = gram.shape[0] // 2
+    core = lax.rem(lax.axis_index("band"), 2)
+    own[...] = gram[pl.ds(pl.multiple_of(core * half, half), half)]
+    other[...] = gram[pl.ds(pl.multiple_of((1 - core) * half, half), half)]
 
 
 def flat_and_gram(slots, orbitals):
@@ -172,17 +177,21 @@
         functools.partial(gram_kernel, pieces, cells),
         out_shape=[
             jax.ShapeDtypeStruct((orbitals, cells * lanes), jnp.float32),
-            jax.ShapeDtypeStruct((orbitals, orbitals), jnp.float32),
+            jax.ShapeDtypeStruct((orbitals // 2, orbitals), jnp.float32),
+            jax.ShapeDtypeStruct((orbitals // 2, orbitals), jnp.float32),
         ],
+        scratch_shapes=[pltpu.VMEM((orbitals, orbitals), jnp.float32)],
         compiler_params=pltpu.CompilerParams(vmem_limit_bytes=32 * 1024 * 1024),
     )(*refs)
 
 
-def factor_kernel(panel, scale, gram, out, left, right):
-    orbitals = gram.shape[0]
+def factor_kernel(panel, scale, own, other, out, left, right):
+    half, orbitals = own.shape
+    core = lax.rem(lax.axis_index("band"), 2)
     row = lax.broadcasted_iota(jnp.int32, (orbitals, orbitals), 0)
     lane = lax.broadcasted_iota(jnp.int32, (orbitals, orbitals), 1)
-    left[...] = gram[...]
+    left[pl.ds(pl.multiple_of(core * half, half), half)] = own[...]
+    left[pl.ds(pl.multiple_of((1 - core) * half, half), half)] = other[...]
     right[...] = jnp.where(row == lane, scale, 0.0)
     inner = lax.broadcasted_iota(jnp.int32, (panel, orbitals), 0)
     for start in range(0, orbitals, panel):
@@ -219,14 +228,14 @@
                 ref[stop:] = ref[stop:] - update[stop:]
 
 
-def scaled_inverse(gram, scale):
-    orbitals = gram.shape[0]
+def scaled_inverse(own, other, scale):
+    orbitals = own.shape[1]
     return pl.pallas_call(
         functools.partial(factor_kernel, PANEL, scale),
-        out_shape=jax.ShapeDtypeStruct(gram.shape, jnp.float32),
+        out_shape=jax.ShapeDtypeStruct((orbitals, orbitals), jnp.float32),
         scratch_shapes=[pltpu.VMEM((orbitals, orbitals), jnp.float32)] * 2,
         compiler_params=pltpu.CompilerParams(vmem_limit_bytes=32 * 1024 * 1024),
-    )(gram)
+    )(own, other)
 
 
 def rotate_kernel(cells, inverse, flat, out):
@@ -252,21 +261,30 @@
     )(inverse, flat)
 
 
-def summed(gram):
-    for bit in (1, 2, 4):
-        gram = gram + permuted(gram, "band", lambda i: i ^ bit)
-    side = SIDE
-    turned = [
-        permuted(gram, "domain", lambda i: i // side * side + (i + k) % side) for k in (1, 2, 3)
-    ]
-    gram = (gram + turned[0]) + (turned[1] + turned[2])
-    plane = side * side
-    turned = [
-        permuted(gram, "domain", lambda i: i // plane * plane + (i + k * side) % plane)
-        for k in (1, 2, 3)
-    ]
-    gram = (gram + turned[0]) + (turned[1] + turned[2])
-    return gram + permuted(gram, "domain", lambda i: i ^ plane)
+def summed(own, other):
+    bands, half = lax.axis_size("band"), SIDE * SIDE
+    depth = lax.axis_size("domain") // half * bands // 2
+
+    def along_z(block, step):
+        pairs = []
+        for domain in range(lax.axis_size("domain")):
+            for band in range(bands):
+                z = (domain // half * (bands // 2) + band // 2 + step) % depth
+                there = z // (bands // 2) * half + domain % half
+                pairs.append((domain * bands + band, there * bands + z % (bands // 2) * 2 + band % 2))
+        return lax.ppermute(block, ("domain", "band"), pairs)
+
+    def turned(block, target):
+        parts = [permuted(block, "domain", lambda i: target(i, k)) for k in (1, 2, 3)]
+        return (block + parts[0]) + (parts[1] + parts[2])
+
+    own = own + permuted(other, "band", lambda i: i ^ 1)
+    own = own + permuted(own, "band", lambda i: i ^ 2)
+    parts = [along_z(own, step) for step in (2, -2, 4)]
+    own = (own + parts[2]) + (parts[0] + parts[1])
+    own = turned(own, lambda i, k: i // SIDE * SIDE + (i + k) % SIDE)
+    own = turned(own, lambda i, k: i // half * half + (i + k * SIDE) % half)
+    return own, permuted(own, "band", lambda i: i ^ 1)
 
 
 def body(orbitals, potential):
@@ -275,20 +293,26 @@
     orb_total = own * stripes
     cell_total = planes * lax.axis_size("domain") * ny_all * nx_all
 
-    share = own // PARTS
-    pieces = []
-    for part in range(PARTS):
-        field = orbitals[part * share : (part + 1) * share]
-        low, high, seams = halos(field, potential)
-        slots = filtered_stripes(field, potential, low, high, seams, stripes)
-        pieces.append(
-            [slots[0]]
-            + [permuted(slots[k], "band", lambda i: i ^ k) for k in range(1, stripes)]
-        )
-    slots = [[piece[k] for piece in pieces] for k in range(stripes)]
-    flat, partial_gram = flat_and_gram(slots, orb_total)
-    gram = summed(partial_gram)
-    inverse = scaled_inverse(gram, math.sqrt(cell_total))
+    cut = SHARES[0]
+    low, high, (seam, *others) = halos(orbitals, potential)
+    pots = (potential, low[own], high[own], seam[cut])
+
+    def sent(slots, chosen):
+        return [permuted(slots[k], "band", lambda i: i ^ k) for k in chosen]
+
+    slots = filtered_stripes(orbitals[:cut], pots, low, high, 0, [seam], stripes)
+    early = sent(slots, EARLY)
+    count = len(others)
+    if TIED:
+        tied = lax.optimization_barrier((*others, *early))
+        others, early = tied[:count], list(tied[count:])
+    rest = [k for k in range(1, stripes) if k not in EARLY]
+    first = dict(zip([0, *EARLY, *rest], [slots[0], *early, *sent(slots, rest)]))
+    slots = filtered_stripes(orbitals[cut:], pots, low, high, cut, others, stripes)
+    second = [slots[0], *sent(slots, range(1, stripes))]
+    slots = [[first[k], second[k]] for k in range(stripes)]
+    flat, own_half, other_half = flat_and_gram(slots, orb_total)
+    inverse = scaled_inverse(*summed(own_half, other_half), math.sqrt(cell_total))
     return rotated(inverse, flat, nx_all).reshape(
         orb_total, planes, ny_all // stripes, nx_all
     )

time: 180 us -> 173 us (0.961)
  waiting for transfers between devices: 110 us -> 89 us
  starting transfers between devices: 46.4 us -> 59 us
    ppermute x1, waiting for transfers between devices: 0.01 us -> 32.7 us  [halos(): seams = [lax.ppermute(blocks[0], 'domain', seam_pairs())]]
    ppermute x2, waiting for transfers between devices: 32.4 us -> 0.01 us  [halos(): lax.ppermute(lax.ppermute(block, 'domain', out), 'domain', back)]
    ppermute x17 -> x23, waiting for transfers between devices: 67.2 us -> 40.9 us  [permuted(): return lax.ppermute(block, axis, [(i, target(i)) for i in range(count)])]
    ppermute x17 -> x23, starting transfers between devices: 24.4 us -> 32.3 us  [permuted(): return lax.ppermute(block, axis, [(i, target(i)) for i in range(count)])]
    ppermute x0 -> x3, starting transfers between devices: none -> 4.57 us  [along_z(): return lax.ppermute(block, ('domain', 'band'), pairs)]
    ppermute x0 -> x3, waiting for transfers between devices: none -> 4.15 us  [along_z(): return lax.ppermute(block, ('domain', 'band'), pairs)]
    pallas_call x1 -> x2, Pallas kernels: 6.63 us -> 6.72 us  [filtered_stripes(): pl.pallas_call(functools.partial(filter_kernel, begin, shares, stripes),...]
  transfers between devices with their start and end apart: 24 -> 33, of which waited for: 20 -> 20; matrix products, arithmetic and copies ran while one was open for 0% -> 0% of each run, Pallas kernels for 0% -> 4%
where the time goes in v7:
time: 173 us; the launch traced here: 170 us
  waiting for transfers between devices  89 us (51%)
  starting transfers between devices  59 us (34%)
  Pallas kernels  18.2 us (11%)
  other arithmetic  2.23 us (1%)
    ppermute x23, waiting for transfers between devices, permuted(): return lax.ppermute(block, axis, [(i, target(i)) for i in range(count)])  40.9 us
    ppermute x1, waiting for transfers between devices, halos(): seams = [lax.ppermute(blocks[0], 'domain', seam_pairs())]  32.7 us
    ppermute x23, starting transfers between devices, permuted(): return lax.ppermute(block, axis, [(i, target(i)) for i in range(count)])  32.3 us
    ppermute x2, waiting for transfers between devices, halos(): lax.ppermute(block, 'domain', out)  11.2 us
    ppermute x1, starting transfers between devices, halos(): seams = [lax.ppermute(blocks[0], 'domain', seam_pairs())]  10.9 us
    pallas_call x2, Pallas kernels, filtered_stripes(): pl.pallas_call(functools.partial(filter_kernel, begin, shares, stripes),...  6.72 us
    ppermute x1, starting transfers between devices, halos(): low = lax.ppermute(both[:, planes - DEPTH:], 'domain', inner_pairs(1))  4.65 us
    ppermute x3, starting transfers between devices, along_z(): return lax.ppermute(block, ('domain', 'band'), pairs)  4.57 us
  transfers between devices with their start and end apart: 33, of which 20 were waited for; matrix products, arithmetic and copies ran while one was open for 0% of the time, Pallas kernels for 4%

profile of v7, /device:TPU:32, one launch (start us, length us, event | category | flops | bytes accessed | tf_op | source)
XLA Modules:
  0.0 170.1 jit_solution(9863696071083457938)
XLA Ops:
  0.0 1.6 slice_select_fusion
  1.6 0.4 copy-done.1
  2.1 0.1 slice_select_fusion.1
  2.1 0.8 copy-done
  3.0 0.1 pad_maximum_fusion.1
  3.1 0.4 pad_maximum_fusion
  3.5 1.3 collective-permute-start.1
  4.8 4.7 %collective-permute-start = (f32[17,3,64,128]{3,2,1,0:T(8,128)S(1)}, f32[17,3,64,128]{3,2,1,0:T(8,128)S(1)}, u32[]{:S(2)}, u32[]{:S(2)}) collective-permute-start(f32[17,3,64,128]{3,2,1,0:T(8,128)S(1)} %get-tuple-element.58), channel_id=1, source_target_pairs={{0,8},{8,16},{16,24},{24,32},{32,40},{40,48},{48,56},{56,64},{64,7... | collective-permute-start | bytes 5013512 | tf_op jit(solution)/shard_map/ppermute | solution.py:141
  9.4 10.9 %collective-permute-start.2 = (f32[9,3,64,128]{3,2,1,0:T(8,128)S(1)}, f32[9,3,64,128]{3,2,1,0:T(8,128)S(1)}, u32[]{:S(2)}, u32[]{:S(2)}) collective-permute-start(f32[9,3,64,128]{3,2,1,0:T(8,128)S(1)} %pad_maximum_fusion.1), channel_id=1, source_target_pairs={{120,128},{0,248},{248,0},{128,120},{121,129},{1,249},{249,1},{129... | collective-permute-start | bytes 2654216 | tf_op jit(solution)/shard_map/ppermute | solution.py:135
  20.4 1.3 collective-permute-start.3
  21.7 1.3 collective-permute-start.5
  23.0 0.1 fusion.1
  23.2 11.2 %collective-permute-done.3 = f32[4,3,64,128]{3,2,1,0:T(8,128)S(1)} collective-permute-done((f32[4,3,64,128]{3,2,1,0:T(8,128)S(1)}, f32[4,3,64,128]{3,2,1,0:T(8,128)S(1)}, u32[]{:S(2)}, u32[]{:S(2)}) %collective-permute-start.3) | collective-permute-done | bytes 393248 | tf_op jit(solution)/shard_map/ppermute | solution.py:138
  34.4 1.3 collective-permute-start.4
  35.7 0.0 collective-permute-done.5
  35.7 1.3 collective-permute-start.6
  37.0 32.7 %collective-permute-done.2.rest_0_ = f32[9,3,64,128]{3,2,1,0:T(8,128)S(1)} collective-permute-done((f32[9,3,64,128]{3,2,1,0:T(8,128)S(1)}, f32[9,3,64,128]{3,2,1,0:T(8,128)S(1)}, u32[]{:S(2)}, u32[]{:S(2)}) %collective-permute-start.2) | collective-permute-done | bytes 884768 | tf_op jit(solution)/shard_map/ppermute | solution.py:135
  69.7 0.0 collective-permute-done.1.high
  69.7 0.0 collective-permute-done.low
  69.8 3.4 %shard_map.28 = (f32[8,4,8,128]{3,2,1,0:T(8,128)S(1)}, f32[8,4,8,128]{3,2,1,0:T(8,128)S(1)}, f32[8,4,8,128]{3,2,1,0:T(8,128)S(1)}, f32[8,4,8,128]{3,2,1,0:T(8,12...) custom-call(f32[8,4,64,128]{3,2,1,0:T(8,128)S(1)} %get-tuple-element, ...), custom_call_target="tpu_custom_call" | custom-call | tf_op jit(solution)/shard_map/pallas_call | solution.py:81
  73.2 3.1 %collective-permute-start.7 = (f32[8,4,8,128]{3,2,1,0:T(8,128)S(1)}, f32[8,4,8,128]{3,2,1,0:T(8,128)S(1)}, u32[]{:S(2)}, u32[]{:S(2)}) collective-permute-start(f32[8,4,8,128]{3,2,1,0:T(8,128)S(1)} %get-tuple-element.34), channel_id=1, source_target_pairs={{0,7},{1,6},{2,5},{3,4},{4,3},{5,2},{6,1},{7,0},{8,15},{9,14},{10,... | collective-permute-start | bytes 393224 | tf_op jit(solution)/shard_map/ppermute | solution.py:22
  76.2 0.8 collective-permute-start.8
  77.0 12.2 %collective-permute-start.9 = (f32[8,4,8,128]{3,2,1,0:T(8,128)S(1)}, f32[8,4,8,128]{3,2,1,0:T(8,128)S(1)}, u32[]{:S(2)}, u32[]{:S(2)}) collective-permute-start(f32[8,4,8,128]{3,2,1,0:T(8,128)S(1)} %get-tuple-element.36), channel_id=1, source_target_pairs={{0,5},{1,4},{2,7},{3,6},{4,1},{5,0},{6,3},{7,2},{8,13},{9,12},{10,... | collective-permute-start | bytes 393224 | tf_op jit(solution)/shard_map/ppermute | solution.py:22
  89.2 0.9 collective-permute-start.16
  90.1 0.0 collective-permute-done.7
  90.1 0.0 collective-permute-start.10
  90.1 1.8 %collective-permute-start.12 = (f32[8,4,8,128]{3,2,1,0:T(8,128)S(1)}, f32[8,4,8,128]{3,2,1,0:T(8,128)S(1)}, u32[]{:S(2)}, u32[]{:S(2)}) collective-permute-start(f32[8,4,8,128]{3,2,1,0:T(8,128)S(1)} %get-tuple-element.42), channel_id=1, source_target_pairs={{0,2},{1,3},{2,0},{3,1},{4,6},{5,7},{6,4},{7,5},{8,10},{9,11},{10,... | collective-permute-start | bytes 393224 | tf_op jit(solution)/shard_map/ppermute | solution.py:22
  91.9 6.0 %collective-permute-done.9 = f32[8,4,8,128]{3,2,1,0:T(8,128)S(1)} collective-permute-done((f32[8,4,8,128]{3,2,1,0:T(8,128)S(1)}, f32[8,4,8,128]{3,2,1,0:T(8,128)S(1)}, u32[]{:S(2)}, u32[]{:S(2)}) %collective-permute-start.9) | collective-permute-done | bytes 131104 | tf_op jit(solution)/shard_map/ppermute | solution.py:22
  97.9 3.3 %shard_map.29 = (f32[8,4,8,128]{3,2,1,0:T(8,128)S(1)}, f32[8,4,8,128]{3,2,1,0:T(8,128)S(1)}, f32[8,4,8,128]{3,2,1,0:T(8,128)S(1)}, f32[8,4,8,128]{3,2,1,0:T(8,12...) custom-call(f32[8,4,64,128]{3,2,1,0:T(8,128)S(1)} %get-tuple-element, ...), custom_call_target="tpu_custom_call" | custom-call | tf_op jit(solution)/shard_map/pallas_call | solution.py:81
  101.2 2.4 %collective-permute-start.13 = (f32[8,4,8,128]{3,2,1,0:T(8,128)S(1)}, f32[8,4,8,128]{3,2,1,0:T(8,128)S(1)}, u32[]{:S(2)}, u32[]{:S(2)}) collective-permute-start(f32[8,4,8,128]{3,2,1,0:T(8,128)S(1)} %get-tuple-element.43), channel_id=1, source_target_pairs={{0,2},{1,3},{2,0},{3,1},{4,6},{5,7},{6,4},{7,5},{8,10},{9,11},{10,... | collective-permute-start | bytes 393224 | tf_op jit(solution)/shard_map/ppermute | solution.py:22
  103.6 2.6 %collective-permute-start.17 = (f32[8,4,8,128]{3,2,1,0:T(8,128)S(1)}, f32[8,4,8,128]{3,2,1,0:T(8,128)S(1)}, u32[]{:S(2)}, u32[]{:S(2)}) collective-permute-start(f32[8,4,8,128]{3,2,1,0:T(8,128)S(1)} %get-tuple-element.47), channel_id=1, source_target_pairs={{0,4},{1,5},{2,6},{3,7},{4,0},{5,1},{6,2},{7,3},{8,12},{9,13},{10,... | collective-permute-start | bytes 393224 | tf_op jit(solution)/shard_map/ppermute | solution.py:22
  106.2 0.3 collective-permute-start.18
  106.5 1.2 collective-permute-start.19
  107.7 2.8 %collective-permute-done.13 = f32[8,4,8,128]{3,2,1,0:T(8,128)S(1)} collective-permute-done((f32[8,4,8,128]{3,2,1,0:T(8,128)S(1)}, f32[8,4,8,128]{3,2,1,0:T(8,128)S(1)}, u32[]{:S(2)}, u32[]{:S(2)}) %collective-permute-start.13) | collective-permute-done | bytes 131104 | tf_op jit(solution)/shard_map/ppermute | solution.py:22
  110.5 2.4 %collective-permute-done.15 = f32[8,4,8,128]{3,2,1,0:T(8,128)S(1)} collective-permute-done((f32[8,4,8,128]{3,2,1,0:T(8,128)S(1)}, f32[8,4,8,128]{3,2,1,0:T(8,128)S(1)}, u32[]{:S(2)}, u32[]{:S(2)}) %collective-permute-start.15) | collective-permute-done | bytes 131104 | tf_op jit(solution)/shard_map/ppermute | solution.py:22
  112.9 0.0 collective-permute-start.11
  112.9 8.4 %collective-permute-done.17 = f32[8,4,8,128]{3,2,1,0:T(8,128)S(1)} collective-permute-done((f32[8,4,8,128]{3,2,1,0:T(8,128)S(1)}, f32[8,4,8,128]{3,2,1,0:T(8,128)S(1)}, u32[]{:S(2)}, u32[]{:S(2)}) %collective-permute-start.17) | collective-permute-done | bytes 131104 | tf_op jit(solution)/shard_map/ppermute | solution.py:22
  121.3 2.8 %collective-permute-done.18 = f32[8,4,8,128]{3,2,1,0:T(8,128)S(1)} collective-permute-done((f32[8,4,8,128]{3,2,1,0:T(8,128)S(1)}, f32[8,4,8,128]{3,2,1,0:T(8,128)S(1)}, u32[]{:S(2)}, u32[]{:S(2)}) %collective-permute-start.18) | collective-permute-done | bytes 131104 | tf_op jit(solution)/shard_map/ppermute | solution.py:22
  124.1 3.7 %collective-permute-done.19 = f32[8,4,8,128]{3,2,1,0:T(8,128)S(1)} collective-permute-done((f32[8,4,8,128]{3,2,1,0:T(8,128)S(1)}, f32[8,4,8,128]{3,2,1,0:T(8,128)S(1)}, u32[]{:S(2)}, u32[]{:S(2)}) %collective-permute-start.19) | collective-permute-done | bytes 131104 | tf_op jit(solution)/shard_map/ppermute | solution.py:22
  127.8 2.2 %collective-permute-done.20 = f32[8,4,8,128]{3,2,1,0:T(8,128)S(1)} collective-permute-done((f32[8,4,8,128]{3,2,1,0:T(8,128)S(1)}, f32[8,4,8,128]{3,2,1,0:T(8,128)S(1)}, u32[]{:S(2)}, u32[]{:S(2)}) %collective-permute-start.20) | collective-permute-done | bytes 131104 | tf_op jit(solution)/shard_map/ppermute | solution.py:22
  130.0 3.1 %shard_map.30 = (f32[128,4096]{1,0:T(8,128)S(1)}, f32[64,128]{1,0:T(8,128)S(1)}, f32[64,128]{1,0:T(8,128)S(1)}) custom-call(f32[256,128]{1,0:T(8,128)S(1)} %bitcast.27, f32[256,128]{1,0:T(8,128)S(1)} %bitcast.35, f32[256,128]{1,0:T(8,128)S(1)} %bitcast.33, f32[256,128]{1,0:T(8,128)S(1)} %bitcast.42, f32[256,128]{1,0:T(8,128)S(1)} %bitcast.34, ...), custom_call_target="tpu_custom_call" | custom-call | tf_op jit(solution)/shard_map/pallas_call | solution.py:176
  133.1 0.2 collective-permute-start.21
  133.3 1.1 collective-permute-done.21
  134.4 3.9 %collective-permute-done.22 = f32[64,128]{1,0:T(8,128)S(1)} collective-permute-done((f32[64,128]{1,0:T(8,128)S(1)}, f32[64,128]{1,0:T(8,128)S(1)}, u32[]{:S(2)}, u32[]{:S(2)}) %collective-permute-start.22) | collective-permute-done | bytes 32800 | tf_op jit(solution)/shard_map/ppermute | solution.py:22
  138.4 1.1 collective-permute-start.24
  139.4 3.5 %collective-permute-start.25 = (f32[64,128]{1,0:T(8,128)S(1)}, f32[64,128]{1,0:T(8,128)S(1)}, u32[]{:S(2)}, u32[]{:S(2)}) collective-permute-start(f32[64,128]{1,0:T(8,128)S(1)} %add.34), channel_id=1, source_target_pairs={{0,132},{1,133},{2,134},{3,135},{4,0},{5,1},{6,2},{7,3},{8,140},{9... | collective-permute-start | bytes 98312 | tf_op jit(solution)/shard_map/ppermute | solution.py:275
  142.9 3.2 %collective-permute-done.23 = f32[64,128]{1,0:T(8,128)S(1)} collective-permute-done((f32[64,128]{1,0:T(8,128)S(1)}, f32[64,128]{1,0:T(8,128)S(1)}, u32[]{:S(2)}, u32[]{:S(2)}) %collective-permute-start.23) | collective-permute-done | bytes 32800 | tf_op jit(solution)/shard_map/ppermute | solution.py:275
  146.2 0.9 collective-permute-done.25
  147.1 0.1 collective-permute-start.26
  147.2 0.1 collective-permute-start.27
  147.3 3.1 %collective-permute-start.28 = (f32[64,128]{1,0:T(8,128)S(1)}, f32[64,128]{1,0:T(8,128)S(1)}, u32[]{:S(2)}, u32[]{:S(2)}) collective-permute-start(f32[64,128]{1,0:T(8,128)S(1)} %add_add_fusion.2), channel_id=1, source_target_pairs={{0,24},{8,0},{16,8},{24,16},{32,56},{40,32},{48,40},{56,48},{64,88... | collective-permute-start | bytes 98312 | tf_op jit(solution)/shard_map/ppermute | solution.py:22
  150.4 1.9 %collective-permute-done.26 = f32[64,128]{1,0:T(8,128)S(1)} collective-permute-done((f32[64,128]{1,0:T(8,128)S(1)}, f32[64,128]{1,0:T(8,128)S(1)}, u32[]{:S(2)}, u32[]{:S(2)}) %collective-permute-start.26) | collective-permute-done | bytes 32800 | tf_op jit(solution)/shard_map/ppermute | solution.py:22
  152.3 0.4 collective-permute-done.27
  152.7 0.8 collective-permute-done.28
  153.5 0.1 collective-permute-start.29
  153.6 2.7 %collective-permute-start.30 = (f32[64,128]{1,0:T(8,128)S(1)}, f32[64,128]{1,0:T(8,128)S(1)}, u32[]{:S(2)}, u32[]{:S(2)}) collective-permute-start(f32[64,128]{1,0:T(8,128)S(1)} %add_add_fusion.1), channel_id=1, source_target_pairs={{0,64},{8,72},{16,80},{24,88},{32,96},{40,104},{48,112},{56,120},{... | collective-permute-start | bytes 98312 | tf_op jit(solution)/shard_map/ppermute | solution.py:22
  156.3 0.6 collective-permute-start.31
  156.8 1.9 %collective-permute-done.29 = f32[64,128]{1,0:T(8,128)S(1)} collective-permute-done((f32[64,128]{1,0:T(8,128)S(1)}, f32[64,128]{1,0:T(8,128)S(1)}, u32[]{:S(2)}, u32[]{:S(2)}) %collective-permute-start.29) | collective-permute-done | bytes 32800 | tf_op jit(solution)/shard_map/ppermute | solution.py:22
  158.7 0.4 collective-permute-done.30
  159.1 1.1 collective-permute-done.31
  160.2 0.3 collective-permute-start.32
  160.5 1.2 collective-permute-done.32.other
  161.7 4.2 %shard_map.31.inverse = f32[128,128]{1,0:T(8,128)S(1)} custom-call(f32[64,128]{1,0:T(8,128)S(1)} %add_add_fusion.own, f32[64,128]{1,0:T(8,128)S(1)} %collective-permute-done.32.other), custom_call_target="tpu_custom_call" | custom-call | tf_op jit(solution)/shard_map/pallas_call | solution.py:233
  165.9 4.2 %shard_map.32 = f32[4096,128]{1,0:T(8,128)} custom-call(f32[128,128]{1,0:T(8,128)S(1)} %shard_map.31.inverse, f32[128,4096]{1,0:T(8,128)S(1)} %get-tuple-element.56.flat), custom_call_target="tpu_custom_call" | custom-call | tf_op jit(solution)/shard_map/pallas_call | solution.py:257
  (25 shorter events, 0.1 us)
Async XLA Ops:
  0.0 2.1 %copy-start.1 = (f32[16,4,64,128]{3,2,1,0:T(8,128)S(1)}, f32[16,4,64,128]{3,2,1,0:T(8,128)}, u32[]{:S(2)}) copy-start(f32[16,4,64,128]{3,2,1,0:T(8,128)} %param.2) | copy-start | bytes 6291460
  2.1 0.9 copy-start
  3.5 66.2 %collective-permute-start.1 = (f32[17,3,64,128]{3,2,1,0:T(8,128)S(1)}, f32[17,3,64,128]{3,2,1,0:T(8,128)S(1)}, u32[]{:S(2)}, u32[]{:S(2)}) collective-permute-start(f32[17,3,64,128]{3,2,1,0:T(8,128)S(1)} %get-tuple-element.57), channel_id=1, source_target_pairs={{8,0},{16,8},{24,16},{32,24},{40,32},{48,40},{56,48},{64,56},{72,6... | collective-permute-start | bytes 5013512 | tf_op jit(solution)/shard_map/ppermute | solution.py:142
  4.8 65.0 %collective-permute-start = (f32[17,3,64,128]{3,2,1,0:T(8,128)S(1)}, f32[17,3,64,128]{3,2,1,0:T(8,128)S(1)}, u32[]{:S(2)}, u32[]{:S(2)}) collective-permute-start(f32[17,3,64,128]{3,2,1,0:T(8,128)S(1)} %get-tuple-element.58), channel_id=1, source_target_pairs={{0,8},{8,16},{16,24},{24,32},{32,40},{40,48},{48,56},{56,64},{64,7... | collective-permute-start | bytes 5013512 | tf_op jit(solution)/shard_map/ppermute | solution.py:141
  9.4 60.3 %collective-permute-start.2 = (f32[9,3,64,128]{3,2,1,0:T(8,128)S(1)}, f32[9,3,64,128]{3,2,1,0:T(8,128)S(1)}, u32[]{:S(2)}, u32[]{:S(2)}) collective-permute-start(f32[9,3,64,128]{3,2,1,0:T(8,128)S(1)} %pad_maximum_fusion.1), channel_id=1, source_target_pairs={{120,128},{0,248},{248,0},{128,120},{121,129},{1,249},{249,1},{129... | collective-permute-start | bytes 2654216 | tf_op jit(solution)/shard_map/ppermute | solution.py:135
  20.4 14.0 %collective-permute-start.3 = (f32[4,3,64,128]{3,2,1,0:T(8,128)S(1)}, f32[4,3,64,128]{3,2,1,0:T(8,128)S(1)}, u32[]{:S(2)}, u32[]{:S(2)}) collective-permute-start(f32[4,3,64,128]{3,2,1,0:T(8,128)S(1)} %get-tuple-element.62), channel_id=1, source_target_pairs={{120,24},{0,96},{248,152},{128,224},{121,25},{1,97},{249,153},{129... | collective-permute-start | bytes 1179656 | tf_op jit(solution)/shard_map/ppermute | solution.py:138
  21.7 14.0 %collective-permute-start.5 = (f32[4,3,64,128]{3,2,1,0:T(8,128)S(1)}, f32[4,3,64,128]{3,2,1,0:T(8,128)S(1)}, u32[]{:S(2)}, u32[]{:S(2)}) collective-permute-start(f32[4,3,64,128]{3,2,1,0:T(8,128)S(1)} %get-tuple-element.61), channel_id=1, source_target_pairs={{120,88},{0,32},{248,216},{128,160},{121,89},{1,33},{249,217},{129... | collective-permute-start | bytes 1179656 | tf_op jit(solution)/shard_map/ppermute | solution.py:138
  34.4 54.7 %collective-permute-start.4 = (f32[4,3,64,128]{3,2,1,0:T(8,128)S(1)}, f32[4,3,64,128]{3,2,1,0:T(8,128)S(1)}, u32[]{:S(2)}, u32[]{:S(2)}) collective-permute-start(f32[4,3,64,128]{3,2,1,0:T(8,128)S(1)} %collective-permute-done.3), channel_id=1, source_target_pairs={{24,128},{96,248},{152,0},{224,120},{25,129},{97,249},{153,1},{225... | collective-permute-start | bytes 1179656 | tf_op jit(solution)/shard_map/ppermute | solution.py:138
  35.7 53.5 %collective-permute-start.6 = (f32[4,3,64,128]{3,2,1,0:T(8,128)S(1)}, f32[4,3,64,128]{3,2,1,0:T(8,128)S(1)}, u32[]{:S(2)}, u32[]{:S(2)}) collective-permute-start(f32[4,3,64,128]{3,2,1,0:T(8,128)S(1)} %collective-permute-done.5), channel_id=1, source_target_pairs={{88,128},{32,248},{216,0},{160,120},{89,129},{33,249},{217,1},{161... | collective-permute-start | bytes 1179656 | tf_op jit(solution)/shard_map/ppermute | solution.py:138
  73.2 17.0 %collective-permute-start.7 = (f32[8,4,8,128]{3,2,1,0:T(8,128)S(1)}, f32[8,4,8,128]{3,2,1,0:T(8,128)S(1)}, u32[]{:S(2)}, u32[]{:S(2)}) collective-permute-start(f32[8,4,8,128]{3,2,1,0:T(8,128)S(1)} %get-tuple-element.34), channel_id=1, source_target_pairs={{0,7},{1,6},{2,5},{3,4},{4,3},{5,2},{6,1},{7,0},{8,15},{9,14},{10,... | collective-permute-start | bytes 393224 | tf_op jit(solution)/shard_map/ppermute | solution.py:22
  76.2 13.9 %collective-permute-start.8 = (f32[8,4,8,128]{3,2,1,0:T(8,128)S(1)}, f32[8,4,8,128]{3,2,1,0:T(8,128)S(1)}, u32[]{:S(2)}, u32[]{:S(2)}) collective-permute-start(f32[8,4,8,128]{3,2,1,0:T(8,128)S(1)} %get-tuple-element.35), channel_id=1, source_target_pairs={{0,6},{1,7},{2,4},{3,5},{4,2},{5,3},{6,0},{7,1},{8,14},{9,15},{10,... | collective-permute-start | bytes 393224 | tf_op jit(solution)/shard_map/ppermute | solution.py:22
  77.0 20.9 %collective-permute-start.9 = (f32[8,4,8,128]{3,2,1,0:T(8,128)S(1)}, f32[8,4,8,128]{3,2,1,0:T(8,128)S(1)}, u32[]{:S(2)}, u32[]{:S(2)}) collective-permute-start(f32[8,4,8,128]{3,2,1,0:T(8,128)S(1)} %get-tuple-element.36), channel_id=1, source_target_pairs={{0,5},{1,4},{2,7},{3,6},{4,1},{5,0},{6,3},{7,2},{8,13},{9,12},{10,... | collective-permute-start | bytes 393224 | tf_op jit(solution)/shard_map/ppermute | solution.py:22
  89.2 14.4 %collective-permute-start.14 = (f32[8,4,8,128]{3,2,1,0:T(8,128)S(1)}, f32[8,4,8,128]{3,2,1,0:T(8,128)S(1)}, u32[]{:S(2)}, u32[]{:S(2)}) collective-permute-start(f32[8,4,8,128]{3,2,1,0:T(8,128)S(1)} %get-tuple-element.44), channel_id=1, source_target_pairs={{0,3},{1,2},{2,1},{3,0},{4,7},{5,6},{6,5},{7,4},{8,11},{9,10},{10,... | collective-permute-start | bytes 393224 | tf_op jit(solution)/shard_map/ppermute | solution.py:22
  89.2 14.4 %collective-permute-start.16 = (f32[8,4,8,128]{3,2,1,0:T(8,128)S(1)}, f32[8,4,8,128]{3,2,1,0:T(8,128)S(1)}, u32[]{:S(2)}, u32[]{:S(2)}) collective-permute-start(f32[8,4,8,128]{3,2,1,0:T(8,128)S(1)} %get-tuple-element.46), channel_id=1, source_target_pairs={{0,4},{1,5},{2,6},{3,7},{4,0},{5,1},{6,2},{7,3},{8,12},{9,13},{10,... | collective-permute-start | bytes 393224 | tf_op jit(solution)/shard_map/ppermute | solution.py:22
  90.1 16.1 %collective-permute-start.10 = (f32[8,4,8,128]{3,2,1,0:T(8,128)S(1)}, f32[8,4,8,128]{3,2,1,0:T(8,128)S(1)}, u32[]{:S(2)}, u32[]{:S(2)}) collective-permute-start(f32[8,4,8,128]{3,2,1,0:T(8,128)S(1)} %get-tuple-element.40), channel_id=1, source_target_pairs={{0,1},{1,0},{2,3},{3,2},{4,5},{5,4},{6,7},{7,6},{8,9},{9,8},{10,11... | collective-permute-start | bytes 393224 | tf_op jit(solution)/shard_map/ppermute | solution.py:22
  90.1 16.4 %collective-permute-start.12 = (f32[8,4,8,128]{3,2,1,0:T(8,128)S(1)}, f32[8,4,8,128]{3,2,1,0:T(8,128)S(1)}, u32[]{:S(2)}, u32[]{:S(2)}) collective-permute-start(f32[8,4,8,128]{3,2,1,0:T(8,128)S(1)} %get-tuple-element.42), channel_id=1, source_target_pairs={{0,2},{1,3},{2,0},{3,1},{4,6},{5,7},{6,4},{7,5},{8,10},{9,11},{10,... | collective-permute-start | bytes 393224 | tf_op jit(solution)/shard_map/ppermute | solution.py:22
  101.2 9.3 %collective-permute-start.13 = (f32[8,4,8,128]{3,2,1,0:T(8,128)S(1)}, f32[8,4,8,128]{3,2,1,0:T(8,128)S(1)}, u32[]{:S(2)}, u32[]{:S(2)}) collective-permute-start(f32[8,4,8,128]{3,2,1,0:T(8,128)S(1)} %get-tuple-element.43), channel_id=1, source_target_pairs={{0,2},{1,3},{2,0},{3,1},{4,6},{5,7},{6,4},{7,5},{8,10},{9,11},{10,... | collective-permute-start | bytes 393224 | tf_op jit(solution)/shard_map/ppermute | solution.py:22
  103.6 9.3 %collective-permute-start.15 = (f32[8,4,8,128]{3,2,1,0:T(8,128)S(1)}, f32[8,4,8,128]{3,2,1,0:T(8,128)S(1)}, u32[]{:S(2)}, u32[]{:S(2)}) collective-permute-start(f32[8,4,8,128]{3,2,1,0:T(8,128)S(1)} %get-tuple-element.45), channel_id=1, source_target_pairs={{0,3},{1,2},{2,1},{3,0},{4,7},{5,6},{6,5},{7,4},{8,11},{9,10},{10,... | collective-permute-start | bytes 393224 | tf_op jit(solution)/shard_map/ppermute | solution.py:22
  103.6 17.7 %collective-permute-start.17 = (f32[8,4,8,128]{3,2,1,0:T(8,128)S(1)}, f32[8,4,8,128]{3,2,1,0:T(8,128)S(1)}, u32[]{:S(2)}, u32[]{:S(2)}) collective-permute-start(f32[8,4,8,128]{3,2,1,0:T(8,128)S(1)} %get-tuple-element.47), channel_id=1, source_target_pairs={{0,4},{1,5},{2,6},{3,7},{4,0},{5,1},{6,2},{7,3},{8,12},{9,13},{10,... | collective-permute-start | bytes 393224 | tf_op jit(solution)/shard_map/ppermute | solution.py:22
  106.2 17.9 %collective-permute-start.18 = (f32[8,4,8,128]{3,2,1,0:T(8,128)S(1)}, f32[8,4,8,128]{3,2,1,0:T(8,128)S(1)}, u32[]{:S(2)}, u32[]{:S(2)}) collective-permute-start(f32[8,4,8,128]{3,2,1,0:T(8,128)S(1)} %get-tuple-element.49), channel_id=1, source_target_pairs={{0,5},{1,4},{2,7},{3,6},{4,1},{5,0},{6,3},{7,2},{8,13},{9,12},{10,... | collective-permute-start | bytes 393224 | tf_op jit(solution)/shard_map/ppermute | solution.py:22
  106.5 21.3 %collective-permute-start.19 = (f32[8,4,8,128]{3,2,1,0:T(8,128)S(1)}, f32[8,4,8,128]{3,2,1,0:T(8,128)S(1)}, u32[]{:S(2)}, u32[]{:S(2)}) collective-permute-start(f32[8,4,8,128]{3,2,1,0:T(8,128)S(1)} %get-tuple-element.51), channel_id=1, source_target_pairs={{0,6},{1,7},{2,4},{3,5},{4,2},{5,3},{6,0},{7,1},{8,14},{9,15},{10,... | collective-permute-start | bytes 393224 | tf_op jit(solution)/shard_map/ppermute | solution.py:22
  110.5 19.5 %collective-permute-start.20 = (f32[8,4,8,128]{3,2,1,0:T(8,128)S(1)}, f32[8,4,8,128]{3,2,1,0:T(8,128)S(1)}, u32[]{:S(2)}, u32[]{:S(2)}) collective-permute-start(f32[8,4,8,128]{3,2,1,0:T(8,128)S(1)} %get-tuple-element.53), channel_id=1, source_target_pairs={{0,7},{1,6},{2,5},{3,4},{4,3},{5,2},{6,1},{7,0},{8,15},{9,14},{10,... | collective-permute-start | bytes 393224 | tf_op jit(solution)/shard_map/ppermute | solution.py:22
  112.9 17.1 %collective-permute-start.11 = (f32[8,4,8,128]{3,2,1,0:T(8,128)S(1)}, f32[8,4,8,128]{3,2,1,0:T(8,128)S(1)}, u32[]{:S(2)}, u32[]{:S(2)}) collective-permute-start(f32[8,4,8,128]{3,2,1,0:T(8,128)S(1)} %get-tuple-element.41), channel_id=1, source_target_pairs={{0,1},{1,0},{2,3},{3,2},{4,5},{5,4},{6,7},{7,6},{8,9},{9,8},{10,11... | collective-permute-start | bytes 393224 | tf_op jit(solution)/shard_map/ppermute | solution.py:22
  133.1 1.3 collective-permute-start.21
  134.4 3.9 %collective-permute-start.22 = (f32[64,128]{1,0:T(8,128)S(1)}, f32[64,128]{1,0:T(8,128)S(1)}, u32[]{:S(2)}, u32[]{:S(2)}) collective-permute-start(f32[64,128]{1,0:T(8,128)S(1)} %add.33), channel_id=1, source_target_pairs={{0,2},{1,3},{2,0},{3,1},{4,6},{5,7},{6,4},{7,5},{8,10},{9,11},{10,... | collective-permute-start | bytes 98312 | tf_op jit(solution)/shard_map/ppermute | solution.py:22
  138.4 7.8 %collective-permute-start.23 = (f32[64,128]{1,0:T(8,128)S(1)}, f32[64,128]{1,0:T(8,128)S(1)}, u32[]{:S(2)}, u32[]{:S(2)}) collective-permute-start(f32[64,128]{1,0:T(8,128)S(1)} %add.34), channel_id=1, source_target_pairs={{0,128},{1,129},{2,130},{3,131},{4,132},{5,133},{6,134},{7,135},{8... | collective-permute-start | bytes 98312 | tf_op jit(solution)/shard_map/ppermute | solution.py:275
  138.4 7.8 %collective-permute-start.24 = (f32[64,128]{1,0:T(8,128)S(1)}, f32[64,128]{1,0:T(8,128)S(1)}, u32[]{:S(2)}, u32[]{:S(2)}) collective-permute-start(f32[64,128]{1,0:T(8,128)S(1)} %add.34), channel_id=1, source_target_pairs={{0,4},{1,5},{2,6},{3,7},{4,128},{5,129},{6,130},{7,131},{8,12},{9,... | collective-permute-start | bytes 98312 | tf_op jit(solution)/shard_map/ppermute | solution.py:275
  139.4 7.6 %collective-permute-start.25 = (f32[64,128]{1,0:T(8,128)S(1)}, f32[64,128]{1,0:T(8,128)S(1)}, u32[]{:S(2)}, u32[]{:S(2)}) collective-permute-start(f32[64,128]{1,0:T(8,128)S(1)} %add.34), channel_id=1, source_target_pairs={{0,132},{1,133},{2,134},{3,135},{4,0},{5,1},{6,2},{7,3},{8,140},{9... | collective-permute-start | bytes 98312 | tf_op jit(solution)/shard_map/ppermute | solution.py:275
  147.1 5.2 %collective-permute-start.26 = (f32[64,128]{1,0:T(8,128)S(1)}, f32[64,128]{1,0:T(8,128)S(1)}, u32[]{:S(2)}, u32[]{:S(2)}) collective-permute-start(f32[64,128]{1,0:T(8,128)S(1)} %add_add_fusion.2), channel_id=1, source_target_pairs={{0,8},{8,16},{16,24},{24,0},{32,40},{40,48},{48,56},{56,32},{64,72... | collective-permute-start | bytes 98312 | tf_op jit(solution)/shard_map/ppermute | solution.py:22
  147.2 5.5 %collective-permute-start.27 = (f32[64,128]{1,0:T(8,128)S(1)}, f32[64,128]{1,0:T(8,128)S(1)}, u32[]{:S(2)}, u32[]{:S(2)}) collective-permute-start(f32[64,128]{1,0:T(8,128)S(1)} %add_add_fusion.2), channel_id=1, source_target_pairs={{0,16},{8,24},{16,0},{24,8},{32,48},{40,56},{48,32},{56,40},{64,80... | collective-permute-start | bytes 98312 | tf_op jit(solution)/shard_map/ppermute | solution.py:22
  147.3 6.2 %collective-permute-start.28 = (f32[64,128]{1,0:T(8,128)S(1)}, f32[64,128]{1,0:T(8,128)S(1)}, u32[]{:S(2)}, u32[]{:S(2)}) collective-permute-start(f32[64,128]{1,0:T(8,128)S(1)} %add_add_fusion.2), channel_id=1, source_target_pairs={{0,24},{8,0},{16,8},{24,16},{32,56},{40,32},{48,40},{56,48},{64,88... | collective-permute-start | bytes 98312 | tf_op jit(solution)/shard_map/ppermute | solution.py:22
  153.5 5.2 %collective-permute-start.29 = (f32[64,128]{1,0:T(8,128)S(1)}, f32[64,128]{1,0:T(8,128)S(1)}, u32[]{:S(2)}, u32[]{:S(2)}) collective-permute-start(f32[64,128]{1,0:T(8,128)S(1)} %add_add_fusion.1), channel_id=1, source_target_pairs={{0,32},{8,40},{16,48},{24,56},{32,64},{40,72},{48,80},{56,88},{64,... | collective-permute-start | bytes 98312 | tf_op jit(solution)/shard_map/ppermute | solution.py:22
  153.6 5.5 %collective-permute-start.30 = (f32[64,128]{1,0:T(8,128)S(1)}, f32[64,128]{1,0:T(8,128)S(1)}, u32[]{:S(2)}, u32[]{:S(2)}) collective-permute-start(f32[64,128]{1,0:T(8,128)S(1)} %add_add_fusion.1), channel_id=1, source_target_pairs={{0,64},{8,72},{16,80},{24,88},{32,96},{40,104},{48,112},{56,120},{... | collective-permute-start | bytes 98312 | tf_op jit(solution)/shard_map/ppermute | solution.py:22
  156.3 3.9 %collective-permute-start.31 = (f32[64,128]{1,0:T(8,128)S(1)}, f32[64,128]{1,0:T(8,128)S(1)}, u32[]{:S(2)}, u32[]{:S(2)}) collective-permute-start(f32[64,128]{1,0:T(8,128)S(1)} %add_add_fusion.1), channel_id=1, source_target_pairs={{0,96},{8,104},{16,112},{24,120},{32,0},{40,8},{48,16},{56,24},{64... | collective-permute-start | bytes 98312 | tf_op jit(solution)/shard_map/ppermute | solution.py:22
  160.2 1.5 collective-permute-start.32

commit v8 on v7

--- a/solution.py
+++ b/solution.py
@@ -10,7 +10,7 @@
 
 DEPTH = 3
 TIED = True
-EARLY = (7, 6, 5)
+EARLY = (6,)
 PANEL = 32
 SIDE = 4
 SHARES = (8, 4, 4)
@@ -143,6 +143,13 @@
     return low, high, seams
 
 
+def thirds(block):
+    first = block.astype(jnp.bfloat16)
+    rest = block - first.astype(jnp.float32)
+    second = rest.astype(jnp.bfloat16)
+    return first, second, (rest - second.astype(jnp.float32)).astype(jnp.bfloat16)
+
+
 def gram_kernel(pieces, cells, *rest):
     refs, (flat, own, other, gram) = rest[:-4], rest[-4:]
     me = lax.axis_index("band")
@@ -154,14 +161,17 @@
         rows = pl.ds(pl.multiple_of(first, share), share)
         for r in range(cells):
             flat[rows, r * lanes : (r + 1) * lanes] = ref[pl.ds(r, share, stride=cells), :]
-    whole = flat[...]
-    gram[...] = lax.dot_general(
-        whole,
-        whole,
-        (((1,), (1,)), ((), ())),
-        precision=lax.Precision.HIGHEST,
-        preferred_element_type=jnp.float32,
-    )
+    one, two, three = thirds(flat[...])
+    size = flat.shape[0]
+
+    def product(left, right):
+        return lax.dot_general(
+            left, right, (((1,), (1,)), ((), ())), preferred_element_type=jnp.float32
+        )
+
+    wide = product(one, jnp.concatenate([one, two]))
+    cross = wide[:, size:] + product(one, three)
+    gram[...] = wide[:, :size] + (product(two, two) + (cross + cross.T))
     half = gram.shape[0] // 2
     core = lax.rem(lax.axis_index("band"), 2)
     own[...] = gram[pl.ds(pl.multiple_of(core * half, half), half)]
@@ -238,25 +248,34 @@
     )(own, other)
 
 
-def rotate_kernel(cells, inverse, flat, out):
-    orbitals = inverse.shape[0]
-    lanes = out.shape[1]
-    solved = jnp.dot(
-        inverse[...],
-        flat[...],
-        precision=lax.Precision.HIGHEST,
-        preferred_element_type=jnp.float32,
-    )
-    for r in range(cells):
-        out[pl.ds(r, orbitals, stride=cells), :] = solved[:, r * lanes : (r + 1) * lanes]
-
-
-def rotated(inverse, flat, lanes):
+def rotate_kernel(inverse, flat, out):
+    width, lanes = out.shape[2:]
+    a, b = thirds(inverse[...]), thirds(flat[...])
+
+    def product(left, right):
+        left = jnp.concatenate([a[left[0]], a[left[1]]], axis=1)
+        right = jnp.concatenate([b[right[0]], b[right[1]]])
+        return jnp.dot(left, right, preferred_element_type=jnp.float32)
+
+    small = product((1, 2), (1, 0)) + product((0, 0), (2, 1))
+    solved = product((0, 1), (0, 0)) + small
+    for r in range(width):
+        out[:, 0, r, :] = solved[:, r * lanes : (r + 1) * lanes]
+
+
+def rotated(inverse, flat, planes, lanes):
     orbitals, columns = flat.shape
-    cells = columns // lanes
+    block = columns // planes
+    shape = (orbitals, planes, block // lanes, lanes)
     return pl.pallas_call(
-        functools.partial(rotate_kernel, cells),
-        out_shape=jax.ShapeDtypeStruct((orbitals * cells, lanes), jnp.float32),
+        rotate_kernel,
+        grid=(planes,),
+        in_specs=[
+            pl.BlockSpec((orbitals, orbitals), lambda i: (0, 0)),
+            pl.BlockSpec((orbitals, block), lambda i: (0, i)),
+        ],
+        out_specs=pl.BlockSpec((orbitals, 1, *shape[2:]), lambda i: (0, i, 0, 0)),
+        out_shape=jax.ShapeDtypeStruct(shape, jnp.float32),
         compiler_params=pltpu.CompilerParams(vmem_limit_bytes=32 * 1024 * 1024),
     )(inverse, flat)
 
@@ -313,9 +332,7 @@
     slots = [[first[k], second[k]] for k in range(stripes)]
     flat, own_half, other_half = flat_and_gram(slots, orb_total)
     inverse = scaled_inverse(*summed(own_half, other_half), math.sqrt(cell_total))
-    return rotated(inverse, flat, nx_all).reshape(
-        orb_total, planes, ny_all // stripes, nx_all
-    )
+    return rotated(inverse, flat, planes, nx_all)
 
 
 def solution(mesh):

time: 173 us -> 170 us (0.983); the launches traced: 170 us -> 169 us
  waiting for transfers between devices: 89 us -> 79.3 us
  starting transfers between devices: 59 us -> 68.4 us
    ppermute x23, starting transfers between devices: 32.3 us -> 42.1 us  [permuted(): return lax.ppermute(block, axis, [(i, target(i)) for i in range(count)])]
    ppermute x23, waiting for transfers between devices: 40.9 us -> 31.2 us  [permuted(): return lax.ppermute(block, axis, [(i, target(i)) for i in range(count)])]
  transfers between devices with their start and end apart: 33 -> 33, of which waited for: 20 -> 18; matrix products, arithmetic and copies ran while one was open for 0% -> 0% of each run, Pallas kernels for 4% -> 4%
where the time goes in v8:
time: 170 us; the launch traced here: 169 us
  waiting for transfers between devices  79.3 us (47%)
  starting transfers between devices  68.4 us (40%)
  Pallas kernels  17.2 us (10%)
  other arithmetic  2.23 us (1%)
    ppermute x23, starting transfers between devices, permuted(): return lax.ppermute(block, axis, [(i, target(i)) for i in range(count)])  42.1 us
    ppermute x1, waiting for transfers between devices, halos(): seams = [lax.ppermute(blocks[0], 'domain', seam_pairs())]  32.7 us
    ppermute x23, waiting for transfers between devices, permuted(): return lax.ppermute(block, axis, [(i, target(i)) for i in range(count)])  31.2 us
    ppermute x2, waiting for transfers between devices, halos(): lax.ppermute(block, 'domain', out)  11.2 us
    ppermute x1, starting transfers between devices, halos(): seams = [lax.ppermute(blocks[0], 'domain', seam_pairs())]  10.9 us
    pallas_call x2, Pallas kernels, filtered_stripes(): pl.pallas_call(functools.partial(filter_kernel, begin, shares, stripes),...  6.73 us
    ppermute x1, starting transfers between devices, halos(): low = lax.ppermute(both[:, planes - DEPTH:], 'domain', inner_pairs(1))  4.65 us
    ppermute x3, starting transfers between devices, along_z(): return lax.ppermute(block, ('domain', 'band'), pairs)  4.22 us
  transfers between devices with their start and end apart: 33, of which 18 were waited for; matrix products, arithmetic and copies ran while one was open for 0% of the time, Pallas kernels for 4%

profile of v8, /device:TPU:32, one launch (start us, length us, event | category | flops | bytes accessed | tf_op | source)
XLA Modules:
  0.0 168.8 jit_solution(17920965453984798124)
XLA Ops:
  0.0 1.6 slice_select_fusion
  1.6 0.4 copy-done.1
  2.1 0.1 slice_select_fusion.1
  2.1 0.8 copy-done
  3.0 0.1 pad_maximum_fusion.1
  3.1 0.4 pad_maximum_fusion
  3.5 1.3 collective-permute-start.1
  4.8 4.7 %collective-permute-start = (f32[17,3,64,128]{3,2,1,0:T(8,128)S(1)}, f32[17,3,64,128]{3,2,1,0:T(8,128)S(1)}, u32[]{:S(2)}, u32[]{:S(2)}) collective-permute-start(f32[17,3,64,128]{3,2,1,0:T(8,128)S(1)} %get-tuple-element.54), channel_id=1, source_target_pairs={{0,8},{8,16},{16,24},{24,32},{32,40},{40,48},{48,56},{56,64},{64,7... | collective-permute-start | bytes 5013512 | tf_op jit(solution)/shard_map/ppermute | solution.py:141
  9.4 10.9 %collective-permute-start.2 = (f32[9,3,64,128]{3,2,1,0:T(8,128)S(1)}, f32[9,3,64,128]{3,2,1,0:T(8,128)S(1)}, u32[]{:S(2)}, u32[]{:S(2)}) collective-permute-start(f32[9,3,64,128]{3,2,1,0:T(8,128)S(1)} %pad_maximum_fusion.1), channel_id=1, source_target_pairs={{120,128},{0,248},{248,0},{128,120},{121,129},{1,249},{249,1},{129... | collective-permute-start | bytes 2654216 | tf_op jit(solution)/shard_map/ppermute | solution.py:135
  20.4 1.3 collective-permute-start.3
  21.7 1.3 collective-permute-start.5
  23.0 0.1 fusion.1
  23.2 11.2 %collective-permute-done.3 = f32[4,3,64,128]{3,2,1,0:T(8,128)S(1)} collective-permute-done((f32[4,3,64,128]{3,2,1,0:T(8,128)S(1)}, f32[4,3,64,128]{3,2,1,0:T(8,128)S(1)}, u32[]{:S(2)}, u32[]{:S(2)}) %collective-permute-start.3) | collective-permute-done | bytes 393248 | tf_op jit(solution)/shard_map/ppermute | solution.py:138
  34.4 1.3 collective-permute-start.4
  35.7 1.3 collective-permute-start.6
  37.0 32.7 %collective-permute-done.2.rest_0_ = f32[9,3,64,128]{3,2,1,0:T(8,128)S(1)} collective-permute-done((f32[9,3,64,128]{3,2,1,0:T(8,128)S(1)}, f32[9,3,64,128]{3,2,1,0:T(8,128)S(1)}, u32[]{:S(2)}, u32[]{:S(2)}) %collective-permute-start.2) | collective-permute-done | bytes 884768 | tf_op jit(solution)/shard_map/ppermute | solution.py:135
  69.7 0.0 collective-permute-done.low
  69.8 3.4 %shard_map.28 = (f32[8,4,8,128]{3,2,1,0:T(8,128)S(1)}, f32[8,4,8,128]{3,2,1,0:T(8,128)S(1)}, f32[8,4,8,128]{3,2,1,0:T(8,128)S(1)}, f32[8,4,8,128]{3,2,1,0:T(8,12...) custom-call(f32[8,4,64,128]{3,2,1,0:T(8,128)S(1)} %get-tuple-element, ...), custom_call_target="tpu_custom_call" | custom-call | tf_op jit(solution)/shard_map/pallas_call | solution.py:81
  73.2 3.7 %collective-permute-start.7 = (f32[8,4,8,128]{3,2,1,0:T(8,128)S(1)}, f32[8,4,8,128]{3,2,1,0:T(8,128)S(1)}, u32[]{:S(2)}, u32[]{:S(2)}) collective-permute-start(f32[8,4,8,128]{3,2,1,0:T(8,128)S(1)} %get-tuple-element.32), channel_id=1, source_target_pairs={{0,6},{1,7},{2,4},{3,5},{4,2},{5,3},{6,0},{7,1},{8,14},{9,15},{10,... | collective-permute-start | bytes 393224 | tf_op jit(solution)/shard_map/ppermute | solution.py:22
  76.9 7.8 %collective-permute-start.12 = (f32[8,4,8,128]{3,2,1,0:T(8,128)S(1)}, f32[8,4,8,128]{3,2,1,0:T(8,128)S(1)}, u32[]{:S(2)}, u32[]{:S(2)}) collective-permute-start(f32[8,4,8,128]{3,2,1,0:T(8,128)S(1)} %get-tuple-element.40), channel_id=1, source_target_pairs={{0,3},{1,2},{2,1},{3,0},{4,7},{5,6},{6,5},{7,4},{8,11},{9,10},{10,... | collective-permute-start | bytes 393224 | tf_op jit(solution)/shard_map/ppermute | solution.py:22
  84.7 1.4 collective-permute-start.14
  86.1 3.6 %collective-permute-start.16 = (f32[8,4,8,128]{3,2,1,0:T(8,128)S(1)}, f32[8,4,8,128]{3,2,1,0:T(8,128)S(1)}, u32[]{:S(2)}, u32[]{:S(2)}) collective-permute-start(f32[8,4,8,128]{3,2,1,0:T(8,128)S(1)} %get-tuple-element.44), channel_id=1, source_target_pairs={{0,5},{1,4},{2,7},{3,6},{4,1},{5,0},{6,3},{7,2},{8,13},{9,12},{10,... | collective-permute-start | bytes 393224 | tf_op jit(solution)/shard_map/ppermute | solution.py:22
  89.7 0.1 collective-permute-start.8
  89.8 3.3 %shard_map.29 = (f32[8,4,8,128]{3,2,1,0:T(8,128)S(1)}, f32[8,4,8,128]{3,2,1,0:T(8,128)S(1)}, f32[8,4,8,128]{3,2,1,0:T(8,128)S(1)}, f32[8,4,8,128]{3,2,1,0:T(8,12...) custom-call(f32[8,4,64,128]{3,2,1,0:T(8,128)S(1)} %get-tuple-element, ...), custom_call_target="tpu_custom_call" | custom-call | tf_op jit(solution)/shard_map/pallas_call | solution.py:81
  93.2 0.0 collective-permute-done.12
  93.2 1.9 %collective-permute-start.10 = (f32[8,4,8,128]{3,2,1,0:T(8,128)S(1)}, f32[8,4,8,128]{3,2,1,0:T(8,128)S(1)}, u32[]{:S(2)}, u32[]{:S(2)}) collective-permute-start(f32[8,4,8,128]{3,2,1,0:T(8,128)S(1)} %get-tuple-element.38), channel_id=1, source_target_pairs={{0,2},{1,3},{2,0},{3,1},{4,6},{5,7},{6,4},{7,5},{8,10},{9,11},{10,... | collective-permute-start | bytes 393224 | tf_op jit(solution)/shard_map/ppermute | solution.py:22
  95.1 8.1 %collective-permute-start.11 = (f32[8,4,8,128]{3,2,1,0:T(8,128)S(1)}, f32[8,4,8,128]{3,2,1,0:T(8,128)S(1)}, u32[]{:S(2)}, u32[]{:S(2)}) collective-permute-start(f32[8,4,8,128]{3,2,1,0:T(8,128)S(1)} %get-tuple-element.39), channel_id=1, source_target_pairs={{0,2},{1,3},{2,0},{3,1},{4,6},{5,7},{6,4},{7,5},{8,10},{9,11},{10,... | collective-permute-start | bytes 393224 | tf_op jit(solution)/shard_map/ppermute | solution.py:22
  103.2 2.2 %collective-permute-start.13 = (f32[8,4,8,128]{3,2,1,0:T(8,128)S(1)}, f32[8,4,8,128]{3,2,1,0:T(8,128)S(1)}, u32[]{:S(2)}, u32[]{:S(2)}) collective-permute-start(f32[8,4,8,128]{3,2,1,0:T(8,128)S(1)} %get-tuple-element.41), channel_id=1, source_target_pairs={{0,3},{1,2},{2,1},{3,0},{4,7},{5,6},{6,5},{7,4},{8,11},{9,10},{10,... | collective-permute-start | bytes 393224 | tf_op jit(solution)/shard_map/ppermute | solution.py:22
  105.4 0.0 collective-permute-done.19
  105.4 1.3 collective-permute-start.15
  106.6 0.0 collective-permute-done.8
  106.6 1.6 collective-permute-start.17
  108.2 1.4 collective-permute-start.18
  109.7 1.0 collective-permute-start.20
  110.7 1.3 collective-permute-done.13
  111.9 0.0 collective-permute-start.9
  111.9 9.2 %collective-permute-done.15 = f32[8,4,8,128]{3,2,1,0:T(8,128)S(1)} collective-permute-done((f32[8,4,8,128]{3,2,1,0:T(8,128)S(1)}, f32[8,4,8,128]{3,2,1,0:T(8,128)S(1)}, u32[]{:S(2)}, u32[]{:S(2)}) %collective-permute-start.15) | collective-permute-done | bytes 131104 | tf_op jit(solution)/shard_map/ppermute | solution.py:22
  121.2 2.8 %collective-permute-done.17 = f32[8,4,8,128]{3,2,1,0:T(8,128)S(1)} collective-permute-done((f32[8,4,8,128]{3,2,1,0:T(8,128)S(1)}, f32[8,4,8,128]{3,2,1,0:T(8,128)S(1)}, u32[]{:S(2)}, u32[]{:S(2)}) %collective-permute-start.17) | collective-permute-done | bytes 131104 | tf_op jit(solution)/shard_map/ppermute | solution.py:22
  124.0 5.1 %collective-permute-done.18 = f32[8,4,8,128]{3,2,1,0:T(8,128)S(1)} collective-permute-done((f32[8,4,8,128]{3,2,1,0:T(8,128)S(1)}, f32[8,4,8,128]{3,2,1,0:T(8,128)S(1)}, u32[]{:S(2)}, u32[]{:S(2)}) %collective-permute-start.18) | collective-permute-done | bytes 131104 | tf_op jit(solution)/shard_map/ppermute | solution.py:22
  129.1 0.5 collective-permute-done.20
  129.6 2.6 %shard_map.30 = (f32[128,4096]{1,0:T(8,128)S(1)}, f32[64,128]{1,0:T(8,128)S(1)}, f32[64,128]{1,0:T(8,128)S(1)}) custom-call(f32[256,128]{1,0:T(8,128)S(1)} %bitcast.26, f32[256,128]{1,0:T(8,128)S(1)} %bitcast.33, f32[256,128]{1,0:T(8,128)S(1)} %bitcast.32, f32[256,128]{1,0:T(8,128)S(1)} %bitcast.41, f32[256,128]{1,0:T(8,128)S(1)} %bitcast.34, ...), custom_call_target="tpu_custom_call" | custom-call | tf_op jit(solution)/shard_map/pallas_call | solution.py:186
  132.2 1.1 collective-permute-start.21
  133.3 0.9 collective-permute-done.21
  134.2 3.9 %collective-permute-done.22 = f32[64,128]{1,0:T(8,128)S(1)} collective-permute-done((f32[64,128]{1,0:T(8,128)S(1)}, f32[64,128]{1,0:T(8,128)S(1)}, u32[]{:S(2)}, u32[]{:S(2)}) %collective-permute-start.22) | collective-permute-done | bytes 32800 | tf_op jit(solution)/shard_map/ppermute | solution.py:22
  138.1 0.1 collective-permute-start.24
  138.2 4.1 %collective-permute-start.25 = (f32[64,128]{1,0:T(8,128)S(1)}, f32[64,128]{1,0:T(8,128)S(1)}, u32[]{:S(2)}, u32[]{:S(2)}) collective-permute-start(f32[64,128]{1,0:T(8,128)S(1)} %add.34), channel_id=1, source_target_pairs={{0,132},{1,133},{2,134},{3,135},{4,0},{5,1},{6,2},{7,3},{8,140},{9... | collective-permute-start | bytes 98312 | tf_op jit(solution)/shard_map/ppermute | solution.py:294
  142.3 3.7 %collective-permute-done.23 = f32[64,128]{1,0:T(8,128)S(1)} collective-permute-done((f32[64,128]{1,0:T(8,128)S(1)}, f32[64,128]{1,0:T(8,128)S(1)}, u32[]{:S(2)}, u32[]{:S(2)}) %collective-permute-start.23) | collective-permute-done | bytes 32800 | tf_op jit(solution)/shard_map/ppermute | solution.py:294
  146.0 0.4 collective-permute-done.25
  146.5 0.1 collective-permute-start.26
  146.6 0.1 collective-permute-start.27
  146.7 3.1 %collective-permute-start.28 = (f32[64,128]{1,0:T(8,128)S(1)}, f32[64,128]{1,0:T(8,128)S(1)}, u32[]{:S(2)}, u32[]{:S(2)}) collective-permute-start(f32[64,128]{1,0:T(8,128)S(1)} %add_add_fusion.2), channel_id=1, source_target_pairs={{0,24},{8,0},{16,8},{24,16},{32,56},{40,32},{48,40},{56,48},{64,88... | collective-permute-start | bytes 98312 | tf_op jit(solution)/shard_map/ppermute | solution.py:22
  149.8 1.9 %collective-permute-done.26 = f32[64,128]{1,0:T(8,128)S(1)} collective-permute-done((f32[64,128]{1,0:T(8,128)S(1)}, f32[64,128]{1,0:T(8,128)S(1)}, u32[]{:S(2)}, u32[]{:S(2)}) %collective-permute-start.26) | collective-permute-done | bytes 32800 | tf_op jit(solution)/shard_map/ppermute | solution.py:22
  151.7 0.4 collective-permute-done.27
  152.1 0.8 collective-permute-done.28
  152.9 0.1 collective-permute-start.29
  153.0 2.5 %collective-permute-start.30 = (f32[64,128]{1,0:T(8,128)S(1)}, f32[64,128]{1,0:T(8,128)S(1)}, u32[]{:S(2)}, u32[]{:S(2)}) collective-permute-start(f32[64,128]{1,0:T(8,128)S(1)} %add_add_fusion.1), channel_id=1, source_target_pairs={{0,64},{8,72},{16,80},{24,88},{32,96},{40,104},{48,112},{56,120},{... | collective-permute-start | bytes 98312 | tf_op jit(solution)/shard_map/ppermute | solution.py:22
  155.5 0.7 collective-permute-start.31
  156.2 1.9 %collective-permute-done.29 = f32[64,128]{1,0:T(8,128)S(1)} collective-permute-done((f32[64,128]{1,0:T(8,128)S(1)}, f32[64,128]{1,0:T(8,128)S(1)}, u32[]{:S(2)}, u32[]{:S(2)}) %collective-permute-start.29) | collective-permute-done | bytes 32800 | tf_op jit(solution)/shard_map/ppermute | solution.py:22
  158.1 0.4 collective-permute-done.30
  158.5 0.9 collective-permute-done.31
  159.4 0.3 collective-permute-start.32
  159.7 1.2 collective-permute-done.32.other
  160.9 4.2 %shard_map.31.inverse = f32[128,128]{1,0:T(8,128)S(1)} custom-call(f32[64,128]{1,0:T(8,128)S(1)} %add_add_fusion.own, f32[64,128]{1,0:T(8,128)S(1)} %collective-permute-done.32.other), custom_call_target="tpu_custom_call" | custom-call | tf_op jit(solution)/shard_map/pallas_call | solution.py:243
  165.1 3.7 %shard_map.32 = f32[128,4,8,128]{3,2,1,0:T(8,128)} custom-call(f32[128,128]{1,0:T(8,128)S(1)} %shard_map.31.inverse, f32[128,4096]{1,0:T(8,128)S(1)} %get-tuple-element.52.flat), custom_call_target="tpu_custom_call" | custom-call | tf_op jit(solution)/shard_map/pallas_call | solution.py:270
  (25 shorter events, 0.1 us)
Async XLA Ops:
  0.0 2.1 %copy-start.1 = (f32[16,4,64,128]{3,2,1,0:T(8,128)S(1)}, f32[16,4,64,128]{3,2,1,0:T(8,128)}, u32[]{:S(2)}) copy-start(f32[16,4,64,128]{3,2,1,0:T(8,128)} %param.2) | copy-start | bytes 6291460
  2.1 0.9 copy-start
  3.5 66.2 %collective-permute-start.1 = (f32[17,3,64,128]{3,2,1,0:T(8,128)S(1)}, f32[17,3,64,128]{3,2,1,0:T(8,128)S(1)}, u32[]{:S(2)}, u32[]{:S(2)}) collective-permute-start(f32[17,3,64,128]{3,2,1,0:T(8,128)S(1)} %get-tuple-element.53), channel_id=1, source_target_pairs={{8,0},{16,8},{24,16},{32,24},{40,32},{48,40},{56,48},{64,56},{72,6... | collective-permute-start | bytes 5013512 | tf_op jit(solution)/shard_map/ppermute | solution.py:142
  4.8 65.0 %collective-permute-start = (f32[17,3,64,128]{3,2,1,0:T(8,128)S(1)}, f32[17,3,64,128]{3,2,1,0:T(8,128)S(1)}, u32[]{:S(2)}, u32[]{:S(2)}) collective-permute-start(f32[17,3,64,128]{3,2,1,0:T(8,128)S(1)} %get-tuple-element.54), channel_id=1, source_target_pairs={{0,8},{8,16},{16,24},{24,32},{32,40},{40,48},{48,56},{56,64},{64,7... | collective-permute-start | bytes 5013512 | tf_op jit(solution)/shard_map/ppermute | solution.py:141
  9.4 60.3 %collective-permute-start.2 = (f32[9,3,64,128]{3,2,1,0:T(8,128)S(1)}, f32[9,3,64,128]{3,2,1,0:T(8,128)S(1)}, u32[]{:S(2)}, u32[]{:S(2)}) collective-permute-start(f32[9,3,64,128]{3,2,1,0:T(8,128)S(1)} %pad_maximum_fusion.1), channel_id=1, source_target_pairs={{120,128},{0,248},{248,0},{128,120},{121,129},{1,249},{249,1},{129... | collective-permute-start | bytes 2654216 | tf_op jit(solution)/shard_map/ppermute | solution.py:135
  20.4 14.0 %collective-permute-start.3 = (f32[4,3,64,128]{3,2,1,0:T(8,128)S(1)}, f32[4,3,64,128]{3,2,1,0:T(8,128)S(1)}, u32[]{:S(2)}, u32[]{:S(2)}) collective-permute-start(f32[4,3,64,128]{3,2,1,0:T(8,128)S(1)} %get-tuple-element.58), channel_id=1, source_target_pairs={{120,24},{0,96},{248,152},{128,224},{121,25},{1,97},{249,153},{129... | collective-permute-start | bytes 1179656 | tf_op jit(solution)/shard_map/ppermute | solution.py:138
  21.7 14.0 %collective-permute-start.5 = (f32[4,3,64,128]{3,2,1,0:T(8,128)S(1)}, f32[4,3,64,128]{3,2,1,0:T(8,128)S(1)}, u32[]{:S(2)}, u32[]{:S(2)}) collective-permute-start(f32[4,3,64,128]{3,2,1,0:T(8,128)S(1)} %get-tuple-element.57), channel_id=1, source_target_pairs={{120,88},{0,32},{248,216},{128,160},{121,89},{1,33},{249,217},{129... | collective-permute-start | bytes 1179656 | tf_op jit(solution)/shard_map/ppermute | solution.py:138
  34.4 51.7 %collective-permute-start.4 = (f32[4,3,64,128]{3,2,1,0:T(8,128)S(1)}, f32[4,3,64,128]{3,2,1,0:T(8,128)S(1)}, u32[]{:S(2)}, u32[]{:S(2)}) collective-permute-start(f32[4,3,64,128]{3,2,1,0:T(8,128)S(1)} %collective-permute-done.3), channel_id=1, source_target_pairs={{24,128},{96,248},{152,0},{224,120},{25,129},{97,249},{153,1},{225... | collective-permute-start | bytes 1179656 | tf_op jit(solution)/shard_map/ppermute | solution.py:138
  35.7 54.0 %collective-permute-start.6 = (f32[4,3,64,128]{3,2,1,0:T(8,128)S(1)}, f32[4,3,64,128]{3,2,1,0:T(8,128)S(1)}, u32[]{:S(2)}, u32[]{:S(2)}) collective-permute-start(f32[4,3,64,128]{3,2,1,0:T(8,128)S(1)} %collective-permute-done.5), channel_id=1, source_target_pairs={{88,128},{32,248},{216,0},{160,120},{89,129},{33,249},{217,1},{161... | collective-permute-start | bytes 1179656 | tf_op jit(solution)/shard_map/ppermute | solution.py:138
  73.2 16.6 %collective-permute-start.7 = (f32[8,4,8,128]{3,2,1,0:T(8,128)S(1)}, f32[8,4,8,128]{3,2,1,0:T(8,128)S(1)}, u32[]{:S(2)}, u32[]{:S(2)}) collective-permute-start(f32[8,4,8,128]{3,2,1,0:T(8,128)S(1)} %get-tuple-element.32), channel_id=1, source_target_pairs={{0,6},{1,7},{2,4},{3,5},{4,2},{5,3},{6,0},{7,1},{8,14},{9,15},{10,... | collective-permute-start | bytes 393224 | tf_op jit(solution)/shard_map/ppermute | solution.py:22
  76.9 16.3 %collective-permute-start.12 = (f32[8,4,8,128]{3,2,1,0:T(8,128)S(1)}, f32[8,4,8,128]{3,2,1,0:T(8,128)S(1)}, u32[]{:S(2)}, u32[]{:S(2)}) collective-permute-start(f32[8,4,8,128]{3,2,1,0:T(8,128)S(1)} %get-tuple-element.40), channel_id=1, source_target_pairs={{0,3},{1,2},{2,1},{3,0},{4,7},{5,6},{6,5},{7,4},{8,11},{9,10},{10,... | collective-permute-start | bytes 393224 | tf_op jit(solution)/shard_map/ppermute | solution.py:22
  84.7 10.4 %collective-permute-start.14 = (f32[8,4,8,128]{3,2,1,0:T(8,128)S(1)}, f32[8,4,8,128]{3,2,1,0:T(8,128)S(1)}, u32[]{:S(2)}, u32[]{:S(2)}) collective-permute-start(f32[8,4,8,128]{3,2,1,0:T(8,128)S(1)} %get-tuple-element.42), channel_id=1, source_target_pairs={{0,4},{1,5},{2,6},{3,7},{4,0},{5,1},{6,2},{7,3},{8,12},{9,13},{10,... | collective-permute-start | bytes 393224 | tf_op jit(solution)/shard_map/ppermute | solution.py:22
  86.1 17.1 %collective-permute-start.16 = (f32[8,4,8,128]{3,2,1,0:T(8,128)S(1)}, f32[8,4,8,128]{3,2,1,0:T(8,128)S(1)}, u32[]{:S(2)}, u32[]{:S(2)}) collective-permute-start(f32[8,4,8,128]{3,2,1,0:T(8,128)S(1)} %get-tuple-element.44), channel_id=1, source_target_pairs={{0,5},{1,4},{2,7},{3,6},{4,1},{5,0},{6,3},{7,2},{8,13},{9,12},{10,... | collective-permute-start | bytes 393224 | tf_op jit(solution)/shard_map/ppermute | solution.py:22
  89.7 15.6 %collective-permute-start.19 = (f32[8,4,8,128]{3,2,1,0:T(8,128)S(1)}, f32[8,4,8,128]{3,2,1,0:T(8,128)S(1)}, u32[]{:S(2)}, u32[]{:S(2)}) collective-permute-start(f32[8,4,8,128]{3,2,1,0:T(8,128)S(1)} %get-tuple-element.48), channel_id=1, source_target_pairs={{0,7},{1,6},{2,5},{3,4},{4,3},{5,2},{6,1},{7,0},{8,15},{9,14},{10,... | collective-permute-start | bytes 393224 | tf_op jit(solution)/shard_map/ppermute | solution.py:22
  89.7 16.9 %collective-permute-start.8 = (f32[8,4,8,128]{3,2,1,0:T(8,128)S(1)}, f32[8,4,8,128]{3,2,1,0:T(8,128)S(1)}, u32[]{:S(2)}, u32[]{:S(2)}) collective-permute-start(f32[8,4,8,128]{3,2,1,0:T(8,128)S(1)} %get-tuple-element.36), channel_id=1, source_target_pairs={{0,1},{1,0},{2,3},{3,2},{4,5},{5,4},{6,7},{7,6},{8,9},{9,8},{10,11... | collective-permute-start | bytes 393224 | tf_op jit(solution)/shard_map/ppermute | solution.py:22
  93.2 15.0 %collective-permute-start.10 = (f32[8,4,8,128]{3,2,1,0:T(8,128)S(1)}, f32[8,4,8,128]{3,2,1,0:T(8,128)S(1)}, u32[]{:S(2)}, u32[]{:S(2)}) collective-permute-start(f32[8,4,8,128]{3,2,1,0:T(8,128)S(1)} %get-tuple-element.38), channel_id=1, source_target_pairs={{0,2},{1,3},{2,0},{3,1},{4,6},{5,7},{6,4},{7,5},{8,10},{9,11},{10,... | collective-permute-start | bytes 393224 | tf_op jit(solution)/shard_map/ppermute | solution.py:22
  95.1 14.6 %collective-permute-start.11 = (f32[8,4,8,128]{3,2,1,0:T(8,128)S(1)}, f32[8,4,8,128]{3,2,1,0:T(8,128)S(1)}, u32[]{:S(2)}, u32[]{:S(2)}) collective-permute-start(f32[8,4,8,128]{3,2,1,0:T(8,128)S(1)} %get-tuple-element.39), channel_id=1, source_target_pairs={{0,2},{1,3},{2,0},{3,1},{4,6},{5,7},{6,4},{7,5},{8,10},{9,11},{10,... | collective-permute-start | bytes 393224 | tf_op jit(solution)/shard_map/ppermute | solution.py:22
  103.2 8.7 %collective-permute-start.13 = (f32[8,4,8,128]{3,2,1,0:T(8,128)S(1)}, f32[8,4,8,128]{3,2,1,0:T(8,128)S(1)}, u32[]{:S(2)}, u32[]{:S(2)}) collective-permute-start(f32[8,4,8,128]{3,2,1,0:T(8,128)S(1)} %get-tuple-element.41), channel_id=1, source_target_pairs={{0,3},{1,2},{2,1},{3,0},{4,7},{5,6},{6,5},{7,4},{8,11},{9,10},{10,... | collective-permute-start | bytes 393224 | tf_op jit(solution)/shard_map/ppermute | solution.py:22
  105.4 15.8 %collective-permute-start.15 = (f32[8,4,8,128]{3,2,1,0:T(8,128)S(1)}, f32[8,4,8,128]{3,2,1,0:T(8,128)S(1)}, u32[]{:S(2)}, u32[]{:S(2)}) collective-permute-start(f32[8,4,8,128]{3,2,1,0:T(8,128)S(1)} %get-tuple-element.43), channel_id=1, source_target_pairs={{0,4},{1,5},{2,6},{3,7},{4,0},{5,1},{6,2},{7,3},{8,12},{9,13},{10,... | collective-permute-start | bytes 393224 | tf_op jit(solution)/shard_map/ppermute | solution.py:22
  106.6 17.3 %collective-permute-start.17 = (f32[8,4,8,128]{3,2,1,0:T(8,128)S(1)}, f32[8,4,8,128]{3,2,1,0:T(8,128)S(1)}, u32[]{:S(2)}, u32[]{:S(2)}) collective-permute-start(f32[8,4,8,128]{3,2,1,0:T(8,128)S(1)} %get-tuple-element.45), channel_id=1, source_target_pairs={{0,5},{1,4},{2,7},{3,6},{4,1},{5,0},{6,3},{7,2},{8,13},{9,12},{10,... | collective-permute-start | bytes 393224 | tf_op jit(solution)/shard_map/ppermute | solution.py:22
  108.2 20.9 %collective-permute-start.18 = (f32[8,4,8,128]{3,2,1,0:T(8,128)S(1)}, f32[8,4,8,128]{3,2,1,0:T(8,128)S(1)}, u32[]{:S(2)}, u32[]{:S(2)}) collective-permute-start(f32[8,4,8,128]{3,2,1,0:T(8,128)S(1)} %get-tuple-element.47), channel_id=1, source_target_pairs={{0,6},{1,7},{2,4},{3,5},{4,2},{5,3},{6,0},{7,1},{8,14},{9,15},{10,... | collective-permute-start | bytes 393224 | tf_op jit(solution)/shard_map/ppermute | solution.py:22
  109.7 20.0 %collective-permute-start.20 = (f32[8,4,8,128]{3,2,1,0:T(8,128)S(1)}, f32[8,4,8,128]{3,2,1,0:T(8,128)S(1)}, u32[]{:S(2)}, u32[]{:S(2)}) collective-permute-start(f32[8,4,8,128]{3,2,1,0:T(8,128)S(1)} %get-tuple-element.49), channel_id=1, source_target_pairs={{0,7},{1,6},{2,5},{3,4},{4,3},{5,2},{6,1},{7,0},{8,15},{9,14},{10,... | collective-permute-start | bytes 393224 | tf_op jit(solution)/shard_map/ppermute | solution.py:22
  111.9 17.7 %collective-permute-start.9 = (f32[8,4,8,128]{3,2,1,0:T(8,128)S(1)}, f32[8,4,8,128]{3,2,1,0:T(8,128)S(1)}, u32[]{:S(2)}, u32[]{:S(2)}) collective-permute-start(f32[8,4,8,128]{3,2,1,0:T(8,128)S(1)} %get-tuple-element.37), channel_id=1, source_target_pairs={{0,1},{1,0},{2,3},{3,2},{4,5},{5,4},{6,7},{7,6},{8,9},{9,8},{10,11... | collective-permute-start | bytes 393224 | tf_op jit(solution)/shard_map/ppermute | solution.py:22
  132.2 1.9 %collective-permute-start.21 = (f32[64,128]{1,0:T(8,128)S(1)}, f32[64,128]{1,0:T(8,128)S(1)}, u32[]{:S(2)}, u32[]{:S(2)}) collective-permute-start(f32[64,128]{1,0:T(8,128)S(1)} %get-tuple-element.51), channel_id=1, source_target_pairs={{0,1},{1,0},{2,3},{3,2},{4,5},{5,4},{6,7},{7,6},{8,9},{9,8},{10,11... | collective-permute-start | bytes 98312 | tf_op jit(solution)/shard_map/ppermute | solution.py:22
  134.1 3.9 %collective-permute-start.22 = (f32[64,128]{1,0:T(8,128)S(1)}, f32[64,128]{1,0:T(8,128)S(1)}, u32[]{:S(2)}, u32[]{:S(2)}) collective-permute-start(f32[64,128]{1,0:T(8,128)S(1)} %add.33), channel_id=1, source_target_pairs={{0,2},{1,3},{2,0},{3,1},{4,6},{5,7},{6,4},{7,5},{8,10},{9,11},{10,... | collective-permute-start | bytes 98312 | tf_op jit(solution)/shard_map/ppermute | solution.py:22
  138.1 8.0 %collective-permute-start.23 = (f32[64,128]{1,0:T(8,128)S(1)}, f32[64,128]{1,0:T(8,128)S(1)}, u32[]{:S(2)}, u32[]{:S(2)}) collective-permute-start(f32[64,128]{1,0:T(8,128)S(1)} %add.34), channel_id=1, source_target_pairs={{0,128},{1,129},{2,130},{3,131},{4,132},{5,133},{6,134},{7,135},{8... | collective-permute-start | bytes 98312 | tf_op jit(solution)/shard_map/ppermute | solution.py:294
  138.1 8.0 %collective-permute-start.24 = (f32[64,128]{1,0:T(8,128)S(1)}, f32[64,128]{1,0:T(8,128)S(1)}, u32[]{:S(2)}, u32[]{:S(2)}) collective-permute-start(f32[64,128]{1,0:T(8,128)S(1)} %add.34), channel_id=1, source_target_pairs={{0,4},{1,5},{2,6},{3,7},{4,128},{5,129},{6,130},{7,131},{8,12},{9,... | collective-permute-start | bytes 98312 | tf_op jit(solution)/shard_map/ppermute | solution.py:294
  138.2 8.3 %collective-permute-start.25 = (f32[64,128]{1,0:T(8,128)S(1)}, f32[64,128]{1,0:T(8,128)S(1)}, u32[]{:S(2)}, u32[]{:S(2)}) collective-permute-start(f32[64,128]{1,0:T(8,128)S(1)} %add.34), channel_id=1, source_target_pairs={{0,132},{1,133},{2,134},{3,135},{4,0},{5,1},{6,2},{7,3},{8,140},{9... | collective-permute-start | bytes 98312 | tf_op jit(solution)/shard_map/ppermute | solution.py:294
  146.5 5.2 %collective-permute-start.26 = (f32[64,128]{1,0:T(8,128)S(1)}, f32[64,128]{1,0:T(8,128)S(1)}, u32[]{:S(2)}, u32[]{:S(2)}) collective-permute-start(f32[64,128]{1,0:T(8,128)S(1)} %add_add_fusion.2), channel_id=1, source_target_pairs={{0,8},{8,16},{16,24},{24,0},{32,40},{40,48},{48,56},{56,32},{64,72... | collective-permute-start | bytes 98312 | tf_op jit(solution)/shard_map/ppermute | solution.py:22
  146.6 5.5 %collective-permute-start.27 = (f32[64,128]{1,0:T(8,128)S(1)}, f32[64,128]{1,0:T(8,128)S(1)}, u32[]{:S(2)}, u32[]{:S(2)}) collective-permute-start(f32[64,128]{1,0:T(8,128)S(1)} %add_add_fusion.2), channel_id=1, source_target_pairs={{0,16},{8,24},{16,0},{24,8},{32,48},{40,56},{48,32},{56,40},{64,80... | collective-permute-start | bytes 98312 | tf_op jit(solution)/shard_map/ppermute | solution.py:22
  146.7 6.2 %collective-permute-start.28 = (f32[64,128]{1,0:T(8,128)S(1)}, f32[64,128]{1,0:T(8,128)S(1)}, u32[]{:S(2)}, u32[]{:S(2)}) collective-permute-start(f32[64,128]{1,0:T(8,128)S(1)} %add_add_fusion.2), channel_id=1, source_target_pairs={{0,24},{8,0},{16,8},{24,16},{32,56},{40,32},{48,40},{56,48},{64,88... | collective-permute-start | bytes 98312 | tf_op jit(solution)/shard_map/ppermute | solution.py:22
  152.9 5.2 %collective-permute-start.29 = (f32[64,128]{1,0:T(8,128)S(1)}, f32[64,128]{1,0:T(8,128)S(1)}, u32[]{:S(2)}, u32[]{:S(2)}) collective-permute-start(f32[64,128]{1,0:T(8,128)S(1)} %add_add_fusion.1), channel_id=1, source_target_pairs={{0,32},{8,40},{16,48},{24,56},{32,64},{40,72},{48,80},{56,88},{64,... | collective-permute-start | bytes 98312 | tf_op jit(solution)/shard_map/ppermute | solution.py:22
  153.0 5.5 %collective-permute-start.30 = (f32[64,128]{1,0:T(8,128)S(1)}, f32[64,128]{1,0:T(8,128)S(1)}, u32[]{:S(2)}, u32[]{:S(2)}) collective-permute-start(f32[64,128]{1,0:T(8,128)S(1)} %add_add_fusion.1), channel_id=1, source_target_pairs={{0,64},{8,72},{16,80},{24,88},{32,96},{40,104},{48,112},{56,120},{... | collective-permute-start | bytes 98312 | tf_op jit(solution)/shard_map/ppermute | solution.py:22
  155.5 3.9 %collective-permute-start.31 = (f32[64,128]{1,0:T(8,128)S(1)}, f32[64,128]{1,0:T(8,128)S(1)}, u32[]{:S(2)}, u32[]{:S(2)}) collective-permute-start(f32[64,128]{1,0:T(8,128)S(1)} %add_add_fusion.1), channel_id=1, source_target_pairs={{0,96},{8,104},{16,112},{24,120},{32,0},{40,8},{48,16},{56,24},{64... | collective-permute-start | bytes 98312 | tf_op jit(solution)/shard_map/ppermute | solution.py:22
  159.4 1.5 collective-permute-start.32

commit v9 on v8

--- a/solution.py
+++ b/solution.py
@@ -10,7 +10,7 @@
 
 DEPTH = 3
 TIED = True
-EARLY = (6,)
+EARLY = (1,)
 PANEL = 32
 SIDE = 4
 SHARES = (8, 4, 4)

time: 170 us -> 173 us (1.018)
  waiting for transfers between devices: 79.3 us -> 89.9 us
  starting transfers between devices: 68.4 us -> 59.4 us
    ppermute x23, waiting for transfers between devices: 31.2 us -> 42.1 us  [permuted(): return lax.ppermute(block, axis, [(i, target(i)) for i in range(count)])]
    ppermute x23, starting transfers between devices: 42.1 us -> 32.8 us  [permuted(): return lax.ppermute(block, axis, [(i, target(i)) for i in range(count)])]
  transfers between devices with their start and end apart: 33 -> 33, of which waited for: 18 -> 21; matrix products, arithmetic and copies ran while one was open for 0% -> 0% of each run, Pallas kernels for 4% -> 4%
where the time goes in v9:
time: 173 us; the launch traced here: 170 us
  waiting for transfers between devices  89.9 us (52%)
  starting transfers between devices  59.4 us (34%)
  Pallas kernels  17.2 us (10%)
  other arithmetic  2.23 us (1%)
    ppermute x23, waiting for transfers between devices, permuted(): return lax.ppermute(block, axis, [(i, target(i)) for i in range(count)])  42.1 us
    ppermute x23, starting transfers between devices, permuted(): return lax.ppermute(block, axis, [(i, target(i)) for i in range(count)])  32.8 us
    ppermute x1, waiting for transfers between devices, halos(): seams = [lax.ppermute(blocks[0], 'domain', seam_pairs())]  32.7 us
    ppermute x2, waiting for transfers between devices, halos(): lax.ppermute(block, 'domain', out)  11.2 us
    ppermute x1, starting transfers between devices, halos(): seams = [lax.ppermute(blocks[0], 'domain', seam_pairs())]  10.9 us
    pallas_call x2, Pallas kernels, filtered_stripes(): pl.pallas_call(functools.partial(filter_kernel, begin, shares, stripes),...  6.72 us
    ppermute x1, starting transfers between devices, halos(): low = lax.ppermute(both[:, planes - DEPTH:], 'domain', inner_pairs(1))  4.65 us
    ppermute x3, starting transfers between devices, along_z(): return lax.ppermute(block, ('domain', 'band'), pairs)  4.53 us
  transfers between devices with their start and end apart: 33, of which 21 were waited for; matrix products, arithmetic and copies ran while one was open for 0% of the time, Pallas kernels for 4%

profile of v9, /device:TPU:32, one launch (start us, length us, event | category | flops | bytes accessed | tf_op | source)
XLA Modules:
  0.0 170.5 jit_solution(8103929724666837967)
XLA Ops:
  0.0 1.6 slice_select_fusion
  1.6 0.4 copy-done.1
  2.1 0.1 slice_select_fusion.1
  2.1 0.8 copy-done
  3.0 0.1 pad_maximum_fusion.1
  3.1 0.4 pad_maximum_fusion
  3.5 1.3 collective-permute-start.1
  4.8 4.7 %collective-permute-start = (f32[17,3,64,128]{3,2,1,0:T(8,128)S(1)}, f32[17,3,64,128]{3,2,1,0:T(8,128)S(1)}, u32[]{:S(2)}, u32[]{:S(2)}) collective-permute-start(f32[17,3,64,128]{3,2,1,0:T(8,128)S(1)} %get-tuple-element.54), channel_id=1, source_target_pairs={{0,8},{8,16},{16,24},{24,32},{32,40},{40,48},{48,56},{56,64},{64,7... | collective-permute-start | bytes 5013512 | tf_op jit(solution)/shard_map/ppermute | solution.py:141
  9.4 10.9 %collective-permute-start.2 = (f32[9,3,64,128]{3,2,1,0:T(8,128)S(1)}, f32[9,3,64,128]{3,2,1,0:T(8,128)S(1)}, u32[]{:S(2)}, u32[]{:S(2)}) collective-permute-start(f32[9,3,64,128]{3,2,1,0:T(8,128)S(1)} %pad_maximum_fusion.1), channel_id=1, source_target_pairs={{120,128},{0,248},{248,0},{128,120},{121,129},{1,249},{249,1},{129... | collective-permute-start | bytes 2654216 | tf_op jit(solution)/shard_map/ppermute | solution.py:135
  20.4 1.3 collective-permute-start.3
  21.7 1.3 collective-permute-start.5
  23.0 0.1 fusion.1
  23.2 11.2 %collective-permute-done.3 = f32[4,3,64,128]{3,2,1,0:T(8,128)S(1)} collective-permute-done((f32[4,3,64,128]{3,2,1,0:T(8,128)S(1)}, f32[4,3,64,128]{3,2,1,0:T(8,128)S(1)}, u32[]{:S(2)}, u32[]{:S(2)}) %collective-permute-start.3) | collective-permute-done | bytes 393248 | tf_op jit(solution)/shard_map/ppermute | solution.py:138
  34.4 1.3 collective-permute-start.4
  35.7 1.3 collective-permute-start.6
  37.0 32.7 %collective-permute-done.2.rest_0_ = f32[9,3,64,128]{3,2,1,0:T(8,128)S(1)} collective-permute-done((f32[9,3,64,128]{3,2,1,0:T(8,128)S(1)}, f32[9,3,64,128]{3,2,1,0:T(8,128)S(1)}, u32[]{:S(2)}, u32[]{:S(2)}) %collective-permute-start.2) | collective-permute-done | bytes 884768 | tf_op jit(solution)/shard_map/ppermute | solution.py:135
  69.7 0.0 collective-permute-done.1.high
  69.7 0.0 collective-permute-done.low
  69.8 3.4 %shard_map.28 = (f32[8,4,8,128]{3,2,1,0:T(8,128)S(1)}, f32[8,4,8,128]{3,2,1,0:T(8,128)S(1)}, f32[8,4,8,128]{3,2,1,0:T(8,128)S(1)}, f32[8,4,8,128]{3,2,1,0:T(8,12...) custom-call(f32[8,4,64,128]{3,2,1,0:T(8,128)S(1)} %get-tuple-element, ...), custom_call_target="tpu_custom_call" | custom-call | tf_op jit(solution)/shard_map/pallas_call | solution.py:81
  73.2 0.1 collective-permute-start.7
  73.3 1.2 collective-permute-start.11
  74.5 11.6 %collective-permute-start.13 = (f32[8,4,8,128]{3,2,1,0:T(8,128)S(1)}, f32[8,4,8,128]{3,2,1,0:T(8,128)S(1)}, u32[]{:S(2)}, u32[]{:S(2)}) collective-permute-start(f32[8,4,8,128]{3,2,1,0:T(8,128)S(1)} %get-tuple-element.42), channel_id=1, source_target_pairs={{0,4},{1,5},{2,6},{3,7},{4,0},{5,1},{6,2},{7,3},{8,12},{9,13},{10,... | collective-permute-start | bytes 393224 | tf_op jit(solution)/shard_map/ppermute | solution.py:22
  86.1 0.0 collective-permute-start.15
  86.1 2.8 %collective-permute-start.17 = (f32[8,4,8,128]{3,2,1,0:T(8,128)S(1)}, f32[8,4,8,128]{3,2,1,0:T(8,128)S(1)}, u32[]{:S(2)}, u32[]{:S(2)}) collective-permute-start(f32[8,4,8,128]{3,2,1,0:T(8,128)S(1)} %get-tuple-element.46), channel_id=1, source_target_pairs={{0,6},{1,7},{2,4},{3,5},{4,2},{5,3},{6,0},{7,1},{8,14},{9,15},{10,... | collective-permute-start | bytes 393224 | tf_op jit(solution)/shard_map/ppermute | solution.py:22
  88.9 0.4 collective-permute-start.19
  89.3 3.3 %shard_map.29 = (f32[8,4,8,128]{3,2,1,0:T(8,128)S(1)}, f32[8,4,8,128]{3,2,1,0:T(8,128)S(1)}, f32[8,4,8,128]{3,2,1,0:T(8,128)S(1)}, f32[8,4,8,128]{3,2,1,0:T(8,12...) custom-call(f32[8,4,64,128]{3,2,1,0:T(8,128)S(1)} %get-tuple-element, ...), custom_call_target="tpu_custom_call" | custom-call | tf_op jit(solution)/shard_map/pallas_call | solution.py:81
  92.7 2.1 %collective-permute-start.9 = (f32[8,4,8,128]{3,2,1,0:T(8,128)S(1)}, f32[8,4,8,128]{3,2,1,0:T(8,128)S(1)}, u32[]{:S(2)}, u32[]{:S(2)}) collective-permute-start(f32[8,4,8,128]{3,2,1,0:T(8,128)S(1)} %get-tuple-element.38), channel_id=1, source_target_pairs={{0,2},{1,3},{2,0},{3,1},{4,6},{5,7},{6,4},{7,5},{8,10},{9,11},{10,... | collective-permute-start | bytes 393224 | tf_op jit(solution)/shard_map/ppermute | solution.py:22
  94.8 6.5 %collective-permute-done.13 = f32[8,4,8,128]{3,2,1,0:T(8,128)S(1)} collective-permute-done((f32[8,4,8,128]{3,2,1,0:T(8,128)S(1)}, f32[8,4,8,128]{3,2,1,0:T(8,128)S(1)}, u32[]{:S(2)}, u32[]{:S(2)}) %collective-permute-start.13) | collective-permute-done | bytes 131104 | tf_op jit(solution)/shard_map/ppermute | solution.py:22
  101.3 2.0 %collective-permute-start.10 = (f32[8,4,8,128]{3,2,1,0:T(8,128)S(1)}, f32[8,4,8,128]{3,2,1,0:T(8,128)S(1)}, u32[]{:S(2)}, u32[]{:S(2)}) collective-permute-start(f32[8,4,8,128]{3,2,1,0:T(8,128)S(1)} %get-tuple-element.39), channel_id=1, source_target_pairs={{0,2},{1,3},{2,0},{3,1},{4,6},{5,7},{6,4},{7,5},{8,10},{9,11},{10,... | collective-permute-start | bytes 393224 | tf_op jit(solution)/shard_map/ppermute | solution.py:22
  103.2 0.8 collective-permute-done.15
  104.1 1.4 collective-permute-start.12
  105.5 1.8 %collective-permute-done.17 = f32[8,4,8,128]{3,2,1,0:T(8,128)S(1)} collective-permute-done((f32[8,4,8,128]{3,2,1,0:T(8,128)S(1)}, f32[8,4,8,128]{3,2,1,0:T(8,128)S(1)}, u32[]{:S(2)}, u32[]{:S(2)}) %collective-permute-start.17) | collective-permute-done | bytes 131104 | tf_op jit(solution)/shard_map/ppermute | solution.py:22
  107.3 2.6 %collective-permute-done.19 = f32[8,4,8,128]{3,2,1,0:T(8,128)S(1)} collective-permute-done((f32[8,4,8,128]{3,2,1,0:T(8,128)S(1)}, f32[8,4,8,128]{3,2,1,0:T(8,128)S(1)}, u32[]{:S(2)}, u32[]{:S(2)}) %collective-permute-start.19) | collective-permute-done | bytes 131104 | tf_op jit(solution)/shard_map/ppermute | solution.py:22
  109.9 1.0 collective-permute-start.18
  111.0 2.1 %collective-permute-start.20 = (f32[8,4,8,128]{3,2,1,0:T(8,128)S(1)}, f32[8,4,8,128]{3,2,1,0:T(8,128)S(1)}, u32[]{:S(2)}, u32[]{:S(2)}) collective-permute-start(f32[8,4,8,128]{3,2,1,0:T(8,128)S(1)} %get-tuple-element.49), channel_id=1, source_target_pairs={{0,7},{1,6},{2,5},{3,4},{4,3},{5,2},{6,1},{7,0},{8,15},{9,14},{10,... | collective-permute-start | bytes 393224 | tf_op jit(solution)/shard_map/ppermute | solution.py:22
  113.1 0.3 collective-permute-start.8
  113.4 10.3 %collective-permute-done.14 = f32[8,4,8,128]{3,2,1,0:T(8,128)S(1)} collective-permute-done((f32[8,4,8,128]{3,2,1,0:T(8,128)S(1)}, f32[8,4,8,128]{3,2,1,0:T(8,128)S(1)}, u32[]{:S(2)}, u32[]{:S(2)}) %collective-permute-start.14) | collective-permute-done | bytes 131104 | tf_op jit(solution)/shard_map/ppermute | solution.py:22
  123.7 2.8 %collective-permute-done.16 = f32[8,4,8,128]{3,2,1,0:T(8,128)S(1)} collective-permute-done((f32[8,4,8,128]{3,2,1,0:T(8,128)S(1)}, f32[8,4,8,128]{3,2,1,0:T(8,128)S(1)}, u32[]{:S(2)}, u32[]{:S(2)}) %collective-permute-start.16) | collective-permute-done | bytes 131104 | tf_op jit(solution)/shard_map/ppermute | solution.py:22
  126.5 4.0 %collective-permute-done.18 = f32[8,4,8,128]{3,2,1,0:T(8,128)S(1)} collective-permute-done((f32[8,4,8,128]{3,2,1,0:T(8,128)S(1)}, f32[8,4,8,128]{3,2,1,0:T(8,128)S(1)}, u32[]{:S(2)}, u32[]{:S(2)}) %collective-permute-start.18) | collective-permute-done | bytes 131104 | tf_op jit(solution)/shard_map/ppermute | solution.py:22
  130.6 1.1 collective-permute-done.20
  131.7 2.6 %shard_map.30 = (f32[128,4096]{1,0:T(8,128)S(1)}, f32[64,128]{1,0:T(8,128)S(1)}, f32[64,128]{1,0:T(8,128)S(1)}) custom-call(f32[256,128]{1,0:T(8,128)S(1)} %bitcast.26, f32[256,128]{1,0:T(8,128)S(1)} %bitcast.33, f32[256,128]{1,0:T(8,128)S(1)} %bitcast.27, f32[256,128]{1,0:T(8,128)S(1)} %bitcast.41, f32[256,128]{1,0:T(8,128)S(1)} %bitcast.34, ...), custom_call_target="tpu_custom_call" | custom-call | tf_op jit(solution)/shard_map/pallas_call | solution.py:186
  134.3 0.8 collective-permute-start.21
  135.0 0.9 collective-permute-done.21
  135.9 3.9 %collective-permute-done.22 = f32[64,128]{1,0:T(8,128)S(1)} collective-permute-done((f32[64,128]{1,0:T(8,128)S(1)}, f32[64,128]{1,0:T(8,128)S(1)}, u32[]{:S(2)}, u32[]{:S(2)}) %collective-permute-start.22) | collective-permute-done | bytes 32800 | tf_op jit(solution)/shard_map/ppermute | solution.py:22
  139.8 1.0 collective-permute-start.24
  140.9 3.5 %collective-permute-start.25 = (f32[64,128]{1,0:T(8,128)S(1)}, f32[64,128]{1,0:T(8,128)S(1)}, u32[]{:S(2)}, u32[]{:S(2)}) collective-permute-start(f32[64,128]{1,0:T(8,128)S(1)} %add.34), channel_id=1, source_target_pairs={{0,132},{1,133},{2,134},{3,135},{4,0},{5,1},{6,2},{7,3},{8,140},{9... | collective-permute-start | bytes 98312 | tf_op jit(solution)/shard_map/ppermute | solution.py:294
  144.3 3.3 %collective-permute-done.23 = f32[64,128]{1,0:T(8,128)S(1)} collective-permute-done((f32[64,128]{1,0:T(8,128)S(1)}, f32[64,128]{1,0:T(8,128)S(1)}, u32[]{:S(2)}, u32[]{:S(2)}) %collective-permute-start.23) | collective-permute-done | bytes 32800 | tf_op jit(solution)/shard_map/ppermute | solution.py:294
  147.6 0.6 collective-permute-done.25
  148.2 0.1 collective-permute-start.26
  148.3 0.1 collective-permute-start.27
  148.4 3.1 %collective-permute-start.28 = (f32[64,128]{1,0:T(8,128)S(1)}, f32[64,128]{1,0:T(8,128)S(1)}, u32[]{:S(2)}, u32[]{:S(2)}) collective-permute-start(f32[64,128]{1,0:T(8,128)S(1)} %add_add_fusion.2), channel_id=1, source_target_pairs={{0,24},{8,0},{16,8},{24,16},{32,56},{40,32},{48,40},{56,48},{64,88... | collective-permute-start | bytes 98312 | tf_op jit(solution)/shard_map/ppermute | solution.py:22
  151.5 1.9 %collective-permute-done.26 = f32[64,128]{1,0:T(8,128)S(1)} collective-permute-done((f32[64,128]{1,0:T(8,128)S(1)}, f32[64,128]{1,0:T(8,128)S(1)}, u32[]{:S(2)}, u32[]{:S(2)}) %collective-permute-start.26) | collective-permute-done | bytes 32800 | tf_op jit(solution)/shard_map/ppermute | solution.py:22
  153.4 0.4 collective-permute-done.27
  153.8 0.8 collective-permute-done.28
  154.6 0.1 collective-permute-start.29
  154.7 2.4 %collective-permute-start.30 = (f32[64,128]{1,0:T(8,128)S(1)}, f32[64,128]{1,0:T(8,128)S(1)}, u32[]{:S(2)}, u32[]{:S(2)}) collective-permute-start(f32[64,128]{1,0:T(8,128)S(1)} %add_add_fusion.1), channel_id=1, source_target_pairs={{0,64},{8,72},{16,80},{24,88},{32,96},{40,104},{48,112},{56,120},{... | collective-permute-start | bytes 98312 | tf_op jit(solution)/shard_map/ppermute | solution.py:22
  157.1 0.8 collective-permute-start.31
  157.9 1.9 %collective-permute-done.29 = f32[64,128]{1,0:T(8,128)S(1)} collective-permute-done((f32[64,128]{1,0:T(8,128)S(1)}, f32[64,128]{1,0:T(8,128)S(1)}, u32[]{:S(2)}, u32[]{:S(2)}) %collective-permute-start.29) | collective-permute-done | bytes 32800 | tf_op jit(solution)/shard_map/ppermute | solution.py:22
  159.8 0.4 collective-permute-done.30
  160.2 0.8 collective-permute-done.31
  161.1 0.3 collective-permute-start.32
  161.4 1.2 collective-permute-done.32.other
  162.6 4.2 %shard_map.31.inverse = f32[128,128]{1,0:T(8,128)S(1)} custom-call(f32[64,128]{1,0:T(8,128)S(1)} %add_add_fusion.own, f32[64,128]{1,0:T(8,128)S(1)} %collective-permute-done.32.other), custom_call_target="tpu_custom_call" | custom-call | tf_op jit(solution)/shard_map/pallas_call | solution.py:243
  166.7 3.7 %shard_map.32 = f32[128,4,8,128]{3,2,1,0:T(8,128)} custom-call(f32[128,128]{1,0:T(8,128)S(1)} %shard_map.31.inverse, f32[128,4096]{1,0:T(8,128)S(1)} %get-tuple-element.52.flat), custom_call_target="tpu_custom_call" | custom-call | tf_op jit(solution)/shard_map/pallas_call | solution.py:270
  (25 shorter events, 0.1 us)
Async XLA Ops:
  0.0 2.1 %copy-start.1 = (f32[16,4,64,128]{3,2,1,0:T(8,128)S(1)}, f32[16,4,64,128]{3,2,1,0:T(8,128)}, u32[]{:S(2)}) copy-start(f32[16,4,64,128]{3,2,1,0:T(8,128)} %param.2) | copy-start | bytes 6291460
  2.1 0.9 copy-start
  3.5 66.2 %collective-permute-start.1 = (f32[17,3,64,128]{3,2,1,0:T(8,128)S(1)}, f32[17,3,64,128]{3,2,1,0:T(8,128)S(1)}, u32[]{:S(2)}, u32[]{:S(2)}) collective-permute-start(f32[17,3,64,128]{3,2,1,0:T(8,128)S(1)} %get-tuple-element.53), channel_id=1, source_target_pairs={{8,0},{16,8},{24,16},{32,24},{40,32},{48,40},{56,48},{64,56},{72,6... | collective-permute-start | bytes 5013512 | tf_op jit(solution)/shard_map/ppermute | solution.py:142
  4.8 65.0 %collective-permute-start = (f32[17,3,64,128]{3,2,1,0:T(8,128)S(1)}, f32[17,3,64,128]{3,2,1,0:T(8,128)S(1)}, u32[]{:S(2)}, u32[]{:S(2)}) collective-permute-start(f32[17,3,64,128]{3,2,1,0:T(8,128)S(1)} %get-tuple-element.54), channel_id=1, source_target_pairs={{0,8},{8,16},{16,24},{24,32},{32,40},{40,48},{48,56},{56,64},{64,7... | collective-permute-start | bytes 5013512 | tf_op jit(solution)/shard_map/ppermute | solution.py:141
  9.4 60.3 %collective-permute-start.2 = (f32[9,3,64,128]{3,2,1,0:T(8,128)S(1)}, f32[9,3,64,128]{3,2,1,0:T(8,128)S(1)}, u32[]{:S(2)}, u32[]{:S(2)}) collective-permute-start(f32[9,3,64,128]{3,2,1,0:T(8,128)S(1)} %pad_maximum_fusion.1), channel_id=1, source_target_pairs={{120,128},{0,248},{248,0},{128,120},{121,129},{1,249},{249,1},{129... | collective-permute-start | bytes 2654216 | tf_op jit(solution)/shard_map/ppermute | solution.py:135
  20.4 14.0 %collective-permute-start.3 = (f32[4,3,64,128]{3,2,1,0:T(8,128)S(1)}, f32[4,3,64,128]{3,2,1,0:T(8,128)S(1)}, u32[]{:S(2)}, u32[]{:S(2)}) collective-permute-start(f32[4,3,64,128]{3,2,1,0:T(8,128)S(1)} %get-tuple-element.58), channel_id=1, source_target_pairs={{120,24},{0,96},{248,152},{128,224},{121,25},{1,97},{249,153},{129... | collective-permute-start | bytes 1179656 | tf_op jit(solution)/shard_map/ppermute | solution.py:138
  21.7 14.0 %collective-permute-start.5 = (f32[4,3,64,128]{3,2,1,0:T(8,128)S(1)}, f32[4,3,64,128]{3,2,1,0:T(8,128)S(1)}, u32[]{:S(2)}, u32[]{:S(2)}) collective-permute-start(f32[4,3,64,128]{3,2,1,0:T(8,128)S(1)} %get-tuple-element.57), channel_id=1, source_target_pairs={{120,88},{0,32},{248,216},{128,160},{121,89},{1,33},{249,217},{129... | collective-permute-start | bytes 1179656 | tf_op jit(solution)/shard_map/ppermute | solution.py:138
  34.4 51.7 %collective-permute-start.4 = (f32[4,3,64,128]{3,2,1,0:T(8,128)S(1)}, f32[4,3,64,128]{3,2,1,0:T(8,128)S(1)}, u32[]{:S(2)}, u32[]{:S(2)}) collective-permute-start(f32[4,3,64,128]{3,2,1,0:T(8,128)S(1)} %collective-permute-done.3), channel_id=1, source_target_pairs={{24,128},{96,248},{152,0},{224,120},{25,129},{97,249},{153,1},{225... | collective-permute-start | bytes 1179656 | tf_op jit(solution)/shard_map/ppermute | solution.py:138
  35.7 50.4 %collective-permute-start.6 = (f32[4,3,64,128]{3,2,1,0:T(8,128)S(1)}, f32[4,3,64,128]{3,2,1,0:T(8,128)S(1)}, u32[]{:S(2)}, u32[]{:S(2)}) collective-permute-start(f32[4,3,64,128]{3,2,1,0:T(8,128)S(1)} %collective-permute-done.5), channel_id=1, source_target_pairs={{88,128},{32,248},{216,0},{160,120},{89,129},{33,249},{217,1},{161... | collective-permute-start | bytes 1179656 | tf_op jit(solution)/shard_map/ppermute | solution.py:138
  73.2 15.8 %collective-permute-start.7 = (f32[8,4,8,128]{3,2,1,0:T(8,128)S(1)}, f32[8,4,8,128]{3,2,1,0:T(8,128)S(1)}, u32[]{:S(2)}, u32[]{:S(2)}) collective-permute-start(f32[8,4,8,128]{3,2,1,0:T(8,128)S(1)} %get-tuple-element.32), channel_id=1, source_target_pairs={{0,1},{1,0},{2,3},{3,2},{4,5},{5,4},{6,7},{7,6},{8,9},{9,8},{10,11... | collective-permute-start | bytes 393224 | tf_op jit(solution)/shard_map/ppermute | solution.py:22
  73.3 19.4 %collective-permute-start.11 = (f32[8,4,8,128]{3,2,1,0:T(8,128)S(1)}, f32[8,4,8,128]{3,2,1,0:T(8,128)S(1)}, u32[]{:S(2)}, u32[]{:S(2)}) collective-permute-start(f32[8,4,8,128]{3,2,1,0:T(8,128)S(1)} %get-tuple-element.40), channel_id=1, source_target_pairs={{0,3},{1,2},{2,1},{3,0},{4,7},{5,6},{6,5},{7,4},{8,11},{9,10},{10,... | collective-permute-start | bytes 393224 | tf_op jit(solution)/shard_map/ppermute | solution.py:22
  74.5 26.8 %collective-permute-start.13 = (f32[8,4,8,128]{3,2,1,0:T(8,128)S(1)}, f32[8,4,8,128]{3,2,1,0:T(8,128)S(1)}, u32[]{:S(2)}, u32[]{:S(2)}) collective-permute-start(f32[8,4,8,128]{3,2,1,0:T(8,128)S(1)} %get-tuple-element.42), channel_id=1, source_target_pairs={{0,4},{1,5},{2,6},{3,7},{4,0},{5,1},{6,2},{7,3},{8,12},{9,13},{10,... | collective-permute-start | bytes 393224 | tf_op jit(solution)/shard_map/ppermute | solution.py:22
  86.1 18.0 %collective-permute-start.15 = (f32[8,4,8,128]{3,2,1,0:T(8,128)S(1)}, f32[8,4,8,128]{3,2,1,0:T(8,128)S(1)}, u32[]{:S(2)}, u32[]{:S(2)}) collective-permute-start(f32[8,4,8,128]{3,2,1,0:T(8,128)S(1)} %get-tuple-element.44), channel_id=1, source_target_pairs={{0,5},{1,4},{2,7},{3,6},{4,1},{5,0},{6,3},{7,2},{8,13},{9,12},{10,... | collective-permute-start | bytes 393224 | tf_op jit(solution)/shard_map/ppermute | solution.py:22
  86.1 21.2 %collective-permute-start.17 = (f32[8,4,8,128]{3,2,1,0:T(8,128)S(1)}, f32[8,4,8,128]{3,2,1,0:T(8,128)S(1)}, u32[]{:S(2)}, u32[]{:S(2)}) collective-permute-start(f32[8,4,8,128]{3,2,1,0:T(8,128)S(1)} %get-tuple-element.46), channel_id=1, source_target_pairs={{0,6},{1,7},{2,4},{3,5},{4,2},{5,3},{6,0},{7,1},{8,14},{9,15},{10,... | collective-permute-start | bytes 393224 | tf_op jit(solution)/shard_map/ppermute | solution.py:22
  88.9 21.0 %collective-permute-start.19 = (f32[8,4,8,128]{3,2,1,0:T(8,128)S(1)}, f32[8,4,8,128]{3,2,1,0:T(8,128)S(1)}, u32[]{:S(2)}, u32[]{:S(2)}) collective-permute-start(f32[8,4,8,128]{3,2,1,0:T(8,128)S(1)} %get-tuple-element.48), channel_id=1, source_target_pairs={{0,7},{1,6},{2,5},{3,4},{4,3},{5,2},{6,1},{7,0},{8,15},{9,14},{10,... | collective-permute-start | bytes 393224 | tf_op jit(solution)/shard_map/ppermute | solution.py:22
  92.7 17.2 %collective-permute-start.9 = (f32[8,4,8,128]{3,2,1,0:T(8,128)S(1)}, f32[8,4,8,128]{3,2,1,0:T(8,128)S(1)}, u32[]{:S(2)}, u32[]{:S(2)}) collective-permute-start(f32[8,4,8,128]{3,2,1,0:T(8,128)S(1)} %get-tuple-element.38), channel_id=1, source_target_pairs={{0,2},{1,3},{2,0},{3,1},{4,6},{5,7},{6,4},{7,5},{8,10},{9,11},{10,... | collective-permute-start | bytes 393224 | tf_op jit(solution)/shard_map/ppermute | solution.py:22
  101.3 9.7 %collective-permute-start.10 = (f32[8,4,8,128]{3,2,1,0:T(8,128)S(1)}, f32[8,4,8,128]{3,2,1,0:T(8,128)S(1)}, u32[]{:S(2)}, u32[]{:S(2)}) collective-permute-start(f32[8,4,8,128]{3,2,1,0:T(8,128)S(1)} %get-tuple-element.39), channel_id=1, source_target_pairs={{0,2},{1,3},{2,0},{3,1},{4,6},{5,7},{6,4},{7,5},{8,10},{9,11},{10,... | collective-permute-start | bytes 393224 | tf_op jit(solution)/shard_map/ppermute | solution.py:22
  104.1 9.0 %collective-permute-start.12 = (f32[8,4,8,128]{3,2,1,0:T(8,128)S(1)}, f32[8,4,8,128]{3,2,1,0:T(8,128)S(1)}, u32[]{:S(2)}, u32[]{:S(2)}) collective-permute-start(f32[8,4,8,128]{3,2,1,0:T(8,128)S(1)} %get-tuple-element.41), channel_id=1, source_target_pairs={{0,3},{1,2},{2,1},{3,0},{4,7},{5,6},{6,5},{7,4},{8,11},{9,10},{10,... | collective-permute-start | bytes 393224 | tf_op jit(solution)/shard_map/ppermute | solution.py:22
  107.3 16.4 %collective-permute-start.14 = (f32[8,4,8,128]{3,2,1,0:T(8,128)S(1)}, f32[8,4,8,128]{3,2,1,0:T(8,128)S(1)}, u32[]{:S(2)}, u32[]{:S(2)}) collective-permute-start(f32[8,4,8,128]{3,2,1,0:T(8,128)S(1)} %get-tuple-element.43), channel_id=1, source_target_pairs={{0,4},{1,5},{2,6},{3,7},{4,0},{5,1},{6,2},{7,3},{8,12},{9,13},{10,... | collective-permute-start | bytes 393224 | tf_op jit(solution)/shard_map/ppermute | solution.py:22
  109.9 16.6 %collective-permute-start.16 = (f32[8,4,8,128]{3,2,1,0:T(8,128)S(1)}, f32[8,4,8,128]{3,2,1,0:T(8,128)S(1)}, u32[]{:S(2)}, u32[]{:S(2)}) collective-permute-start(f32[8,4,8,128]{3,2,1,0:T(8,128)S(1)} %get-tuple-element.45), channel_id=1, source_target_pairs={{0,5},{1,4},{2,7},{3,6},{4,1},{5,0},{6,3},{7,2},{8,13},{9,12},{10,... | collective-permute-start | bytes 393224 | tf_op jit(solution)/shard_map/ppermute | solution.py:22
  109.9 20.6 %collective-permute-start.18 = (f32[8,4,8,128]{3,2,1,0:T(8,128)S(1)}, f32[8,4,8,128]{3,2,1,0:T(8,128)S(1)}, u32[]{:S(2)}, u32[]{:S(2)}) collective-permute-start(f32[8,4,8,128]{3,2,1,0:T(8,128)S(1)} %get-tuple-element.47), channel_id=1, source_target_pairs={{0,6},{1,7},{2,4},{3,5},{4,2},{5,3},{6,0},{7,1},{8,14},{9,15},{10,... | collective-permute-start | bytes 393224 | tf_op jit(solution)/shard_map/ppermute | solution.py:22
  111.0 20.7 %collective-permute-start.20 = (f32[8,4,8,128]{3,2,1,0:T(8,128)S(1)}, f32[8,4,8,128]{3,2,1,0:T(8,128)S(1)}, u32[]{:S(2)}, u32[]{:S(2)}) collective-permute-start(f32[8,4,8,128]{3,2,1,0:T(8,128)S(1)} %get-tuple-element.49), channel_id=1, source_target_pairs={{0,7},{1,6},{2,5},{3,4},{4,3},{5,2},{6,1},{7,0},{8,15},{9,14},{10,... | collective-permute-start | bytes 393224 | tf_op jit(solution)/shard_map/ppermute | solution.py:22
  113.1 18.5 %collective-permute-start.8 = (f32[8,4,8,128]{3,2,1,0:T(8,128)S(1)}, f32[8,4,8,128]{3,2,1,0:T(8,128)S(1)}, u32[]{:S(2)}, u32[]{:S(2)}) collective-permute-start(f32[8,4,8,128]{3,2,1,0:T(8,128)S(1)} %get-tuple-element.37), channel_id=1, source_target_pairs={{0,1},{1,0},{2,3},{3,2},{4,5},{5,4},{6,7},{7,6},{8,9},{9,8},{10,11... | collective-permute-start | bytes 393224 | tf_op jit(solution)/shard_map/ppermute | solution.py:22
  134.3 1.6 collective-permute-start.21
  135.9 3.9 %collective-permute-start.22 = (f32[64,128]{1,0:T(8,128)S(1)}, f32[64,128]{1,0:T(8,128)S(1)}, u32[]{:S(2)}, u32[]{:S(2)}) collective-permute-start(f32[64,128]{1,0:T(8,128)S(1)} %add.33), channel_id=1, source_target_pairs={{0,2},{1,3},{2,0},{3,1},{4,6},{5,7},{6,4},{7,5},{8,10},{9,11},{10,... | collective-permute-start | bytes 98312 | tf_op jit(solution)/shard_map/ppermute | solution.py:22
  139.8 7.8 %collective-permute-start.23 = (f32[64,128]{1,0:T(8,128)S(1)}, f32[64,128]{1,0:T(8,128)S(1)}, u32[]{:S(2)}, u32[]{:S(2)}) collective-permute-start(f32[64,128]{1,0:T(8,128)S(1)} %add.34), channel_id=1, source_target_pairs={{0,128},{1,129},{2,130},{3,131},{4,132},{5,133},{6,134},{7,135},{8... | collective-permute-start | bytes 98312 | tf_op jit(solution)/shard_map/ppermute | solution.py:294
  139.8 7.8 %collective-permute-start.24 = (f32[64,128]{1,0:T(8,128)S(1)}, f32[64,128]{1,0:T(8,128)S(1)}, u32[]{:S(2)}, u32[]{:S(2)}) collective-permute-start(f32[64,128]{1,0:T(8,128)S(1)} %add.34), channel_id=1, source_target_pairs={{0,4},{1,5},{2,6},{3,7},{4,128},{5,129},{6,130},{7,131},{8,12},{9,... | collective-permute-start | bytes 98312 | tf_op jit(solution)/shard_map/ppermute | solution.py:294
  140.9 7.3 %collective-permute-start.25 = (f32[64,128]{1,0:T(8,128)S(1)}, f32[64,128]{1,0:T(8,128)S(1)}, u32[]{:S(2)}, u32[]{:S(2)}) collective-permute-start(f32[64,128]{1,0:T(8,128)S(1)} %add.34), channel_id=1, source_target_pairs={{0,132},{1,133},{2,134},{3,135},{4,0},{5,1},{6,2},{7,3},{8,140},{9... | collective-permute-start | bytes 98312 | tf_op jit(solution)/shard_map/ppermute | solution.py:294
  148.2 5.2 %collective-permute-start.26 = (f32[64,128]{1,0:T(8,128)S(1)}, f32[64,128]{1,0:T(8,128)S(1)}, u32[]{:S(2)}, u32[]{:S(2)}) collective-permute-start(f32[64,128]{1,0:T(8,128)S(1)} %add_add_fusion.2), channel_id=1, source_target_pairs={{0,8},{8,16},{16,24},{24,0},{32,40},{40,48},{48,56},{56,32},{64,72... | collective-permute-start | bytes 98312 | tf_op jit(solution)/shard_map/ppermute | solution.py:22
  148.3 5.5 %collective-permute-start.27 = (f32[64,128]{1,0:T(8,128)S(1)}, f32[64,128]{1,0:T(8,128)S(1)}, u32[]{:S(2)}, u32[]{:S(2)}) collective-permute-start(f32[64,128]{1,0:T(8,128)S(1)} %add_add_fusion.2), channel_id=1, source_target_pairs={{0,16},{8,24},{16,0},{24,8},{32,48},{40,56},{48,32},{56,40},{64,80... | collective-permute-start | bytes 98312 | tf_op jit(solution)/shard_map/ppermute | solution.py:22
  148.4 6.2 %collective-permute-start.28 = (f32[64,128]{1,0:T(8,128)S(1)}, f32[64,128]{1,0:T(8,128)S(1)}, u32[]{:S(2)}, u32[]{:S(2)}) collective-permute-start(f32[64,128]{1,0:T(8,128)S(1)} %add_add_fusion.2), channel_id=1, source_target_pairs={{0,24},{8,0},{16,8},{24,16},{32,56},{40,32},{48,40},{56,48},{64,88... | collective-permute-start | bytes 98312 | tf_op jit(solution)/shard_map/ppermute | solution.py:22
  154.6 5.2 %collective-permute-start.29 = (f32[64,128]{1,0:T(8,128)S(1)}, f32[64,128]{1,0:T(8,128)S(1)}, u32[]{:S(2)}, u32[]{:S(2)}) collective-permute-start(f32[64,128]{1,0:T(8,128)S(1)} %add_add_fusion.1), channel_id=1, source_target_pairs={{0,32},{8,40},{16,48},{24,56},{32,64},{40,72},{48,80},{56,88},{64,... | collective-permute-start | bytes 98312 | tf_op jit(solution)/shard_map/ppermute | solution.py:22
  154.7 5.5 %collective-permute-start.30 = (f32[64,128]{1,0:T(8,128)S(1)}, f32[64,128]{1,0:T(8,128)S(1)}, u32[]{:S(2)}, u32[]{:S(2)}) collective-permute-start(f32[64,128]{1,0:T(8,128)S(1)} %add_add_fusion.1), channel_id=1, source_target_pairs={{0,64},{8,72},{16,80},{24,88},{32,96},{40,104},{48,112},{56,120},{... | collective-permute-start | bytes 98312 | tf_op jit(solution)/shard_map/ppermute | solution.py:22
  157.1 3.9 %collective-permute-start.31 = (f32[64,128]{1,0:T(8,128)S(1)}, f32[64,128]{1,0:T(8,128)S(1)}, u32[]{:S(2)}, u32[]{:S(2)}) collective-permute-start(f32[64,128]{1,0:T(8,128)S(1)} %add_add_fusion.1), channel_id=1, source_target_pairs={{0,96},{8,104},{16,112},{24,120},{32,0},{40,8},{48,16},{56,24},{64... | collective-permute-start | bytes 98312 | tf_op jit(solution)/shard_map/ppermute | solution.py:22
  161.1 1.5 collective-permute-start.32
